TPU v7x, 32 devices: a whole 2x2x4 slice. The times are simulated.
32 devices in a mesh: row: 16 (over z, y, x), col: 2 (over core).
Axes of the slice: x: 2, y: 2, z: 4, core: 2. Of those that a mesh axis runs over, the one named last changes fastest.
Arguments:
- tile_values: float32 [16, 2, 64, 128, 128], P('row', 'col'), may hold values from -0.09375 to 0.09375
- tile_row: int32 [16, 2, 64], P('row', 'col'), may hold values from 0 to 7
- tile_col: int32 [16, 2, 64], P('row', 'col'), may hold values from 0 to 63
- counts: int32 [16, 2], P('row', 'col'), may hold values from 21 to 64, as said below
- diagonal: float32 [16384], P(('row', 'col')), may hold values from 1 to 3
- current: float32 [8, 16384], P(None, ('row', 'col')), may hold values from -6 to 6
- previous: float32 [8, 16384], P(None, ('row', 'col')), may hold values from -6 to 6
- previous_image: float32 [8, 16384], P(None, ('row', 'col')), may hold values from -6 to 6
Outputs:
- image: float32 [8, 16384], P(None, ('row', 'col'))
- residual: float32 [8, 16384], P(None, ('row', 'col'))
- residual_image: float32 [8, 16384], P(None, ('row', 'col'))
- reduced: float32 [24, 24], replicated
Inputs may be any that keep to these rules, and one draw needn't show every extreme that they name: `counts`: every device has between 21 and 64 live slots; in every draw one device has exactly 64 and one exactly 21.
All inputs are finite; a program needn't handle non-finite values.
Results may differ from a plain program's by a relative error of at most 0.0003.
Values sent between devices are 32-bit elements; how exact they have to be, the bound alone decides.
No kernel may reach another device: no remote copies, remote signals or barrier semaphores. Data moves between devices by JAX's collectives and lax.ppermute only.
A program may use at most 64 MiB of HBM per device.

v0:
```python
import jax
import jax.numpy as jnp
from jax import lax
from jax.sharding import PartitionSpec as P

highest = lax.Precision.HIGHEST
group_width = 8


def apply_operator(vectors, diagonal, tile_values, tile_row, tile_col, counts):
    vector_count = vectors.shape[0]
    tile_size = tile_values.shape[-1]
    slot_count = tile_values.shape[2]
    blocks = tile_values.reshape(slot_count, tile_size, tile_size)
    rows_here = tile_row.reshape(slot_count)
    cols_here = tile_col.reshape(slot_count)
    live_count = counts.reshape(())
    row_vectors = lax.all_gather(vectors, "col", axis=1, tiled=True)
    column_vectors = lax.all_gather(vectors, "row", axis=1, tiled=True)
    row_tiles = row_vectors.reshape(vector_count, -1, tile_size)
    column_tiles = column_vectors.reshape(vector_count, -1, tile_size)
    slot_ids = jnp.arange(group_width, dtype=jnp.int32)

    def visit(group_index, carry):
        row_sum, column_sum = carry
        first_slot = group_index * group_width
        chosen = lax.dynamic_slice_in_dim(blocks, first_slot, group_width, 0)
        rows_now = lax.dynamic_slice_in_dim(rows_here, first_slot, group_width, 0)
        cols_now = lax.dynamic_slice_in_dim(cols_here, first_slot, group_width, 0)
        weight = (first_slot + slot_ids < live_count).astype(jnp.float32)[None, :, None]
        direct = (
            jnp.einsum("sij,ksj->ksi", chosen, column_tiles[:, cols_now, :], precision=highest)
            * weight
        )
        mirror = (
            jnp.einsum("sij,ksi->ksj", chosen, row_tiles[:, rows_now, :], precision=highest)
            * weight
        )
        return (row_sum.at[:, rows_now, :].add(direct), column_sum.at[:, cols_now, :].add(mirror))

    groups = (live_count + group_width - 1) // group_width
    row_sum, column_sum = lax.fori_loop(
        0, groups, visit, (jnp.zeros_like(row_tiles), jnp.zeros_like(column_tiles))
    )
    owned = lax.psum_scatter(
        row_sum.reshape(vector_count, -1), "col", scatter_dimension=1, tiled=True
    )
    owned = owned + lax.psum_scatter(
        column_sum.reshape(vector_count, -1), "row", scatter_dimension=1, tiled=True
    )
    return diagonal[None, :] * vectors + owned


def dot_rows(left, right):
    return jnp.dot(left, right.T, precision=highest)


def local(tile_values, tile_row, tile_col, counts, diagonal, current, previous, previous_image):
    image = apply_operator(current, diagonal, tile_values, tile_row, tile_col, counts)
    small_gram, small_proj = lax.psum(
        (dot_rows(current, current), dot_rows(current, image)), ("row", "col")
    )
    factor = jnp.linalg.cholesky(small_gram)
    ritz_matrix = jax.scipy.linalg.cho_solve((factor, True), small_proj)
    residual = image - jnp.dot(ritz_matrix.T, current, precision=highest)
    residual_image = apply_operator(residual, diagonal, tile_values, tile_row, tile_col, counts)
    search_basis = jnp.concatenate([current, residual, previous], 0)
    basis_image = jnp.concatenate([image, residual_image, previous_image], 0)
    correlation, mixed_terms = lax.psum(
        (dot_rows(search_basis, search_basis), dot_rows(search_basis, basis_image)), ("row", "col")
    )
    pencil = 0.5 * (mixed_terms + mixed_terms.T)
    lower_factor = jnp.linalg.cholesky(correlation)
    half_solve = jax.scipy.linalg.solve_triangular(lower_factor, pencil, lower=True)
    reduced = jax.scipy.linalg.solve_triangular(lower_factor, half_solve.T, lower=True)
    return (image, residual, residual_image, reduced)


def solution(mesh):
    return jax.shard_map(
        local,
        mesh=mesh,
        in_specs=(
            P("row", "col", None, None, None),
            P("row", "col", None),
            P("row", "col", None),
            P("row", "col"),
            P(("row", "col")),
            P(None, ("row", "col")),
            P(None, ("row", "col")),
            P(None, ("row", "col")),
        ),
        out_specs=(P(None, ("row", "col")), P(None, ("row", "col")), P(None, ("row", "col")), P()),
        check_vma=False,
    )
```

profile of v0, /device:TPU:0, one launch (start us, length us, event | category | flops | bytes accessed | tf_op | source)
XLA Modules:
  0.0 479.5 jit_solution(4071081358549390962)
XLA Ops:
  7.9 44.0 %all_gather.12 = f32[8,8192]{1,0:T(8,128)S(1)} all-gather(f32[8,512]{1,0:T(8,128)} %param.19), channel_id=1, replica_groups=mesh['row'=16,'col'=2] {'row'}, dimensions={1}, use_global_device_ids=true | all-gather | bytes 278528 | tf_op jit(solution)/shard_map/all_gather | solution.py:19
  51.9 2.0 all_gather.13
  54.0 30.9 %while.26 = (s32[]{:T(128)}, f32[8,8,128]{2,0,1:T(8,128)S(1)}, f32[8,64,128]{2,0,1:T(8,128)S(1)}, s32[]{:T(128)}, s32[64]{0:T(128)}, /*index=5*/s32[64]{0:T(128)...) while((s32[]{:T(128)}, f32[8,8,128]{2,0,1:T(8,128)S(1)}, ...), condition=%wide.region_3.4_spmd.clone, body=%wide.region_0.3_spmd.clone.sunk | while | flops 25200716 | bytes 1516143 | solution.py:42
  56.0 2.0 convolution_multiply_fusion.8
  57.9 0.8 scatter_fusion
  59.3 1.6 convolution_multiply_fusion.9
  60.9 0.8 scatter_fusion.1
  63.7 2.0 convolution_multiply_fusion.8
  65.7 0.8 scatter_fusion
  67.0 1.6 convolution_multiply_fusion.9
  68.6 0.8 scatter_fusion.1
  71.4 2.0 convolution_multiply_fusion.8
  73.4 0.8 scatter_fusion
  74.8 1.6 convolution_multiply_fusion.9
  76.3 0.8 scatter_fusion.1
  77.1 0.8 compare_select_fusion.6
  79.1 2.0 convolution_multiply_fusion.8
  81.1 0.8 scatter_fusion
  82.5 1.6 convolution_multiply_fusion.9
  84.0 0.8 scatter_fusion.1
  86.4 33.4 %reduce-scatter.5.cloned.1.call-done = f32[8,512]{1,0:T(8,128)} async-done(((f32[8,1024]{1,0:T(8,128)}), f32[8,512]{1,0:T(8,128)}) %reduce-scatter.5.cloned.1.call-update) | async-done | bytes 16400 | tf_op jit(solution)/shard_map/reduce_scatter | solution.py:45
  119.8 79.6 %reduce-scatter.7.cloned.1.call-done = f32[8,512]{1,0:T(8,128)} async-done(((f32[8,8192]{1,0:T(8,128)}), f32[8,512]{1,0:T(8,128)}) %reduce-scatter.7.cloned.1.call-update) | async-done | bytes 16400 | tf_op jit(solution)/shard_map/reduce_scatter | solution.py:48
  200.2 36.9 %all-reduce.1 = (f32[8,8]{0,1:T(8,128)S(1)}, f32[8,8]{0,1:T(8,128)S(1)}) all-reduce(f32[8,8]{0,1:T(8,128)S(1)} %convolution_bitcast_fusion.1, f32[8,8]{0,1:T(8,128)S(1)} %fusion.40), channel_id=1, replica_groups=mesh['row'=16,'col'=2] {'row','col'}, use_global_device_ids=true, to_apply=%region_9.10 | all-reduce | flops 128 | bytes 1024 | tf_op jit(solution)/shard_map/psum | solution.py:60
  240.4 40.5 %all_gather.14 = f32[8,8192]{1,0:T(8,128)S(1)} all-gather(f32[8,512]{1,0:T(8,128)S(1)} %convolution_subtract_fusion), channel_id=1, replica_groups=mesh['row'=16,'col'=2] {'row'}, dimensions={1}, use_global_device_ids=true | all-gather | bytes 278528 | tf_op jit(solution)/shard_map/all_gather | solution.py:19
  281.0 1.8 all_gather.15
  282.8 30.9 %while.27 = (s32[]{:T(128)}, f32[8,8,128]{2,0,1:T(8,128)S(1)}, f32[8,64,128]{2,0,1:T(8,128)S(1)}, s32[]{:T(128)}, s32[64]{0:T(128)}, /*index=5*/s32[64]{0:T(128)...) while((s32[]{:T(128)}, f32[8,8,128]{2,0,1:T(8,128)S(1)}, ...), condition=%wide.region_13.14_spmd.clone, body=%wide.region_10.13_spmd.clone.sunk | while | flops 25200716 | bytes 1516143 | solution.py:42
  284.8 2.0 convolution_multiply_fusion.10
  286.8 0.8 scatter_fusion.2
  288.2 1.6 convolution_multiply_fusion.11
  289.7 0.8 scatter_fusion.3
  292.5 2.0 convolution_multiply_fusion.10
  294.5 0.8 scatter_fusion.2
  295.9 1.6 convolution_multiply_fusion.11
  297.5 0.8 scatter_fusion.3
  300.2 2.0 convolution_multiply_fusion.10
  302.2 0.8 scatter_fusion.2
  303.6 1.6 convolution_multiply_fusion.11
  305.2 0.8 scatter_fusion.3
  308.0 2.0 convolution_multiply_fusion.10
  309.9 0.8 scatter_fusion.2
  311.3 1.6 convolution_multiply_fusion.11
  312.9 0.8 scatter_fusion.3
  315.1 33.6 %reduce-scatter.9.cloned.1.call-done = f32[8,512]{1,0:T(8,128)} async-done(((f32[8,1024]{1,0:T(8,128)}), f32[8,512]{1,0:T(8,128)}) %reduce-scatter.9.cloned.1.call-update) | async-done | bytes 16400 | tf_op jit(solution)/shard_map/reduce_scatter | solution.py:45
  348.7 79.5 %reduce-scatter.11.cloned.1.call-done = f32[8,512]{1,0:T(8,128)} async-done(((f32[8,8192]{1,0:T(8,128)}), f32[8,512]{1,0:T(8,128)}) %reduce-scatter.11.cloned.1.call-update) | async-done | bytes 16400 | tf_op jit(solution)/shard_map/reduce_scatter | solution.py:48
  429.2 37.2 %all-reduce = (f32[24,24]{0,1:T(8,128)S(1)}, f32[24,24]{0,1:T(8,128)S(1)}) all-reduce(f32[24,24]{0,1:T(8,128)S(1)} %fusion.16, f32[24,24]{0,1:T(8,128)S(1)} %fusion.22), channel_id=1, replica_groups=mesh['row'=16,'col'=2] {'row','col'}, use_global_device_ids=true, to_apply=%region_19.20 | all-reduce | flops 1152 | bytes 9216 | tf_op jit(solution)/shard_map/psum | solution.py:69
  466.5 2.2 cholesky.64
  470.0 1.8 custom-call.19
  472.1 0.8 fusion.27
  (104 shorter events, 29.1 us)
Async XLA Ops:
  7.2 112.6 %reduce-scatter.5.cloned.1.call-start = ((), (), s32[]{:S(2)}) async-start(), calls=%async_computation.4 | async-start | bytes 49152 | tf_op jit(solution)/shard_map/reduce_scatter | solution.py:45
  53.9 32.3 %copy-start.4 = (f32[8,512]{1,0:T(8,128)S(1)}, f32[8,512]{1,0:T(8,128)}, u32[]{:S(2)}) copy-start(f32[8,512]{1,0:T(8,128)} %param.19) | copy-start | bytes 49156
  54.0 145.4 %copy-start.8 = (f32[512]{0:T(512)S(1)}, f32[512]{0:T(512)}, u32[]{:S(2)}) copy-start(f32[512]{0:T(512)} %param.18) | copy-start | bytes 6148
  84.8 0.6 copy-start.3
  84.8 0.7 copy-start.1
  85.5 113.9 %reduce-scatter.7.cloned.1.call-start = ((), (), s32[]{:S(2)}) async-start(), calls=%async_computation.5 | async-start | bytes 278528 | tf_op jit(solution)/shard_map/reduce_scatter | solution.py:48
  86.2 262.5 %reduce-scatter.9.cloned.1.call-start = ((), (), s32[]{:S(2)}) async-start(), calls=%async_computation.6 | async-start | bytes 49152 | tf_op jit(solution)/shard_map/reduce_scatter | solution.py:45
  200.1 228.9 %copy-start.6 = (f32[8,512]{1,0:T(8,128)}, f32[8,512]{1,0:T(8,128)S(1)}, u32[]{:S(2)}) copy-start(f32[8,512]{1,0:T(8,128)S(1)} %add_add_fusion.1) | copy-start | bytes 49156
  240.4 188.5 %copy-start.5 = (f32[8,512]{1,0:T(8,128)}, f32[8,512]{1,0:T(8,128)S(1)}, u32[]{:S(2)}) copy-start(f32[8,512]{1,0:T(8,128)S(1)} %convolution_subtract_fusion) | copy-start | bytes 49156
  282.8 32.1 %copy-start.10 = (f32[8,512]{1,0:T(8,128)S(1)}, f32[8,512]{1,0:T(8,128)}, u32[]{:S(2)}) copy-start(f32[8,512]{1,0:T(8,128)} %param.20) | copy-start | bytes 49156
  282.8 146.2 %copy-start.9 = (f32[8,512]{1,0:T(8,128)S(1)}, f32[8,512]{1,0:T(8,128)}, u32[]{:S(2)}) copy-start(f32[8,512]{1,0:T(8,128)} %param.21) | copy-start | bytes 49156
  313.7 0.6 copy-start.2
  313.7 0.7 copy-start
  314.3 113.9 %reduce-scatter.11.cloned.1.call-start = ((), (), s32[]{:S(2)}) async-start(), calls=%async_computation.7 | async-start | bytes 278528 | tf_op jit(solution)/shard_map/reduce_scatter | solution.py:48
  429.0 44.0 %copy-start.7 = (f32[8,512]{1,0:T(8,128)}, f32[8,512]{1,0:T(8,128)S(1)}, u32[]{:S(2)}) copy-start(f32[8,512]{1,0:T(8,128)S(1)} %add_add_fusion) | copy-start | bytes 49156
Sparse Core Ops, SparseCore 0:
  85.6 34.1 reduce-scatter.4
  122.0 77.2 reduce-scatter.6
  314.4 34.2 reduce-scatter.8
  350.9 77.2 reduce-scatter.10
where the time goes:
time: 480 us; the launch traced here: 479 us
  waiting for transfers between devices  227 us (47%)
  blocking collectives  163 us (34%)
  other arithmetic  33.4 us (7%)
  matrix products  30.5 us (6%)
  between operations  14.6 us (3%)
  local copies, waits for them, and re-layouts  10.4 us (2%)
    reduce_scatter x2, waiting for transfers between devices, apply_operator(): lax.psum_scatter(column_sum.reshape(vector_count, -1), 'row', scatter_dim...  159 us
    all_gather x2, blocking collectives, apply_operator(): column_vectors = lax.all_gather(vectors, 'row', axis=1, tiled=True)  84.5 us
    reduce_scatter x2, waiting for transfers between devices, apply_operator(): lax.psum_scatter(row_sum.reshape(vector_count, -1), 'col', scatter_dimens...  67 us
    psum x1, blocking collectives, local(): lax.psum((dot_rows(search_basis, search_basis), dot_rows(search_basis, ba...  37.2 us
    psum x1, blocking collectives, local(): lax.psum((dot_rows(current, current), dot_rows(current, image)), ('row',...  36.9 us
    dot_general x8, matrix products, visit(): jnp.einsum('sij,ksj->ksi', chosen, column_tiles[:, cols_now, :], precisio...  15.7 us
    dot_general x8, matrix products, visit(): jnp.einsum('sij,ksi->ksj', chosen, row_tiles[:, rows_now, :], precision=h...  12.6 us
  transfers between devices with their start and end apart: 4, of which 4 were waited for; matrix products, arithmetic and copies ran while one was open for 0% of the time, Pallas kernels for 0%

commit v1 on v0

v1 whole, which is shorter than its diff:
```python
import functools
import math

import jax
import jax.numpy as jnp
from jax import lax
from jax.experimental import pallas as pl
from jax.experimental.pallas import tpu as pltpu
from jax.sharding import PartitionSpec as P

f32 = jnp.float32
bf16 = jnp.bfloat16
highest = lax.Precision.HIGHEST
LANES = 128
in_vmem = pl.BlockSpec(memory_space=pltpu.VMEM)
in_smem = pl.BlockSpec(memory_space=pltpu.SMEM)
params = pltpu.CompilerParams(vmem_limit_bytes=40 * 2**20)


def call(kernel, name, out_shape, operands, specs, scratch=()):
    return pl.pallas_call(
        kernel,
        out_shape=out_shape,
        in_specs=specs,
        out_specs=jax.tree.map(lambda _: in_vmem, out_shape),
        scratch_shapes=scratch,
        compiler_params=params,
        name=name,
    )(*operands)


def shape(*dims):
    return jax.ShapeDtypeStruct(dims, f32)


def halves(values):
    high = values.astype(bf16)
    return high, (values - high.astype(f32)).astype(bf16)


def times_transpose(left, right, precision=None):
    return lax.dot_general(
        left, right, (((1,), (1,)), ((), ())), preferred_element_type=f32, precision=precision
    )


def times(left, right, precision=None):
    return lax.dot_general(
        left, right, (((1,), (0,)), ((), ())), preferred_element_type=f32, precision=precision
    )


def tile_of(ref, t):
    return ref[:, t * LANES : (t + 1) * LANES]


def spread_kernel(x_ref, p_ref, spread_ref, own_ref):
    for t in range(own_ref.shape[0]):
        pair = jnp.concatenate([tile_of(x_ref, t), tile_of(p_ref, t)], axis=0)
        own_ref[t] = pair
        for r in range(spread_ref.shape[0]):
            spread_ref[r, t] = pair


def fill_row_block(block_ref, own_ref, other_ref, here, paired):
    tiles = own_ref.shape[0]
    if paired:
        for t in range(tiles):
            block_ref[here * tiles + t] = own_ref[t]
            block_ref[(1 - here) * tiles + t] = other_ref[t]
    else:
        for c in range(other_ref.shape[0]):
            for t in range(tiles):
                block_ref[c * tiles + t] = other_ref[c, t]


def hand_row_sums(row_sum, keep_ref, send_ref, here, paired):
    tiles = keep_ref.shape[0]
    if paired:
        for t in range(tiles):
            keep_ref[t] = row_sum[here * tiles + t]
            send_ref[t] = row_sum[(1 - here) * tiles + t]
    else:
        keep_ref[...] = jnp.zeros_like(keep_ref)
        for c in range(send_ref.shape[0]):
            for t in range(tiles):
                send_ref[c, t] = row_sum[c * tiles + t]


def visit_slots(live, rows, cols, blocks, column_halves, row_halves, row_sums, column_sum):
    slots = blocks.shape[0]
    group = math.gcd(slots, 16)
    count = 8 * len(row_sums)

    def visit(index, _):
        products = []
        for s in range(group):
            slot = index * group + s
            a = rows[slot]
            b = cols[slot]
            high, low = halves(blocks[slot])
            x = column_halves[b]
            u = row_halves[a]
            weight = jnp.where(slot < live, 1.0, 0.0).astype(f32)
            direct = times_transpose(
                jnp.concatenate([x, x], axis=1), jnp.concatenate([high, low], axis=1)
            )
            mirror = times(jnp.concatenate([u, u], axis=1), jnp.concatenate([high, low], axis=0))
            products.append(
                (
                    a,
                    b,
                    (direct[:count] + direct[count:]) * weight,
                    (mirror[:8] + mirror[8:]) * weight,
                )
            )
        for a, b, direct, mirror in products:
            for n, row_sum in enumerate(row_sums):
                row_sum[a] += direct[8 * n : 8 * n + 8]
            column_sum[b] += mirror
        return 0

    lax.fori_loop(0, (live + group - 1) // group, visit, 0)


def first_kernel(
    paired, live, rows, cols, here, blocks, gathered, own, other,
    keep, send, previous_sum, column_sum,
    column_halves, row_block, row_halves, row_sum,
):
    here = here[0]
    for j in range(gathered.shape[0]):
        high, low = halves(gathered[j])
        column_halves[j] = jnp.concatenate([high, low], axis=0)
    fill_row_block(row_block, own, other, here, paired)
    for j in range(row_block.shape[0]):
        high, low = halves(row_block[j, 0:8])
        row_halves[j] = jnp.concatenate([high, low], axis=0)
    row_sum[...] = jnp.zeros_like(row_sum)
    previous_sum[...] = jnp.zeros_like(previous_sum)
    column_sum[...] = jnp.zeros_like(column_sum)
    visit_slots(
        live[0], rows, cols, blocks, column_halves, row_halves, [row_sum, previous_sum], column_sum
    )
    hand_row_sums(row_sum, keep, send, here, paired)


def owned_sum(t, diagonal, vectors, keep, received, parts, paired):
    total = tile_of(diagonal, t) * vectors + keep[t]
    if paired:
        total = total + received[t]
    else:
        for c in range(received.shape[0]):
            total = total + received[c, t]
    columns = [parts[r, t] for r in range(parts.shape[0])]
    while len(columns) > 1:
        columns = [sum(columns[n : n + 2]) for n in range(0, len(columns), 2)]
    return total + columns[0]


def image_kernel(paired, diagonal, x_ref, keep, received, parts, image, own, spread):
    for t in range(own.shape[0]):
        value = owned_sum(t, diagonal, tile_of(x_ref, t), keep, received, parts, paired)
        image[:, t * LANES : (t + 1) * LANES] = value
        own[t] = value
        for r in range(spread.shape[0]):
            spread[r, t] = value


def second_kernel(
    paired, live, rows, cols, here, blocks, gathered, own, other, pair_own, pair_other, previous_sum,
    diagonal, x_ref, y_ref, p_ref, q_ref,
    keep, send, payload,
    column_halves, row_block, pair_block, row_halves, row_sum, column_sum,
):
    here = here[0]
    for j in range(gathered.shape[0]):
        high, low = halves(gathered[j])
        column_halves[j] = jnp.concatenate([high, low], axis=0)
    fill_row_block(row_block, own, other, here, paired)
    fill_row_block(pair_block, pair_own, pair_other, here, paired)
    for j in range(row_block.shape[0]):
        high, low = halves(row_block[j])
        row_halves[j] = jnp.concatenate([high, low], axis=0)
    row_sum[...] = jnp.zeros_like(row_sum)
    column_sum[...] = jnp.zeros_like(column_sum)
    visit_slots(live[0], rows, cols, blocks, column_halves, row_halves, [row_sum], column_sum)
    hand_row_sums(row_sum, keep, send, here, paired)
    tiles = own.shape[0]
    for r in range(payload.shape[0]):
        for t in range(tiles):
            payload[r, t] = column_sum[r * tiles + t]
    x, y, p, q = x_ref[...], y_ref[...], p_ref[...], q_ref[...]
    raw = jnp.concatenate([x, y, p, q], axis=0)
    outer = times_transpose(jnp.concatenate([x, y, p], axis=0), raw, highest)
    own_rows = times_transpose(diagonal[...] * y, jnp.concatenate([y, p], axis=0), highest)
    images = jnp.concatenate([row_sum[j] for j in range(row_sum.shape[0])], axis=1)
    images_previous = jnp.concatenate([previous_sum[j] for j in range(row_sum.shape[0])], axis=1)
    block_y = jnp.concatenate([row_block[j] for j in range(row_sum.shape[0])], axis=1)
    block_p = jnp.concatenate([pair_block[j, 8:16] for j in range(row_sum.shape[0])], axis=1)
    stored = times_transpose(images, jnp.concatenate([block_y, block_p], axis=0), highest)
    stored_previous = times_transpose(block_y, images_previous, highest)
    yz = 2.0 * stored[:, 0:8] + own_rows[:, 0:8]
    zp = stored[:, 8:16] + own_rows[:, 8:16] + stored_previous
    gram = jnp.concatenate(
        [
            outer[0:8, 0:24],
            outer[0:8, 8:16],
            outer[8:16, 8:16],
            outer[0:8, 24:32] + outer[8:16, 16:24],
            outer[8:16, 16:24],
            yz,
            outer[8:16, 24:32] + zp,
            outer[16:24, 16:24],
            outer[16:24, 24:32],
            jnp.zeros((8, LANES - 88), f32),
        ],
        axis=1,
    )
    for r in range(payload.shape[0]):
        payload[r, tiles] = gram


def gather_sum_kernel(paired, diagonal, y_ref, keep, received, parts, z_ref, gram):
    tiles = keep.shape[0]
    for t in range(tiles):
        z_ref[:, t * LANES : (t + 1) * LANES] = owned_sum(
            t, diagonal, tile_of(y_ref, t), keep, received, parts, paired
        )
    gram[...] = sum(parts[r, tiles] for r in range(parts.shape[0]))


def finish_kernel(x_ref, y_ref, z_ref, mine, theirs, residual, residual_image, reduced):
    gram = mine[...] + theirs[...]
    turned = gram.T

    def block(n):
        return gram[:, 8 * n : 8 * n + 8]

    def flipped(n):
        return turned[8 * n : 8 * n + 8, :]

    xx, xy, xp, xy_again, yy, mixed, yp, yz, zp, pp, pq = range(11)
    unit = (
        lax.broadcasted_iota(jnp.int32, (24, 24), 0) == lax.broadcasted_iota(jnp.int32, (24, 24), 1)
    ).astype(f32)
    work = jnp.concatenate(
        [
            jnp.concatenate(
                [gram[:, 0:24], 0.5 * (block(xy) + flipped(xy)), block(yy), 0.5 * block(mixed)], axis=1
            ),
            jnp.concatenate(
                [
                    flipped(xy), block(yy), block(yp),
                    block(yy), 0.5 * (block(yz) + flipped(yz)), 0.5 * block(zp),
                ],
                axis=1,
            ),
            jnp.concatenate(
                [
                    flipped(xp), flipped(yp), block(pp),
                    0.5 * flipped(mixed), 0.5 * flipped(zp), 0.5 * (block(pq) + flipped(pq)),
                ],
                axis=1,
            ),
        ],
        axis=0,
    )
    work = jnp.concatenate([work, unit, jnp.zeros((24, LANES - 72), f32)], axis=1)
    row_ids = lax.broadcasted_iota(jnp.int32, (24, 1), 0)
    ritz = None
    for k in range(24):
        if k == 8:
            ritz = work[8:16, 48:56]
        if k < 23:
            pivot_row = work[k : k + 1, :] / work[k : k + 1, k : k + 1]
            factor = jnp.where(row_ids > k, work[:, k : k + 1], 0.0)
            work = work - factor * pivot_row
    diagonal = jnp.sum(work[:, 0:24] * unit, axis=1, keepdims=True)
    scale = lax.rsqrt(diagonal)
    scaled = work * scale
    reduced[...] = times_transpose(scaled[:, 24:48], scaled[:, 48:72], highest)
    r = y_ref[...]
    s = z_ref[...]
    for j in range(8):
        r = r + ritz[:, j : j + 1] * x_ref[j : j + 1, :]
        s = s + ritz[:, j : j + 1] * y_ref[j : j + 1, :]
    residual[...] = r
    residual_image[...] = s


def local(tile_values, tile_row, tile_col, counts, diagonal, current, previous, previous_image, *, sizes):
    n_row, n_col = sizes
    slots, side = tile_values.shape[2], tile_values.shape[-1]
    width = current.shape[1]
    tiles = width // side
    paired = n_col == 2
    blocks = pltpu.with_memory_space_constraint(
        tile_values.reshape(slots, side, side), pltpu.VMEM
    )
    rows_here = tile_row.reshape(slots)
    cols_here = tile_col.reshape(slots)
    live = counts.reshape(1)
    here = lax.axis_index("col").reshape(1).astype(jnp.int32)
    diagonal = diagonal.reshape(1, width)

    def to_rows(values):
        return lax.all_to_all(values, "row", 0, 0, tiled=True)

    def from_columns(values):
        if paired:
            return lax.ppermute(values, "col", [(0, 1), (1, 0)])
        return lax.all_gather(values, "col", axis=0)

    def sums_to_columns(values):
        if paired:
            return lax.ppermute(values, "col", [(0, 1), (1, 0)])
        return lax.all_to_all(values, "col", 0, 0, tiled=True)

    send_shape = shape(tiles, 8, side) if paired else shape(n_col, tiles, 8, side)
    row_tiles = n_col * tiles
    column_tiles = n_row * tiles

    spread, pair_own = call(
        spread_kernel,
        "spread_vectors",
        [shape(n_row, tiles, 16, side), shape(tiles, 16, side)],
        [current, previous],
        [in_vmem] * 2,
    )
    pair_other = from_columns(pair_own)
    gathered = to_rows(spread).reshape(column_tiles, 16, side)
    keep, send, previous_sum, column_sum = call(
        functools.partial(first_kernel, paired),
        "apply_to_current",
        [shape(tiles, 8, side), send_shape, shape(row_tiles, 8, side), shape(column_tiles, 8, side)],
        [live, rows_here, cols_here, here, blocks, gathered, pair_own, pair_other],
        [in_smem] * 4 + [in_vmem] * 4,
        [
            pltpu.VMEM((column_tiles, 32, side), bf16),
            pltpu.VMEM((row_tiles, 16, side), f32),
            pltpu.VMEM((row_tiles, 16, side), bf16),
            pltpu.VMEM((row_tiles, 8, side), f32),
        ],
    )
    received = sums_to_columns(send)
    parts = to_rows(column_sum.reshape(n_row, tiles, 8, side))
    image, own, spread = call(
        functools.partial(image_kernel, paired),
        "sum_image",
        [shape(8, width), shape(tiles, 8, side), shape(n_row, tiles, 8, side)],
        [diagonal, current, keep, received, parts],
        [in_vmem] * 5,
    )
    other = from_columns(own)
    gathered = to_rows(spread).reshape(column_tiles, 8, side)
    keep, send, payload = call(
        functools.partial(second_kernel, paired),
        "apply_to_image",
        [shape(tiles, 8, side), send_shape, shape(n_row, tiles + 1, 8, side)],
        [
            live, rows_here, cols_here, here, blocks, gathered, own, other, pair_own, pair_other,
            previous_sum, diagonal, current, image, previous, previous_image,
        ],
        [in_smem] * 4 + [in_vmem] * 12,
        [
            pltpu.VMEM((column_tiles, 16, side), bf16),
            pltpu.VMEM((row_tiles, 8, side), f32),
            pltpu.VMEM((row_tiles, 16, side), f32),
            pltpu.VMEM((row_tiles, 16, side), bf16),
            pltpu.VMEM((row_tiles, 8, side), f32),
            pltpu.VMEM((column_tiles, 8, side), f32),
        ],
    )
    received = sums_to_columns(send)
    parts = to_rows(payload)
    twice, gram = call(
        functools.partial(gather_sum_kernel, paired),
        "sum_second_image",
        [shape(8, width), shape(8, LANES)],
        [diagonal, image, keep, received, parts],
        [in_vmem] * 5,
    )
    if paired:
        theirs = lax.ppermute(gram, "col", [(0, 1), (1, 0)])
    else:
        theirs = lax.psum(gram, "col") - gram
    residual, residual_image, reduced = call(
        finish_kernel,
        "finish",
        [shape(8, width), shape(8, width), shape(24, 24)],
        [current, image, twice, gram, theirs],
        [in_vmem] * 5,
    )
    return (image, residual, residual_image, reduced)


def solution(mesh):
    return jax.shard_map(
        functools.partial(local, sizes=(mesh.shape["row"], mesh.shape["col"])),
        mesh=mesh,
        in_specs=(
            P("row", "col", None, None, None),
            P("row", "col", None),
            P("row", "col", None),
            P("row", "col"),
            P(("row", "col")),
            P(None, ("row", "col")),
            P(None, ("row", "col")),
            P(None, ("row", "col")),
        ),
        out_specs=(P(None, ("row", "col")), P(None, ("row", "col")), P(None, ("row", "col")), P()),
        check_vma=False,
    )
```

time: 480 us -> 83.5 us (0.17)
  waiting for transfers between devices: 227 us -> 43.7 us
  blocking collectives: 163 us -> 0 us
  other arithmetic: 33.4 us -> 0 us
  matrix products: 30.5 us -> 0 us
  starting transfers between devices: 0.16 us -> 20 us
  between operations: 14.6 us -> 1.42 us
  Pallas kernels: 0 us -> 10.2 us
    reduce_scatter x4 -> x0, waiting for transfers between devices: 226 us -> none  [the longest x2 159 us: apply_operator(): lax.psum_scatter(column_sum.reshape(vector_count, -1), 'row', scatter_dim...]
    all_gather x4 -> x0, blocking collectives: 88.4 us -> none  [the longest x2 84.5 us: apply_operator(): column_vectors = lax.all_gather(vectors, 'row', axis=1, tiled=True)]
    psum x2 -> x0, blocking collectives: 74.1 us -> none  [the longest x1 37.2 us: local(): lax.psum((dot_rows(search_basis, search_basis), dot_rows(search_basis, ba...]
    all_to_all x0 -> x4, waiting for transfers between devices: none -> 38.5 us  [to_rows(): return lax.all_to_all(values, 'row', 0, 0, tiled=True)]
    dot_general x21 -> x0, matrix products: 29.1 us -> none  [the longest x8 15.7 us: visit(): jnp.einsum('sij,ksj->ksi', chosen, column_tiles[:, cols_now, :], precisio...]
    all_to_all x0 -> x4, starting transfers between devices: none -> 19.6 us  [to_rows(): return lax.all_to_all(values, 'row', 0, 0, tiled=True)]
    scatter-add x16 -> x0, other arithmetic: 12.6 us -> none  [the longest x8 6.39 us: visit(): row_sum.at[:, rows_now, :].add(direct)]
    pallas_call x0 -> x6, Pallas kernels: none -> 10.2 us  [call(): pl.pallas_call(kernel, out_shape=out_shape, in_specs=specs, out_specs=jax...]
  transfers between devices with their start and end apart: 4 -> 9, of which waited for: 4 -> 9; matrix products, arithmetic and copies ran while one was open for 0% -> 0% of each run, Pallas kernels for 0% -> 0%
where the time goes in v1:
time: 83.5 us; the launch traced here: 83.1 us
  waiting for transfers between devices  43.7 us (52%)
  starting transfers between devices  20 us (24%)
  Pallas kernels  10.2 us (12%)
  local copies, waits for them, and re-layouts  7.86 us (9%)
  between operations  1.42 us (2%)
    all_to_all x4, waiting for transfers between devices, to_rows(): return lax.all_to_all(values, 'row', 0, 0, tiled=True)  38.5 us
    all_to_all x4, starting transfers between devices, to_rows(): return lax.all_to_all(values, 'row', 0, 0, tiled=True)  19.6 us
    pallas_call x6, Pallas kernels, call(): pl.pallas_call(kernel, out_shape=out_shape, in_specs=specs, out_specs=jax...  10.2 us
    unnamed x28, local copies, waits for them, and re-layouts  7.86 us
    ppermute x2, waiting for transfers between devices, sums_to_columns(): return lax.ppermute(values, 'col', [(0, 1), (1, 0)])  2.34 us
    ppermute x2, waiting for transfers between devices, from_columns(): return lax.ppermute(values, 'col', [(0, 1), (1, 0)])  1.71 us
  transfers between devices with their start and end apart: 9, of which 9 were waited for; matrix products, arithmetic and copies ran while one was open for 0% of the time, Pallas kernels for 0%

profile of v1, /device:TPU:0, one launch (start us, length us, event | category | flops | bytes accessed | tf_op | source)
XLA Modules:
  0.0 83.1 jit_solution(10404504813944539013)
XLA Ops:
  0.6 0.0 copy-start.2
  0.6 0.7 copy-done.2
  1.4 0.0 copy-start.6
  1.4 0.7 copy-done.6
  2.1 0.0 copy-start.3
  2.1 0.0 copy-start.8
  2.1 0.0 copy-start.7
  2.1 0.0 copy-start.9
  2.1 0.0 copy-start.11
  2.1 0.0 copy-start.13
  2.1 0.9 %spread_vectors.1 = (f32[16,4,16,128]{3,2,1,0:T(8,128)}, f32[4,16,128]{2,1,0:T(8,128)S(1)}) custom-call(f32[8,512]{1,0:T(8,128)S(1)} %copy-done.2, f32[8,512]{1,0:T(8,128)S(1)} %copy-done.6), custom_call_target="tpu_custom_call" | custom-call | tf_op jit(solution)/shard_map/spread_vectors/pallas_call | solution.py:21
  3.0 8.3 %all-to-all-start = ((f32[16,4,16,128]{3,2,1,0:T(8,128)}), f32[16,4,16,128]{3,2,1,0:T(8,128)S(1)}, u32[]{:S(2)}, u32[]{:S(2)}) async-start(f32[16,4,16,128]{3,2,1,0:T(8,128)} %get-tuple-element.21), calls=%async_computation | async-start | bytes 1048576 | tf_op jit(solution)/shard_map/all_to_all | solution.py:308
  11.3 0.1 collective-permute-start
  12.0 0.5 collective-permute-done.other.pair_other
  12.6 13.9 %all-to-all-done = f32[16,4,16,128]{3,2,1,0:T(8,128)S(1)} async-done(((f32[16,4,16,128]{3,2,1,0:T(8,128)}), f32[16,4,16,128]{3,2,1,0:T(8,128)S(1)}, u32[]{:S(2)}, u32[]{:S(2)}) %all-to-all-start) | async-done | bytes 524320 | tf_op jit(solution)/shard_map/all_to_all | solution.py:308
  26.4 0.0 copy-start
  26.4 2.2 %copy-done = f32[1,1,64,128,128]{4,3,2,1,0:T(8,128)S(1)} copy-done((f32[1,1,64,128,128]{4,3,2,1,0:T(8,128)S(1)}, f32[1,1,64,128,128]{4,3,2,1,0:T(8,128)}, u32[]{:S(2)}) %copy-start) | copy-done | bytes 4194328
  28.6 0.0 copy-start.10
  28.6 0.7 copy-done.10
  29.3 0.7 copy-done.12
  29.9 2.5 %apply_to_current.1 = (f32[4,8,128]{2,1,0:T(8,128)S(1)}, f32[4,8,128]{2,1,0:T(8,128)S(1)}, f32[8,8,128]{2,1,0:T(8,128)S(1)}, f32[64,8,128]{2,1,0:T(8,128)}) custom-call(s32[1]{0:T(128)} %bitcast.9.live, s32[64]{0:T(128)S(1)} %bitcast.18, s32[64]{0:T(128)S(1)} %bitcast.20, s32[1]{0:T(128)} %bitcast.4.here, f32[64,128,128]{2,1,0:T(8,128)S(1)} %bitcast.11, ...), custom_call_target="tpu_custom_call" | custom-call | tf_op jit(solution)/shard_map/apply_to_current/pallas_call | solution.py:21
  32.4 3.9 %all-to-all-start.1 = ((f32[16,4,8,128]{3,2,1,0:T(8,128)}), f32[16,4,8,128]{3,2,1,0:T(8,128)S(1)}, u32[]{:S(2)}, u32[]{:S(2)}) async-start(f32[16,4,8,128]{3,2,1,0:T(8,128)} %bitcast.7), calls=%async_computation.1 | async-start | bytes 524288 | tf_op jit(solution)/shard_map/all_to_all | solution.py:308
  36.3 0.1 collective-permute-start.1
  36.4 1.2 %collective-permute-done.1.received = f32[4,8,128]{2,1,0:T(8,128)S(1)} collective-permute-done((f32[4,8,128]{2,1,0:T(8,128)S(1)}, f32[4,8,128]{2,1,0:T(8,128)S(1)}, u32[]{:S(2)}, u32[]{:S(2)}) %collective-permute-start.1) | collective-permute-done | bytes 16416 | tf_op jit(solution)/shard_map/ppermute | solution.py:317
  37.5 7.8 %all-to-all-done.1.parts = f32[16,4,8,128]{3,2,1,0:T(8,128)S(1)} async-done(((f32[16,4,8,128]{3,2,1,0:T(8,128)}), f32[16,4,8,128]{3,2,1,0:T(8,128)S(1)}, u32[]{:S(2)}, u32[]{:S(2)}) %all-to-all-start.1) | async-done | bytes 262176 | tf_op jit(solution)/shard_map/all_to_all | solution.py:308
  45.4 0.0 copy-done.3
  45.4 0.0 copy-done.8
  45.4 0.7 sum_image.1
  46.1 3.7 %all-to-all-start.2 = ((f32[16,4,8,128]{3,2,1,0:T(8,128)}), f32[16,4,8,128]{3,2,1,0:T(8,128)S(1)}, u32[]{:S(2)}, u32[]{:S(2)}) async-start(f32[16,4,8,128]{3,2,1,0:T(8,128)} %get-tuple-element.27), calls=%async_computation.2 | async-start | bytes 524288 | tf_op jit(solution)/shard_map/all_to_all | solution.py:308
  49.8 0.1 collective-permute-start.2
  49.9 1.2 %collective-permute-done.2.other = f32[4,8,128]{2,1,0:T(8,128)S(1)} collective-permute-done((f32[4,8,128]{2,1,0:T(8,128)S(1)}, f32[4,8,128]{2,1,0:T(8,128)S(1)}, u32[]{:S(2)}, u32[]{:S(2)}) %collective-permute-start.2) | collective-permute-done | bytes 16416 | tf_op jit(solution)/shard_map/ppermute | solution.py:312
  51.1 7.8 %all-to-all-done.2 = f32[16,4,8,128]{3,2,1,0:T(8,128)S(1)} async-done(((f32[16,4,8,128]{3,2,1,0:T(8,128)}), f32[16,4,8,128]{3,2,1,0:T(8,128)S(1)}, u32[]{:S(2)}, u32[]{:S(2)}) %all-to-all-start.2) | async-done | bytes 262176 | tf_op jit(solution)/shard_map/all_to_all | solution.py:308
  58.8 0.0 copy-done.7
  58.8 0.0 copy-done.9
  58.8 0.0 copy-done.11
  58.8 0.0 copy-done.13
  58.9 0.0 copy-start.1
  58.9 2.2 %copy-done.1 = f32[1,1,64,128,128]{4,3,2,1,0:T(8,128)S(1)} copy-done((f32[1,1,64,128,128]{4,3,2,1,0:T(8,128)S(1)}, f32[1,1,64,128,128]{4,3,2,1,0:T(8,128)}, u32[]{:S(2)}) %copy-start.1) | copy-done | bytes 4194328
  61.0 0.7 copy-done.4
  61.8 3.1 %apply_to_image.1 = (f32[4,8,128]{2,1,0:T(8,128)S(1)}, f32[4,8,128]{2,1,0:T(8,128)S(1)}, f32[16,5,8,128]{3,2,1,0:T(8,128)}) custom-call(s32[1]{0:T(128)} %bitcast.10.live, s32[64]{0:T(128)S(1)} %bitcast.19, s32[64]{0:T(128)S(1)} %bitcast.21, s32[1]{0:T(128)} %bitcast.4.here, f32[64,128,128]{2,1,0:T(8,128)S(1)} %bitcast.12, f32[64,8,128]{2,1,0:T(8,128)S(1)} %bitcast.14, ...), custom_call_target="tpu_custom_call" | custom-call | tf_op jit(solution)/shard_map/apply_to_image/pallas_call | solution.py:21
  64.8 3.7 %all-to-all-start.3 = ((f32[16,5,8,128]{3,2,1,0:T(8,128)}), f32[16,5,8,128]{3,2,1,0:T(8,128)S(1)}, u32[]{:S(2)}, u32[]{:S(2)}) async-start(f32[16,5,8,128]{3,2,1,0:T(8,128)} %get-tuple-element.32), calls=%async_computation.3 | async-start | bytes 655360 | tf_op jit(solution)/shard_map/all_to_all | solution.py:308
  68.6 0.1 collective-permute-start.3
  68.6 1.2 %collective-permute-done.3.received = f32[4,8,128]{2,1,0:T(8,128)S(1)} collective-permute-done((f32[4,8,128]{2,1,0:T(8,128)S(1)}, f32[4,8,128]{2,1,0:T(8,128)S(1)}, u32[]{:S(2)}, u32[]{:S(2)}) %collective-permute-start.3) | collective-permute-done | bytes 16416 | tf_op jit(solution)/shard_map/ppermute | solution.py:317
  69.8 9.0 %all-to-all-done.3.parts = f32[16,5,8,128]{3,2,1,0:T(8,128)S(1)} async-done(((f32[16,5,8,128]{3,2,1,0:T(8,128)}), f32[16,5,8,128]{3,2,1,0:T(8,128)S(1)}, u32[]{:S(2)}, u32[]{:S(2)}) %all-to-all-start.3) | async-done | bytes 327712 | tf_op jit(solution)/shard_map/all_to_all | solution.py:308
  78.8 0.0 copy-done.5
  78.9 0.1 collective-permute-start.4
  78.9 1.2 %collective-permute-done.4.theirs = f32[8,128]{1,0:T(8,128)S(1)} collective-permute-done((f32[8,128]{1,0:T(8,128)S(1)}, f32[8,128]{1,0:T(8,128)S(1)}, u32[]{:S(2)}, u32[]{:S(2)}) %collective-permute-start.4) | collective-permute-done | bytes 4128 | tf_op jit(solution)/shard_map/ppermute | solution.py:385
  80.1 3.0 %finish.1 = (f32[8,512]{1,0:T(8,128)}, f32[8,512]{1,0:T(8,128)}, f32[24,24]{1,0:T(8,128)}) custom-call(f32[8,512]{1,0:T(8,128)S(1)} %copy-done.3, f32[8,512]{1,0:T(8,128)S(1)} %copy-done.5, f32[8,512]{1,0:T(8,128)S(1)} %get-tuple-element.33.z_ref, f32[8,128]{1,0:T(8,128)S(1)} %get-tuple-element.34.mine, f32[8,128]{1,0:T(8,128)S(1)} %collective-permute-done.4.theirs), custom_call_target="tpu_custom_call" | custom-call | tf_op jit(solution)/shard_map/finish/pallas_call | solution.py:21
  (4 shorter events, 0.0 us)
Async XLA Ops:
  0.6 0.7 copy-start.2
  1.4 0.7 copy-start.6
  2.1 43.3 %copy-start.3 = (f32[8,512]{1,0:T(8,128)S(1)}, f32[8,512]{1,0:T(8,128)}, u32[]{:S(2)}) copy-start(f32[8,512]{1,0:T(8,128)} %x_ref.7) | copy-start | bytes 49156
  2.1 43.3 %copy-start.8 = (f32[512]{0:T(512)S(1)}, f32[512]{0:T(512)}, u32[]{:S(2)}) copy-start(f32[512]{0:T(512)} %param.12) | copy-start | bytes 6148
  2.1 56.8 %copy-start.7 = (f32[8,512]{1,0:T(8,128)S(1)}, f32[8,512]{1,0:T(8,128)}, u32[]{:S(2)}) copy-start(f32[8,512]{1,0:T(8,128)} %p_ref.3) | copy-start | bytes 49156
  2.1 56.8 %copy-start.9 = (f32[8,512]{1,0:T(8,128)S(1)}, f32[8,512]{1,0:T(8,128)}, u32[]{:S(2)}) copy-start(f32[8,512]{1,0:T(8,128)} %q_ref.1) | copy-start | bytes 49156
  2.1 56.8 %copy-start.11 = (s32[1,1,64]{2,1,0:T(1,128)S(1)}, s32[1,1,64]{2,1,0:T(1,128)}, u32[]{:S(2)}) copy-start(s32[1,1,64]{2,1,0:T(1,128)} %param.9) | copy-start | bytes 772
  2.1 56.8 %copy-start.13 = (s32[1,1,64]{2,1,0:T(1,128)S(1)}, s32[1,1,64]{2,1,0:T(1,128)}, u32[]{:S(2)}) copy-start(s32[1,1,64]{2,1,0:T(1,128)} %param.10) | copy-start | bytes 772
  3.0 23.5 %all-to-all-start = ((f32[16,4,16,128]{3,2,1,0:T(8,128)}), f32[16,4,16,128]{3,2,1,0:T(8,128)S(1)}, u32[]{:S(2)}, u32[]{:S(2)}) async-start(f32[16,4,16,128]{3,2,1,0:T(8,128)} %get-tuple-element.21), calls=%async_computation | async-start | bytes 1048576 | tf_op jit(solution)/shard_map/all_to_all | solution.py:308
  11.3 1.3 %collective-permute-start = (f32[4,16,128]{2,1,0:T(8,128)S(1)}, f32[4,16,128]{2,1,0:T(8,128)S(1)}, u32[]{:S(2)}, u32[]{:S(2)}) collective-permute-start(f32[4,16,128]{2,1,0:T(8,128)S(1)} %get-tuple-element.22.own.pair_own), channel_id=1, source_target_pairs={{0,1},{1,0},{2,3},{3,2},{4,5},{5,4},{6,7},{7,6},{8,9},{9,8},{10,11... | collective-permute-start | bytes 98312 | tf_op jit(solution)/shard_map/ppermute | solution.py:312
  26.4 2.2 %copy-start = (f32[1,1,64,128,128]{4,3,2,1,0:T(8,128)S(1)}, f32[1,1,64,128,128]{4,3,2,1,0:T(8,128)}, u32[]{:S(2)}) copy-start(f32[1,1,64,128,128]{4,3,2,1,0:T(8,128)} %param.8) | copy-start | bytes 12582916
  28.6 0.7 copy-start.10
  29.3 0.7 copy-start.12
  32.4 13.0 %all-to-all-start.1 = ((f32[16,4,8,128]{3,2,1,0:T(8,128)}), f32[16,4,8,128]{3,2,1,0:T(8,128)S(1)}, u32[]{:S(2)}, u32[]{:S(2)}) async-start(f32[16,4,8,128]{3,2,1,0:T(8,128)} %bitcast.7), calls=%async_computation.1 | async-start | bytes 524288 | tf_op jit(solution)/shard_map/all_to_all | solution.py:308
  36.3 1.2 %collective-permute-start.1 = (f32[4,8,128]{2,1,0:T(8,128)S(1)}, f32[4,8,128]{2,1,0:T(8,128)S(1)}, u32[]{:S(2)}, u32[]{:S(2)}) collective-permute-start(f32[4,8,128]{2,1,0:T(8,128)S(1)} %get-tuple-element.24), channel_id=1, source_target_pairs={{0,1},{1,0},{2,3},{3,2},{4,5},{5,4},{6,7},{7,6},{8,9},{9,8},{10,11... | collective-permute-start | bytes 49160 | tf_op jit(solution)/shard_map/ppermute | solution.py:317
  46.1 32.7 %copy-start.5 = (f32[8,512]{1,0:T(8,128)S(1)}, f32[8,512]{1,0:T(8,128)}, u32[]{:S(2)}) copy-start(f32[8,512]{1,0:T(8,128)} %get-tuple-element.17.y_ref) | copy-start | bytes 49156
  46.1 12.7 %all-to-all-start.2 = ((f32[16,4,8,128]{3,2,1,0:T(8,128)}), f32[16,4,8,128]{3,2,1,0:T(8,128)S(1)}, u32[]{:S(2)}, u32[]{:S(2)}) async-start(f32[16,4,8,128]{3,2,1,0:T(8,128)} %get-tuple-element.27), calls=%async_computation.2 | async-start | bytes 524288 | tf_op jit(solution)/shard_map/all_to_all | solution.py:308
  49.8 1.2 %collective-permute-start.2 = (f32[4,8,128]{2,1,0:T(8,128)S(1)}, f32[4,8,128]{2,1,0:T(8,128)S(1)}, u32[]{:S(2)}, u32[]{:S(2)}) collective-permute-start(f32[4,8,128]{2,1,0:T(8,128)S(1)} %get-tuple-element.28.own), channel_id=1, source_target_pairs={{0,1},{1,0},{2,3},{3,2},{4,5},{5,4},{6,7},{7,6},{8,9},{9,8},{10,11... | collective-permute-start | bytes 49160 | tf_op jit(solution)/shard_map/ppermute | solution.py:312
  58.9 2.2 %copy-start.1 = (f32[1,1,64,128,128]{4,3,2,1,0:T(8,128)S(1)}, f32[1,1,64,128,128]{4,3,2,1,0:T(8,128)}, u32[]{:S(2)}) copy-start(f32[1,1,64,128,128]{4,3,2,1,0:T(8,128)} %param.8) | copy-start | bytes 12582916
  61.0 0.7 copy-start.4
  64.8 14.0 %all-to-all-start.3 = ((f32[16,5,8,128]{3,2,1,0:T(8,128)}), f32[16,5,8,128]{3,2,1,0:T(8,128)S(1)}, u32[]{:S(2)}, u32[]{:S(2)}) async-start(f32[16,5,8,128]{3,2,1,0:T(8,128)} %get-tuple-element.32), calls=%async_computation.3 | async-start | bytes 655360 | tf_op jit(solution)/shard_map/all_to_all | solution.py:308
  68.6 1.2 %collective-permute-start.3 = (f32[4,8,128]{2,1,0:T(8,128)S(1)}, f32[4,8,128]{2,1,0:T(8,128)S(1)}, u32[]{:S(2)}, u32[]{:S(2)}) collective-permute-start(f32[4,8,128]{2,1,0:T(8,128)S(1)} %get-tuple-element.31), channel_id=1, source_target_pairs={{0,1},{1,0},{2,3},{3,2},{4,5},{5,4},{6,7},{7,6},{8,9},{9,8},{10,11... | collective-permute-start | bytes 49160 | tf_op jit(solution)/shard_map/ppermute | solution.py:317
  78.9 1.2 %collective-permute-start.4 = (f32[8,128]{1,0:T(8,128)S(1)}, f32[8,128]{1,0:T(8,128)S(1)}, u32[]{:S(2)}, u32[]{:S(2)}) collective-permute-start(f32[8,128]{1,0:T(8,128)S(1)} %get-tuple-element.34.mine), channel_id=1, source_target_pairs={{0,1},{1,0},{2,3},{3,2},{4,5},{5,4},{6,7},{7,6},{8,9},{9,8},{10,11... | collective-permute-start | bytes 12296 | tf_op jit(solution)/shard_map/ppermute | solution.py:385

commit v2 on v0

v2 whole, which is shorter than its diff:
```python
import functools
import math

import jax
import jax.numpy as jnp
from jax import lax
from jax.experimental import pallas as pl
from jax.experimental.pallas import tpu as pltpu
from jax.sharding import PartitionSpec as P

f32 = jnp.float32
bf16 = jnp.bfloat16
highest = lax.Precision.HIGHEST
LANES = 128
in_vmem = pl.BlockSpec(memory_space=pltpu.VMEM)
in_smem = pl.BlockSpec(memory_space=pltpu.SMEM)
in_hbm = pl.BlockSpec(memory_space=pltpu.HBM)
params = pltpu.CompilerParams(vmem_limit_bytes=32 * 2**20)


def call(kernel, name, out_shape, operands, specs, scratch=()):
    return pl.pallas_call(
        kernel,
        out_shape=out_shape,
        in_specs=specs,
        out_specs=jax.tree.map(lambda _: in_vmem, out_shape),
        scratch_shapes=scratch,
        compiler_params=params,
        name=name,
    )(*operands)


def shape(*dims, dtype=f32):
    return jax.ShapeDtypeStruct(dims, dtype)


def halves(values):
    high = values.astype(bf16)
    return high, (values - high.astype(f32)).astype(bf16)


def stacked_halves(values):
    return jnp.concatenate(halves(values), axis=0)


def times_transpose(left, right, precision=None):
    return lax.dot_general(
        left, right, (((1,), (1,)), ((), ())), preferred_element_type=f32, precision=precision
    )


def times(left, right, precision=None):
    return lax.dot_general(
        left, right, (((1,), (0,)), ((), ())), preferred_element_type=f32, precision=precision
    )


def lanes(t):
    return slice(t * LANES, (t + 1) * LANES)


def balanced_sum(terms):
    while len(terms) > 1:
        terms = [sum(terms[n : n + 2]) for n in range(0, len(terms), 2)]
    return terms[0]


def row_block_tiles(t, own, other, paired):
    if paired:
        return [(0, own[:, lanes(t)]), (1, other[:, lanes(t)])]
    return [(c, other[c, :, lanes(t)]) for c in range(other.shape[0])]


class Places:
    def __init__(self, ref, slots, row_tiles, column_tiles, paired):
        self.ref, self.slots, self.live, self.here = ref, slots, ref[0], ref[1]
        self.row_tiles, self.column_tiles = row_tiles, column_tiles
        self.row_shift = ref[1] * (row_tiles // 2) if paired else 0
        self.column_shift = ref[2] * (column_tiles // 2)

    def row(self, slot):
        return lax.rem(self.ref[3 + slot] + self.row_shift, self.row_tiles)

    def column(self, slot):
        return lax.rem(self.ref[3 + self.slots + slot] + self.column_shift, self.column_tiles)

    def weight(self, slot):
        return jnp.where(slot < self.live, 1.0, 0.0).astype(f32)


def group_of(slots):
    return math.gcd(slots, 16)


class Stream:
    def __init__(self, places, blocks, staged, semaphores):
        self.places, self.blocks, self.staged, self.semaphores = places, blocks, staged, semaphores
        self.group = group_of(blocks.shape[0])

    def copy(self, index):
        part = pl.ds(index * self.group, self.group)
        return pltpu.make_async_copy(
            self.blocks.at[part], self.staged.at[part], self.semaphores.at[index]
        )

    def start(self):
        for index in range(self.blocks.shape[0] // self.group):
            @pl.when(index * self.group < self.places.live)
            def _(index=index):
                self.copy(index).start()

    def loop(self, visit):
        def step(index, _):
            self.copy(index).wait()
            visit([index * self.group + s for s in range(self.group)])
            return 0

        lax.fori_loop(0, (self.places.live + self.group - 1) // self.group, step, 0)


def stream_scratch(slots, side):
    return [
        pltpu.VMEM((slots, side, side), f32),
        pltpu.SemaphoreType.DMA((slots // group_of(slots),)),
    ]


def visit_transposed(slots, places, tile, row_halves, column_sum):
    count = column_sum.shape[1]
    products = []
    for slot in slots:
        u = row_halves[places.row(slot)]
        pair = tile(slot)
        both = jnp.concatenate([pair[:, :LANES], pair[:, LANES:]], axis=0)
        product = times(jnp.concatenate([u, u], axis=1), both)
        products.append((product[:count] + product[count:]) * places.weight(slot))
    for slot, product in zip(slots, products):
        column_sum[places.column(slot)] += product


def visit_direct(slots, places, tile, column_halves, row_sum):
    products = []
    for slot in slots:
        x = column_halves[places.column(slot)]
        product = times_transpose(jnp.concatenate([x, x], axis=1), tile(slot))
        products.append((product[:8] + product[8:]) * places.weight(slot))
    for slot, product in zip(slots, products):
        row_sum[places.row(slot)] += product


def tile_from(staged):
    return lambda slot: jnp.concatenate(halves(staged[slot]), axis=1)


def loop_held(places, held, visit):
    group = group_of(held.shape[0])

    def step(index, _):
        visit([index * group + s for s in range(group)])
        return 0

    lax.fori_loop(0, (places.live + group - 1) // group, step, 0)


def transposed_current_kernel(
    paired, places, blocks, own, other, column_sum, held, staged, semaphores, row_halves
):
    places = Places(places, blocks.shape[0], row_halves.shape[0], column_sum.shape[0], paired)
    stream = Stream(places, blocks, staged, semaphores)
    stream.start()
    tiles = own.shape[-1] // LANES
    for t in range(tiles):
        for c, values in row_block_tiles(t, own, other, paired):
            row_halves[c * tiles + t] = stacked_halves(values)
    column_sum[...] = jnp.zeros_like(column_sum)

    def split(slot):
        pair = jnp.concatenate(halves(staged[slot]), axis=1)
        held[slot] = pair
        return pair

    stream.loop(lambda slots: visit_transposed(slots, places, split, row_halves, column_sum))


def assemble_kernel(own, partner, column_sum, payload):
    tiles = own.shape[-1] // LANES
    near = payload.shape[0]
    for n in range(near):
        for t in range(tiles):
            payload[n, t] = own[:, lanes(t)]
            payload[n, tiles + t] = partner[:, lanes(t)]
            payload[n, 2 * tiles + t] = column_sum[n * tiles + t]
            payload[n, 3 * tiles + t] = column_sum[(near + n) * tiles + t]


def assemble_image_kernel(own, partner, column_sum, payload):
    tiles = own.shape[0] - 1
    near = payload.shape[0]
    gram = own[tiles] + partner[tiles]
    for n in range(near):
        for t in range(tiles):
            payload[n, t] = own[t]
            payload[n, tiles + t] = partner[t]
            payload[n, 2 * tiles + t] = column_sum[n * tiles + t, 0:8]
            payload[n, 3 * tiles + t] = column_sum[(near + n) * tiles + t, 0:8]
        payload[n, 4 * tiles] = gram


def partner_sums_kernel(parts, previous, sums):
    near = parts.shape[0]
    tiles = parts.shape[1] // 4
    for t in range(tiles):
        sums[t] = balanced_sum([parts[n, 3 * tiles + t] for n in range(near)])
        sums[tiles + t] = previous[:, lanes(t)]


def fill_column_set(column_halves, parts):
    near = parts.shape[0]
    tiles = parts.shape[1] // 4
    for n in range(near):
        for t in range(tiles):
            column_halves[n * tiles + t] = stacked_halves(parts[n, t])
            column_halves[(near + n) * tiles + t] = stacked_halves(parts[n, tiles + t])


def direct_held_kernel(paired, places, held, parts, row_sum, column_halves):
    places = Places(places, held.shape[0], row_sum.shape[0], column_halves.shape[0], paired)
    fill_column_set(column_halves, parts)
    row_sum[...] = jnp.zeros_like(row_sum)
    loop_held(
        places,
        held,
        lambda slots: visit_direct(slots, places, lambda slot: held[slot], column_halves, row_sum),
    )


def direct_kernel(paired, places, blocks, parts, row_sum, staged, semaphores, column_halves):
    places = Places(places, blocks.shape[0], row_sum.shape[0], column_halves.shape[0], paired)
    stream = Stream(places, blocks, staged, semaphores)
    stream.start()
    fill_column_set(column_halves, parts)
    row_sum[...] = jnp.zeros_like(row_sum)
    stream.loop(
        lambda slots: visit_direct(slots, places, tile_from(staged), column_halves, row_sum)
    )


def combine_kernel(paired, parts, received, row_sum, diagonal, vectors, previous, both, *rows):
    near = parts.shape[0]
    tiles = parts.shape[1] // 4
    for t in range(tiles):
        total = (
            diagonal[:, lanes(t)] * vectors[:, lanes(t)]
            + received[t]
            + balanced_sum([parts[n, 2 * tiles + t] for n in range(near)])
        )
        if paired:
            both[:, lanes(t)] = total + row_sum[t]
            both[:, lanes(tiles + t)] = row_sum[tiles + t]
            both[:, lanes(2 * tiles + t)] = previous[:, lanes(t)]
        else:
            both[:, lanes(t)] = total
            for c in range(rows[0].shape[0]):
                rows[0][c, :, lanes(t)] = row_sum[c * tiles + t]


def image_kernel(paired, mine, theirs, x_ref, p_ref, q_ref, own, other, ship):
    width = x_ref.shape[-1]
    if paired:
        y = mine[:, :width] + theirs[:, width : 2 * width]
        other[...] = theirs[:, :width] + mine[:, width : 2 * width]
    else:
        y = mine[...] + theirs[...]
        other[...] = jnp.zeros_like(other)
    own[...] = y
    x, p, q = x_ref[...], p_ref[...], q_ref[...]
    outer = times_transpose(
        jnp.concatenate([x, y, p], axis=0), jnp.concatenate([x, y, p, q], axis=0), highest
    )
    tiles = width // LANES
    for t in range(tiles):
        ship[t] = y[:, lanes(t)]
    ship[tiles] = jnp.concatenate(
        [
            outer[0:8, 0:24],
            outer[0:8, 24:32] + outer[8:16, 16:24],
            outer[8:16, 8:32],
            outer[16:24, 16:32],
            jnp.zeros((8, LANES - 72), f32),
        ],
        axis=1,
    )


def transposed_image_kernel(
    paired, places, held, own, other, p_ref, p_other, column_sum, sum_halves, row_halves
):
    places = Places(places, held.shape[0], row_halves.shape[0], column_sum.shape[0], paired)
    width = own.shape[-1]
    tiles = width // LANES
    if paired:
        p_other = p_other[:, 2 * width :]
    for t in range(tiles):
        for (c, values), (_, previous) in zip(
            row_block_tiles(t, own, other, paired), row_block_tiles(t, p_ref, p_other, paired)
        ):
            row_halves[c * tiles + t] = stacked_halves(jnp.concatenate([values, previous], axis=0))
    column_sum[...] = jnp.zeros_like(column_sum)
    loop_held(
        places,
        held,
        lambda slots: visit_transposed(
            slots, places, lambda slot: held[slot], row_halves, column_sum
        ),
    )
    for j in range(column_sum.shape[0]):
        sum_halves[j] = stacked_halves(column_sum[j])


def inner_kernel(parts, sum_halves, diagonal, y_ref, p_ref, received, spread, sums, gram):
    near = parts.shape[0]
    tiles = y_ref.shape[-1] // LANES
    column_set = [
        stacked_halves(parts[n, first + t])
        for first in (0, tiles)
        for n in range(near)
        for t in range(tiles)
    ]
    cross = times_transpose(
        jnp.concatenate(column_set, axis=1),
        jnp.concatenate([sum_halves[j] for j in range(sum_halves.shape[0])], axis=1),
    )
    stored = cross[0:8, 0:16] + cross[8:16, 0:16] + cross[0:8, 16:32]
    scaled = diagonal[...] * y_ref[...]

    def summed(tile):
        return balanced_sum([parts[n, tile] for n in range(near)])

    for_partner = [summed(3 * tiles + t) for t in range(tiles)]
    for t in range(tiles):
        sums[t] = for_partner[t]
    gram[...] = summed(4 * tiles)
    for_own = jnp.concatenate([summed(2 * tiles + t) for t in range(tiles)], axis=1)
    yz = times_transpose(scaled, 0.5 * y_ref[...], highest)
    zp = times_transpose(
        jnp.concatenate([scaled + for_own, *for_partner], axis=1),
        jnp.concatenate([p_ref[...]] + [received[tiles + t] for t in range(tiles)], axis=1),
        highest,
    )
    total = stored + jnp.concatenate([yz, zp], axis=1)
    total = jnp.concatenate([total, jnp.zeros((8, LANES - 16), f32)], axis=1)
    for n in range(spread.shape[0]):
        spread[n] = total


def eliminate_kernel(mine, theirs, ritz, inverse, pencil):
    gram = mine[...] + theirs[...]
    turned = gram.T

    def block(n):
        return gram[:, 8 * n : 8 * n + 8]

    def flipped(n):
        return turned[8 * n : 8 * n + 8, :]

    xx, xy, xp, mixed, yy, yp, yq, pp, pq = range(9)
    nothing = jnp.zeros((8, 8), f32)
    unit = (
        lax.broadcasted_iota(jnp.int32, (24, 24), 0) == lax.broadcasted_iota(jnp.int32, (24, 24), 1)
    ).astype(f32)
    work = jnp.concatenate(
        [
            gram[:, 0:24],
            jnp.concatenate([flipped(xy), block(yy), block(yp)], axis=1),
            jnp.concatenate([flipped(xp), flipped(yp), block(pp)], axis=1),
        ],
        axis=0,
    )
    work = jnp.concatenate([work, unit, jnp.zeros((24, LANES - 48), f32)], axis=1)
    pencil[...] = 0.5 * jnp.concatenate(
        [
            jnp.concatenate([block(xy) + flipped(xy), 2.0 * block(yy), block(mixed)], axis=1),
            jnp.concatenate([2.0 * block(yy), nothing, block(yq)], axis=1),
            jnp.concatenate([flipped(mixed), flipped(yq), block(pq) + flipped(pq)], axis=1),
        ],
        axis=0,
    )
    row_ids = lax.broadcasted_iota(jnp.int32, (24, 1), 0)
    for k in range(23):
        if k == 8:
            ritz[...] = work[8:16, 24:32]
        pivot_row = work[k : k + 1, :] / work[k : k + 1, k : k + 1]
        factor = jnp.where(row_ids > k, work[:, k : k + 1], 0.0)
        work = work - factor * pivot_row
    inverse[...] = work[:, 24:48] * lax.rsqrt(jnp.sum(work[:, 0:24] * unit, axis=1, keepdims=True))


def residual_kernel(paired, ritz, x_ref, y_ref, mine, theirs, image, residual, residual_image):
    width = x_ref.shape[-1]
    r = y_ref[...]
    image[...] = r
    s = mine[:, :width] + (theirs[:, width : 2 * width] if paired else theirs[...])
    for j in range(8):
        factor = ritz[:, j : j + 1]
        r = r + factor * x_ref[j : j + 1, :]
        s = s + factor * y_ref[j : j + 1, :]
    residual[...] = r
    residual_image[...] = s


def reduce_kernel(inverse, pencil, parts, reduced):
    total = balanced_sum([parts[n] for n in range(parts.shape[0])])
    turned = total.T
    yz = total[:, 0:8] + turned[0:8, :]
    zp = 0.5 * total[:, 8:16]
    pz = 0.5 * turned[8:16, :]
    nothing = jnp.zeros((8, 8), f32)
    full = pencil[...] + jnp.concatenate(
        [
            jnp.zeros((8, 24), f32),
            jnp.concatenate([nothing, yz, zp], axis=1),
            jnp.concatenate([nothing, pz, nothing], axis=1),
        ],
        axis=0,
    )
    lower = inverse[...]
    reduced[...] = times_transpose(times(lower, full, highest), lower, highest)


def local(tile_values, tile_row, tile_col, counts, diagonal, current, previous, previous_image, *, sizes):
    near, n_col = sizes
    slots, side = tile_values.shape[2], tile_values.shape[-1]
    width = current.shape[1]
    tiles = width // side
    paired = n_col == 2
    row_tiles = n_col * tiles
    column_tiles = 2 * near * tiles
    blocks = pltpu.with_memory_space_constraint(
        tile_values.reshape(slots, side, side), pltpu.HBM
    )
    places = jnp.concatenate(
        [
            counts.reshape(1),
            lax.axis_index("col").reshape(1).astype(jnp.int32),
            lax.axis_index("half").reshape(1).astype(jnp.int32),
            tile_row.reshape(slots),
            tile_col.reshape(slots),
        ]
    )
    diagonal = diagonal.reshape(1, width)

    def swap(values, axis="col"):
        return lax.ppermute(values, axis, [(0, 1), (1, 0)])

    def to_partner(values):
        return swap(values, "half")

    def to_near(values):
        return lax.all_to_all(values, "near", 0, 0, tiled=True)

    def from_columns(values):
        return swap(values) if paired else lax.all_gather(values, "col", axis=0)

    def row_sums_shared(parts, received, row_sum, vectors):
        operands = [parts, received, row_sum, diagonal, vectors, previous]
        specs = [in_vmem] * 6
        kernel = functools.partial(combine_kernel, paired)
        if paired:
            mine = call(kernel, "combine", shape(8, 3 * width), operands, specs)
            return mine, swap(mine)
        mine, rows = call(
            kernel, "combine", [shape(8, width), shape(n_col, 8, width)], operands, specs
        )
        return mine, jnp.sum(lax.all_to_all(rows, "col", 0, 0, tiled=True), axis=0)

    other = from_columns(current)
    partner = to_partner(current)
    column_sum, held = call(
        functools.partial(transposed_current_kernel, paired),
        "transposed_current",
        [shape(column_tiles, 8, side), shape(slots, side, 2 * side, dtype=bf16)],
        [places, blocks, current, other],
        [in_smem, in_hbm] + [in_vmem] * 2,
        stream_scratch(slots, side) + [pltpu.VMEM((row_tiles, 16, side), bf16)],
    )
    payload = call(
        assemble_kernel,
        "assemble_current",
        shape(near, 4 * tiles, 8, side),
        [current, partner, column_sum],
        [in_vmem] * 3,
    )
    parts = to_near(payload)
    sums = call(
        partner_sums_kernel, "partner_sums", shape(2 * tiles, 8, side), [parts, previous], [in_vmem] * 2
    )
    received = to_partner(sums)
    row_sum = call(
        functools.partial(direct_held_kernel, paired),
        "direct_current",
        shape(row_tiles, 8, side),
        [places, held, parts],
        [in_smem] + [in_vmem] * 2,
        [pltpu.VMEM((column_tiles, 16, side), bf16)],
    )
    mine, theirs = row_sums_shared(parts, received, row_sum, current)
    own, other, ship = call(
        functools.partial(image_kernel, paired),
        "image",
        [shape(8, width), shape(8, width), shape(tiles + 1, 8, side)],
        [mine, theirs, current, previous, previous_image],
        [in_vmem] * 5,
    )
    previous_other = theirs
    if not paired:
        other = lax.all_gather(own, "col", axis=0)
        previous_other = lax.all_gather(previous, "col", axis=0)
    partner_ship = to_partner(ship)
    column_sum, sum_halves = call(
        functools.partial(transposed_image_kernel, paired),
        "transposed_image",
        [shape(column_tiles, 16, side), shape(column_tiles, 32, side, dtype=bf16)],
        [places, held, own, other, previous, previous_other],
        [in_smem] + [in_vmem] * 5,
        [pltpu.VMEM((row_tiles, 32, side), bf16)],
    )
    payload = call(
        assemble_image_kernel,
        "assemble_image",
        shape(near, 4 * tiles + 1, 8, side),
        [ship, partner_ship, column_sum],
        [in_vmem] * 3,
    )
    parts = to_near(payload)
    spread, sums, gram = call(
        inner_kernel,
        "inner_products",
        [shape(2 * near * n_col, 8, LANES), shape(tiles, 8, side), shape(8, LANES)],
        [parts, sum_halves, diagonal, own, previous, received],
        [in_vmem] * 6,
    )
    inner_parts = lax.all_to_all(spread, ("half", "near", "col"), 0, 0, tiled=True)
    received = to_partner(sums)
    their_gram = swap(gram) if paired else lax.psum(gram, "col") - gram
    row_sum = call(
        functools.partial(direct_kernel, paired),
        "direct_image",
        shape(row_tiles, 8, side),
        [places, blocks, parts],
        [in_smem, in_hbm, in_vmem],
        stream_scratch(slots, side) + [pltpu.VMEM((column_tiles, 16, side), bf16)],
    )
    ritz, inverse, pencil = call(
        eliminate_kernel,
        "eliminate",
        [shape(8, 8), shape(24, 24), shape(24, 24)],
        [gram, their_gram],
        [in_vmem] * 2,
    )
    mine, theirs = row_sums_shared(parts, received, row_sum, own)
    image, residual, residual_image = call(
        functools.partial(residual_kernel, paired),
        "residuals",
        [shape(8, width)] * 3,
        [ritz, current, own, mine, theirs],
        [in_vmem] * 5,
    )
    reduced = call(
        reduce_kernel, "reduce", shape(24, 24), [inverse, pencil, inner_parts], [in_vmem] * 3
    )
    return (image, residual, residual_image, reduced)


def solution(mesh):
    n_row, n_col = mesh.shape["row"], mesh.shape["col"]
    near = n_row // 2
    cut = jax.sharding.Mesh(mesh.devices.reshape(2, near, n_col), ("half", "near", "col"))
    row = ("half", "near")
    vectors = P(None, ("half", "near", "col"))
    return jax.shard_map(
        functools.partial(local, sizes=(near, n_col)),
        mesh=cut,
        in_specs=(
            P(row, "col", None, None, None),
            P(row, "col", None),
            P(row, "col", None),
            P(row, "col"),
            P(("half", "near", "col")),
            vectors,
            vectors,
            vectors,
        ),
        out_specs=(vectors, vectors, vectors, P()),
        check_vma=False,
    )
```

time: 480 us -> 63.7 us (0.13)
  waiting for transfers between devices: 227 us -> 10.2 us
  blocking collectives: 163 us -> 26.2 us
  other arithmetic: 33.4 us -> 0 us
  matrix products: 30.5 us -> 0 us
  between operations: 14.6 us -> 1.41 us
  Pallas kernels: 0 us -> 13 us
  starting transfers between devices: 0.16 us -> 10.9 us
  local copies, waits for them, and re-layouts: 10.4 us -> 1.48 us
    reduce_scatter x4 -> x0, waiting for transfers between devices: 226 us -> none  [the longest x2 159 us: apply_operator(): lax.psum_scatter(column_sum.reshape(vector_count, -1), 'row', scatter_dim...]
    all_gather x4 -> x0, blocking collectives: 88.4 us -> none  [the longest x2 84.5 us: apply_operator(): column_vectors = lax.all_gather(vectors, 'row', axis=1, tiled=True)]
    psum x2 -> x0, blocking collectives: 74.1 us -> none  [the longest x1 37.2 us: local(): lax.psum((dot_rows(search_basis, search_basis), dot_rows(search_basis, ba...]
    dot_general x21 -> x0, matrix products: 29.1 us -> none  [the longest x8 15.7 us: visit(): jnp.einsum('sij,ksj->ksi', chosen, column_tiles[:, cols_now, :], precisio...]
    all_to_all x0 -> x2, blocking collectives: none -> 26.2 us  [to_near(): return lax.all_to_all(values, 'near', 0, 0, tiled=True)]
    pallas_call x0 -> x14, Pallas kernels: none -> 13 us  [call(): pl.pallas_call(kernel, out_shape=out_shape, in_specs=specs, out_specs=jax...]
    scatter-add x16 -> x0, other arithmetic: 12.6 us -> none  [the longest x8 6.39 us: visit(): row_sum.at[:, rows_now, :].add(direct)]
    ppermute x0 -> x8, waiting for transfers between devices: none -> 10.2 us  [swap(): return lax.ppermute(values, axis, [(0, 1), (1, 0)])]
  transfers between devices with their start and end apart: 4 -> 9, of which waited for: 4 -> 5; matrix products, arithmetic and copies ran while one was open for 0% -> 1% of each run, Pallas kernels for 0% -> 17%
where the time goes in v2:
time: 63.7 us; the launch traced here: 63.1 us
  blocking collectives  26.2 us (41%)
  Pallas kernels  13 us (20%)
  starting transfers between devices  10.9 us (17%)
  waiting for transfers between devices  10.2 us (16%)
  local copies, waits for them, and re-layouts  1.48 us (2%)
  between operations  1.41 us (2%)
    all_to_all x2, blocking collectives, to_near(): return lax.all_to_all(values, 'near', 0, 0, tiled=True)  26.2 us
    pallas_call x14, Pallas kernels, call(): pl.pallas_call(kernel, out_shape=out_shape, in_specs=specs, out_specs=jax...  13 us
    ppermute x8, waiting for transfers between devices, swap(): return lax.ppermute(values, axis, [(0, 1), (1, 0)])  10.2 us
    ppermute x8, starting transfers between devices, swap(): return lax.ppermute(values, axis, [(0, 1), (1, 0)])  8.29 us
    all_to_all x1, starting transfers between devices, local(): lax.all_to_all(spread, ('half', 'near', 'col'), 0, 0, tiled=True)  2.56 us
  transfers between devices with their start and end apart: 9, of which 5 were waited for; matrix products, arithmetic and copies ran while one was open for 1% of the time, Pallas kernels for 17%

profile of v2, /device:TPU:0, one launch (start us, length us, event | category | flops | bytes accessed | tf_op | source)
XLA Modules:
  0.0 63.1 jit_solution(9950598421703548423)
XLA Ops:
  0.6 0.0 copy-start
  0.6 0.5 collective-permute-start.1
  1.2 3.7 %collective-permute-start = (f32[8,512]{1,0:T(8,128)}, f32[8,512]{1,0:T(8,128)S(1)}, u32[]{:S(2)}, u32[]{:S(2)}) collective-permute-start(f32[8,512]{1,0:T(8,128)} %x_ref.3), channel_id=1, source_target_pairs={{0,16},{16,0},{1,17},{17,1},{2,18},{18,2},{3,19},{19,3},{4,20},{20... | collective-permute-start | bytes 49160 | tf_op jit(solution)/shard_map/ppermute | solution.py:453
  5.5 0.7 %concatenate.3.places = s32[131]{0:T(256)S(1)} concatenate(s32[1]{0:T(128)} %bitcast.7, s32[1]{0:T(128)} %bitcast.1, s32[1]{0:T(128)} %bitcast.2, s32[64]{0:T(128)} %bitcast.13, s32[64]{0:T(128)} %bitcast.14), dimensions={0} | concatenate | bytes 1048 | tf_op jit(solution)/shard_map/concatenate | solution.py:441
  6.2 0.0 collective-permute-done.1.other
  6.2 0.0 copy-start.1
  6.2 0.7 %copy-done.1 = f32[8,512]{1,0:T(8,128)S(1)} copy-done((f32[8,512]{1,0:T(8,128)S(1)}, f32[8,512]{1,0:T(8,128)}, u32[]{:S(2)}) %copy-start.1) | copy-done | bytes 16408
  6.9 0.0 copy-start.2
  7.0 2.4 %transposed_current.1 = (f32[64,8,128]{2,1,0:T(8,128)S(1)}, bf16[64,128,256]{2,1,0:T(8,128)(2,1)S(1)}) custom-call(s32[131]{0:T(256)S(1)} %concatenate.3.places, f32[64,128,128]{2,1,0:T(8,128)} %bitcast.11, f32[8,512]{1,0:T(8,128)S(1)} %copy-done.1, f32[8,512]{1,0:T(8,128)S(1)} %collective-permute-done.1.other), custom_call_target="tpu_custom_call" | custom-call | tf_op jit(solution)/shard_map/transposed_current/pallas_call | solution.py:22
  9.4 0.0 copy-start.3
  9.4 0.0 copy-start.4
  9.4 0.0 collective-permute-done.partner
  9.4 0.0 copy-done.2
  9.5 14.3 %all_to_all.15.parts = f32[8,16,8,128]{3,2,1,0:T(8,128)S(1)} all-to-all(f32[8,16,8,128]{3,2,1,0:T(8,128)S(1)} %assemble_current.1), channel_id=1, replica_groups=mesh['half'=2,'near'=8,'col'=2] {'near'}, dimensions={0} | all-to-all | bytes 1048576 | tf_op jit(solution)/shard_map/all_to_all | solution.py:459
  23.7 0.0 copy-done
  23.8 0.4 collective-permute-start.2
  24.2 1.4 %direct_current.1.row_sum = f32[8,8,128]{2,1,0:T(8,128)S(1)} custom-call(s32[131]{0:T(256)S(1)} %concatenate.3.places, bf16[64,128,256]{2,1,0:T(8,128)(2,1)S(1)} %get-tuple-element.21.held, f32[8,16,8,128]{3,2,1,0:T(8,128)S(1)} %all_to_all.15.parts), custom_call_target="tpu_custom_call" | custom-call | tf_op jit(solution)/shard_map/direct_current/pallas_call | solution.py:22
  25.6 3.1 %collective-permute-done.2.received = f32[8,8,128]{2,1,0:T(8,128)S(1)} collective-permute-done((f32[8,8,128]{2,1,0:T(8,128)S(1)}, f32[8,8,128]{2,1,0:T(8,128)S(1)}, u32[]{:S(2)}, u32[]{:S(2)}) %collective-permute-start.2) | collective-permute-done | bytes 32800 | tf_op jit(solution)/shard_map/ppermute | solution.py:453
  28.6 0.0 copy-done.3
  28.7 0.1 collective-permute-start.3
  28.7 1.2 %collective-permute-done.3.theirs.p_other = f32[8,1536]{1,0:T(8,128)S(1)} collective-permute-done((f32[8,1536]{1,0:T(8,128)S(1)}, f32[8,1536]{1,0:T(8,128)S(1)}, u32[]{:S(2)}, u32[]{:S(2)}) %collective-permute-start.3) | collective-permute-done | bytes 49184 | tf_op jit(solution)/shard_map/ppermute | solution.py:453
  30.0 0.0 copy-done.4
  30.0 0.2 image.1
  30.2 0.3 collective-permute-start.4
  30.6 1.2 %transposed_image.1 = (f32[64,16,128]{2,1,0:T(8,128)S(1)}, bf16[64,32,128]{2,1,0:T(8,128)(2,1)S(1)}) custom-call(s32[131]{0:T(256)S(1)} %concatenate.3.places, bf16[64,128,256]{2,1,0:T(8,128)(2,1)S(1)} %get-tuple-element.21.held, f32[8,512]{1,0:T(8,128)S(1)} %get-tuple-element.23.own.y_ref.vectors, f32[8,512]{1,0:T(8,128)S(1)} %get-tuple-element.24.other, ...), custom_call_target="tpu_custom_call" | custom-call | tf_op jit(solution)/shard_map/transposed_image/pallas_call | solution.py:22
  31.8 3.1 %collective-permute-done.4.partner = f32[5,8,128]{2,1,0:T(8,128)S(1)} collective-permute-done((f32[5,8,128]{2,1,0:T(8,128)S(1)}, f32[5,8,128]{2,1,0:T(8,128)S(1)}, u32[]{:S(2)}, u32[]{:S(2)}) %collective-permute-start.4) | collective-permute-done | bytes 20512 | tf_op jit(solution)/shard_map/ppermute | solution.py:453
  34.9 11.9 %all_to_all.16.parts = f32[8,17,8,128]{3,2,1,0:T(8,128)S(1)} all-to-all(f32[8,17,8,128]{3,2,1,0:T(8,128)S(1)} %assemble_image.1), channel_id=1, replica_groups=mesh['half'=2,'near'=8,'col'=2] {'near'}, dimensions={0} | all-to-all | bytes 1114112 | tf_op jit(solution)/shard_map/all_to_all | solution.py:459
  46.9 1.1 %inner_products.1 = (f32[32,8,128]{2,1,0:T(8,128)}, f32[4,8,128]{2,1,0:T(8,128)S(1)}, f32[8,128]{1,0:T(8,128)S(1)}) custom-call(f32[8,17,8,128]{3,2,1,0:T(8,128)S(1)} %all_to_all.16.parts, bf16[64,32,128]{2,1,0:T(8,128)(2,1)S(1)} %get-tuple-element.26.sum_halves, f32[1,512]{1,0:T(1,128)S(1)} %bitcast.9, f32[8,512]{1,0:T(8,128)S(1)} %get-tuple-element.23.own.y_ref.vectors, ...), custom_call_target="tpu_custom_call" | custom-call | tf_op jit(solution)/shard_map/inner_products/pallas_call | solution.py:22
  48.0 2.6 %all-to-all-start.2 = ((f32[32,8,128]{2,1,0:T(8,128)}), f32[32,8,128]{2,1,0:T(8,128)S(1)}, u32[]{:S(2)}, u32[]{:S(2)}) async-start(f32[32,8,128]{2,1,0:T(8,128)} %get-tuple-element.35), calls=%async_computation.2 | async-start | bytes 262144 | tf_op jit(solution)/shard_map/all_to_all | solution.py:542
  50.6 2.7 %collective-permute-start.6 = (f32[4,8,128]{2,1,0:T(8,128)S(1)}, f32[4,8,128]{2,1,0:T(8,128)S(1)}, u32[]{:S(2)}, u32[]{:S(2)}) collective-permute-start(f32[4,8,128]{2,1,0:T(8,128)S(1)} %get-tuple-element.29), channel_id=1, source_target_pairs={{0,16},{16,0},{1,17},{17,1},{2,18},{18,2},{3,19},{19,3},{4,20},{20... | collective-permute-start | bytes 49160 | tf_op jit(solution)/shard_map/ppermute | solution.py:453
  53.3 2.6 %direct_image.1.row_sum = f32[8,8,128]{2,1,0:T(8,128)S(1)} custom-call(s32[131]{0:T(256)S(1)} %concatenate.3.places, f32[64,128,128]{2,1,0:T(8,128)} %bitcast.12, f32[8,17,8,128]{3,2,1,0:T(8,128)S(1)} %all_to_all.16.parts), custom_call_target="tpu_custom_call" | custom-call | tf_op jit(solution)/shard_map/direct_image/pallas_call | solution.py:22
  55.9 1.9 %collective-permute-done.6.received = f32[4,8,128]{2,1,0:T(8,128)S(1)} collective-permute-done((f32[4,8,128]{2,1,0:T(8,128)S(1)}, f32[4,8,128]{2,1,0:T(8,128)S(1)}, u32[]{:S(2)}, u32[]{:S(2)}) %collective-permute-start.6) | collective-permute-done | bytes 16416 | tf_op jit(solution)/shard_map/ppermute | solution.py:453
  57.8 0.1 collective-permute-start.7
  57.9 0.5 collective-permute-start.5
  58.4 0.8 %collective-permute-done.5.theirs = f32[8,128]{1,0:T(8,128)S(1)} collective-permute-done((f32[8,128]{1,0:T(8,128)S(1)}, f32[8,128]{1,0:T(8,128)S(1)}, u32[]{:S(2)}, u32[]{:S(2)}) %collective-permute-start.5) | collective-permute-done | bytes 4128 | tf_op jit(solution)/shard_map/ppermute | solution.py:453
  59.2 2.1 %eliminate.1 = (f32[8,8]{1,0:T(8,128)S(1)}, f32[24,24]{1,0:T(8,128)S(1)}, f32[24,24]{1,0:T(8,128)S(1)}) custom-call(f32[8,128]{1,0:T(8,128)S(1)} %get-tuple-element.27.mine, f32[8,128]{1,0:T(8,128)S(1)} %collective-permute-done.5.theirs), custom_call_target="tpu_custom_call" | custom-call | tf_op jit(solution)/shard_map/eliminate/pallas_call | solution.py:22
  61.3 0.0 collective-permute-done.7.theirs
  61.3 0.7 %residuals.1 = (f32[8,512]{1,0:T(8,128)}, f32[8,512]{1,0:T(8,128)}, f32[8,512]{1,0:T(8,128)}) custom-call(f32[8,8]{1,0:T(8,128)S(1)} %get-tuple-element.28.ritz, f32[8,512]{1,0:T(8,128)S(1)} %copy-done.2, f32[8,512]{1,0:T(8,128)S(1)} %get-tuple-element.23.own.y_ref.vectors, f32[8,1536]{1,0:T(8,128)S(1)} %combine.3.mine, ...), custom_call_target="tpu_custom_call" | custom-call | tf_op jit(solution)/shard_map/residuals/pallas_call | solution.py:22
  62.0 0.0 all-to-all-done.2.parts
  62.0 1.1 %reduce.1 = f32[24,24]{1,0:T(8,128)} custom-call(f32[24,24]{1,0:T(8,128)S(1)} %get-tuple-element.33.inverse, f32[24,24]{1,0:T(8,128)S(1)} %get-tuple-element.34.pencil, f32[32,8,128]{2,1,0:T(8,128)S(1)} %all-to-all-done.2.parts), custom_call_target="tpu_custom_call" | custom-call | tf_op jit(solution)/shard_map/reduce/pallas_call | solution.py:22
  (5 shorter events, 0.1 us)
Async XLA Ops:
  0.6 23.1 %copy-start = (f32[8,512]{1,0:T(8,128)S(1)}, f32[8,512]{1,0:T(8,128)}, u32[]{:S(2)}) copy-start(f32[8,512]{1,0:T(8,128)} %previous.5) | copy-start | bytes 49156
  0.6 5.6 %collective-permute-start.1 = (f32[8,512]{1,0:T(8,128)}, f32[8,512]{1,0:T(8,128)S(1)}, u32[]{:S(2)}, u32[]{:S(2)}) collective-permute-start(f32[8,512]{1,0:T(8,128)} %x_ref.3), channel_id=1, source_target_pairs={{0,1},{1,0},{2,3},{3,2},{4,5},{5,4},{6,7},{7,6},{8,9},{9,8},{10,11... | collective-permute-start | bytes 49160 | tf_op jit(solution)/shard_map/ppermute | solution.py:453
  1.2 8.2 %collective-permute-start = (f32[8,512]{1,0:T(8,128)}, f32[8,512]{1,0:T(8,128)S(1)}, u32[]{:S(2)}, u32[]{:S(2)}) collective-permute-start(f32[8,512]{1,0:T(8,128)} %x_ref.3), channel_id=1, source_target_pairs={{0,16},{16,0},{1,17},{17,1},{2,18},{18,2},{3,19},{19,3},{4,20},{20... | collective-permute-start | bytes 49160 | tf_op jit(solution)/shard_map/ppermute | solution.py:453
  6.2 0.7 %copy-start.1 = (f32[8,512]{1,0:T(8,128)S(1)}, f32[8,512]{1,0:T(8,128)}, u32[]{:S(2)}) copy-start(f32[8,512]{1,0:T(8,128)} %x_ref.3) | copy-start | bytes 49156
  6.9 2.5 %copy-start.2 = (f32[8,512]{1,0:T(8,128)S(1)}, f32[8,512]{1,0:T(8,128)}, u32[]{:S(2)}) copy-start(f32[8,512]{1,0:T(8,128)} %x_ref.3) | copy-start | bytes 49156
  9.4 19.3 %copy-start.3 = (f32[512]{0:T(512)S(1)}, f32[512]{0:T(512)}, u32[]{:S(2)}) copy-start(f32[512]{0:T(512)} %param.12) | copy-start | bytes 6148
  9.4 20.6 %copy-start.4 = (f32[8,512]{1,0:T(8,128)S(1)}, f32[8,512]{1,0:T(8,128)}, u32[]{:S(2)}) copy-start(f32[8,512]{1,0:T(8,128)} %q_ref.1) | copy-start | bytes 49156
  23.8 4.9 %collective-permute-start.2 = (f32[8,8,128]{2,1,0:T(8,128)S(1)}, f32[8,8,128]{2,1,0:T(8,128)S(1)}, u32[]{:S(2)}, u32[]{:S(2)}) collective-permute-start(f32[8,8,128]{2,1,0:T(8,128)S(1)} %partner_sums.1), channel_id=1, source_target_pairs={{0,16},{16,0},{1,17},{17,1},{2,18},{18,2},{3,19},{19,3},{4,20},{20... | collective-permute-start | bytes 98312 | tf_op jit(solution)/shard_map/ppermute | solution.py:453
  28.7 1.3 %collective-permute-start.3 = (f32[8,1536]{1,0:T(8,128)S(1)}, f32[8,1536]{1,0:T(8,128)S(1)}, u32[]{:S(2)}, u32[]{:S(2)}) collective-permute-start(f32[8,1536]{1,0:T(8,128)S(1)} %combine.2.mine), channel_id=1, source_target_pairs={{0,1},{1,0},{2,3},{3,2},{4,5},{5,4},{6,7},{7,6},{8,9},{9,8},{10,11... | collective-permute-start | bytes 147464 | tf_op jit(solution)/shard_map/ppermute | solution.py:453
  30.2 4.7 %collective-permute-start.4 = (f32[5,8,128]{2,1,0:T(8,128)S(1)}, f32[5,8,128]{2,1,0:T(8,128)S(1)}, u32[]{:S(2)}, u32[]{:S(2)}) collective-permute-start(f32[5,8,128]{2,1,0:T(8,128)S(1)} %get-tuple-element.22.own), channel_id=1, source_target_pairs={{0,16},{16,0},{1,17},{17,1},{2,18},{18,2},{3,19},{19,3},{4,20},{20... | collective-permute-start | bytes 61448 | tf_op jit(solution)/shard_map/ppermute | solution.py:453
  48.0 14.1 %all-to-all-start.2 = ((f32[32,8,128]{2,1,0:T(8,128)}), f32[32,8,128]{2,1,0:T(8,128)S(1)}, u32[]{:S(2)}, u32[]{:S(2)}) async-start(f32[32,8,128]{2,1,0:T(8,128)} %get-tuple-element.35), calls=%async_computation.2 | async-start | bytes 262144 | tf_op jit(solution)/shard_map/all_to_all | solution.py:542
  50.6 7.3 %collective-permute-start.6 = (f32[4,8,128]{2,1,0:T(8,128)S(1)}, f32[4,8,128]{2,1,0:T(8,128)S(1)}, u32[]{:S(2)}, u32[]{:S(2)}) collective-permute-start(f32[4,8,128]{2,1,0:T(8,128)S(1)} %get-tuple-element.29), channel_id=1, source_target_pairs={{0,16},{16,0},{1,17},{17,1},{2,18},{18,2},{3,19},{19,3},{4,20},{20... | collective-permute-start | bytes 49160 | tf_op jit(solution)/shard_map/ppermute | solution.py:453
  57.8 3.5 %collective-permute-start.7 = (f32[8,1536]{1,0:T(8,128)S(1)}, f32[8,1536]{1,0:T(8,128)S(1)}, u32[]{:S(2)}, u32[]{:S(2)}) collective-permute-start(f32[8,1536]{1,0:T(8,128)S(1)} %combine.3.mine), channel_id=1, source_target_pairs={{0,1},{1,0},{2,3},{3,2},{4,5},{5,4},{6,7},{7,6},{8,9},{9,8},{10,11... | collective-permute-start | bytes 147464 | tf_op jit(solution)/shard_map/ppermute | solution.py:453
  57.9 1.3 %collective-permute-start.5 = (f32[8,128]{1,0:T(8,128)S(1)}, f32[8,128]{1,0:T(8,128)S(1)}, u32[]{:S(2)}, u32[]{:S(2)}) collective-permute-start(f32[8,128]{1,0:T(8,128)S(1)} %get-tuple-element.27.mine), channel_id=1, source_target_pairs={{0,1},{1,0},{2,3},{3,2},{4,5},{5,4},{6,7},{7,6},{8,9},{9,8},{10,11... | collective-permute-start | bytes 12296 | tf_op jit(solution)/shard_map/ppermute | solution.py:453

commit v3 on v2

--- a/solution.py
+++ b/solution.py
@@ -18,16 +18,27 @@
 params = pltpu.CompilerParams(vmem_limit_bytes=32 * 2**20)
 
 
-def call(kernel, name, out_shape, operands, specs, scratch=()):
+def cost_of(micros):
+    return pl.CostEstimate(flops=0, bytes_accessed=1, transcendentals=0)
+
+
+def call(kernel, name, out_shape, operands, specs, scratch=(), micros=0.1):
     return pl.pallas_call(
         kernel,
         out_shape=out_shape,
         in_specs=specs,
-        out_specs=jax.tree.map(lambda _: in_vmem, out_shape),
+        out_specs=jax.tree.map(
+            lambda out: in_vmem if isinstance(out, jax.ShapeDtypeStruct) else in_smem, out_shape
+        ),
         scratch_shapes=scratch,
         compiler_params=params,
+        cost_estimate=cost_of(micros),
         name=name,
     )(*operands)
+
+
+def kept_in_hbm(values):
+    return pltpu.with_memory_space_constraint(values, pltpu.HBM)
 
 
 def shape(*dims, dtype=f32):
@@ -72,17 +83,18 @@
 
 
 class Places:
-    def __init__(self, ref, slots, row_tiles, column_tiles, paired):
-        self.ref, self.slots, self.live, self.here = ref, slots, ref[0], ref[1]
+    def __init__(self, refs, slots, row_tiles, column_tiles, paired):
+        counts, self.rows, self.columns = refs
+        self.live = counts[0, 0]
         self.row_tiles, self.column_tiles = row_tiles, column_tiles
-        self.row_shift = ref[1] * (row_tiles // 2) if paired else 0
-        self.column_shift = ref[2] * (column_tiles // 2)
+        self.row_shift = lax.axis_index("col") * (row_tiles // 2) if paired else 0
+        self.column_shift = lax.axis_index("half") * (column_tiles // 2)
 
     def row(self, slot):
-        return lax.rem(self.ref[3 + slot] + self.row_shift, self.row_tiles)
+        return lax.rem(self.rows[0, 0, slot] + self.row_shift, self.row_tiles)
 
     def column(self, slot):
-        return lax.rem(self.ref[3 + self.slots + slot] + self.column_shift, self.column_tiles)
+        return lax.rem(self.columns[0, 0, slot] + self.column_shift, self.column_tiles)
 
     def weight(self, slot):
         return jnp.where(slot < self.live, 1.0, 0.0).astype(f32)
@@ -93,9 +105,11 @@
 
 
 class Stream:
-    def __init__(self, places, blocks, staged, semaphores):
-        self.places, self.blocks, self.staged, self.semaphores = places, blocks, staged, semaphores
+    def __init__(self, blocks, staged, semaphores):
+        self.blocks, self.staged, self.semaphores = blocks, staged, semaphores
         self.group = group_of(blocks.shape[0])
+        for index in range(blocks.shape[0] // self.group):
+            self.copy(index).start()
 
     def copy(self, index):
         part = pl.ds(index * self.group, self.group)
@@ -103,19 +117,19 @@
             self.blocks.at[part], self.staged.at[part], self.semaphores.at[index]
         )
 
-    def start(self):
-        for index in range(self.blocks.shape[0] // self.group):
-            @pl.when(index * self.group < self.places.live)
-            def _(index=index):
-                self.copy(index).start()
-
-    def loop(self, visit):
+    def loop(self, live, visit):
         def step(index, _):
             self.copy(index).wait()
             visit([index * self.group + s for s in range(self.group)])
             return 0
 
-        lax.fori_loop(0, (self.places.live + self.group - 1) // self.group, step, 0)
+        def leave(index, _):
+            self.copy(index).wait()
+            return 0
+
+        groups = (live + self.group - 1) // self.group
+        lax.fori_loop(0, groups, step, 0)
+        lax.fori_loop(groups, self.blocks.shape[0] // self.group, leave, 0)
 
 
 def stream_scratch(slots, side):
@@ -163,11 +177,23 @@
 
 
 def transposed_current_kernel(
-    paired, places, blocks, own, other, column_sum, held, staged, semaphores, row_halves
+    paired, *refs
 ):
-    places = Places(places, blocks.shape[0], row_halves.shape[0], column_sum.shape[0], paired)
-    stream = Stream(places, blocks, staged, semaphores)
-    stream.start()
+    counts, rows, columns, blocks, x_ref, other, *refs = refs
+    rows_held, columns_held, column_sum, held, own, semaphore, staged, semaphores, row_halves = refs
+    copies = [
+        pltpu.make_async_copy(source, target, semaphore.at[n])
+        for n, (source, target) in enumerate(
+            [(rows, rows_held), (columns, columns_held), (x_ref, own)]
+        )
+    ]
+    for copy in copies:
+        copy.start()
+    stream = Stream(blocks, staged, semaphores)
+    for copy in copies:
+        copy.wait()
+    refs = counts, rows_held, columns_held
+    places = Places(refs, blocks.shape[0], row_halves.shape[0], column_sum.shape[0], paired)
     tiles = own.shape[-1] // LANES
     for t in range(tiles):
         for c, values in row_block_tiles(t, own, other, paired):
@@ -179,7 +205,7 @@
         held[slot] = pair
         return pair
 
-    stream.loop(lambda slots: visit_transposed(slots, places, split, row_halves, column_sum))
+    stream.loop(places.live, lambda slots: visit_transposed(slots, places, split, row_halves, column_sum))
 
 
 def assemble_kernel(own, partner, column_sum, payload):
@@ -206,12 +232,22 @@
         payload[n, 4 * tiles] = gram
 
 
-def partner_sums_kernel(parts, previous, sums):
+def first_partner_sums_kernel(parts, previous, sums):
     near = parts.shape[0]
     tiles = parts.shape[1] // 4
     for t in range(tiles):
         sums[t] = balanced_sum([parts[n, 3 * tiles + t] for n in range(near)])
         sums[tiles + t] = previous[:, lanes(t)]
+    for t in range(2 * tiles, sums.shape[0]):
+        sums[t] = jnp.zeros_like(sums[t])
+
+
+def partner_sums_kernel(parts, sums, gram):
+    near = parts.shape[0]
+    tiles = parts.shape[1] // 4
+    for t in range(tiles):
+        sums[t] = balanced_sum([parts[n, 3 * tiles + t] for n in range(near)])
+    gram[...] = balanced_sum([parts[n, 4 * tiles] for n in range(near)])
 
 
 def fill_column_set(column_halves, parts):
@@ -223,8 +259,9 @@
             column_halves[(near + n) * tiles + t] = stacked_halves(parts[n, tiles + t])
 
 
-def direct_held_kernel(paired, places, held, parts, row_sum, column_halves):
-    places = Places(places, held.shape[0], row_sum.shape[0], column_halves.shape[0], paired)
+def direct_held_kernel(paired, counts, rows, columns, held, parts, row_sum, column_halves):
+    refs = counts, rows, columns
+    places = Places(refs, held.shape[0], row_sum.shape[0], column_halves.shape[0], paired)
     fill_column_set(column_halves, parts)
     row_sum[...] = jnp.zeros_like(row_sum)
     loop_held(
@@ -234,50 +271,59 @@
     )
 
 
-def direct_kernel(paired, places, blocks, parts, row_sum, staged, semaphores, column_halves):
-    places = Places(places, blocks.shape[0], row_sum.shape[0], column_halves.shape[0], paired)
-    stream = Stream(places, blocks, staged, semaphores)
-    stream.start()
+def direct_kernel(
+    paired, counts, rows, columns, blocks, parts,
+    row_sum, rest,
+    staged, semaphores, column_halves,
+):
+    refs = counts, rows, columns
+    places = Places(refs, blocks.shape[0], row_sum.shape[0], column_halves.shape[0], paired)
+    stream = Stream(blocks, staged, semaphores)
     fill_column_set(column_halves, parts)
     row_sum[...] = jnp.zeros_like(row_sum)
     stream.loop(
-        lambda slots: visit_direct(slots, places, tile_from(staged), column_halves, row_sum)
-    )
-
-
-def combine_kernel(paired, parts, received, row_sum, diagonal, vectors, previous, both, *rows):
+        places.live, lambda slots: visit_direct(slots, places, tile_from(staged), column_halves, row_sum)
+    )
+    for t in range(rest.shape[0]):
+        rest[t] = row_sum[row_sum.shape[0] - rest.shape[0] + t]
+
+
+def half_result(t, parts, diagonal, vectors):
     near = parts.shape[0]
     tiles = parts.shape[1] // 4
+    return diagonal[:, lanes(t)] * vectors[:, lanes(t)] + balanced_sum(
+        [parts[n, 2 * tiles + t] for n in range(near)]
+    )
+
+
+def combine_kernel(paired, parts, row_sum, diagonal, vectors, previous, mine, rows):
+    tiles = parts.shape[1] // 4
     for t in range(tiles):
-        total = (
-            diagonal[:, lanes(t)] * vectors[:, lanes(t)]
-            + received[t]
-            + balanced_sum([parts[n, 2 * tiles + t] for n in range(near)])
-        )
+        total = half_result(t, parts, diagonal, vectors)
         if paired:
-            both[:, lanes(t)] = total + row_sum[t]
-            both[:, lanes(tiles + t)] = row_sum[tiles + t]
-            both[:, lanes(2 * tiles + t)] = previous[:, lanes(t)]
+            mine[:, lanes(t)] = total + row_sum[t]
+            rows[:, lanes(t)] = row_sum[tiles + t]
+            rows[:, lanes(tiles + t)] = previous[:, lanes(t)]
         else:
-            both[:, lanes(t)] = total
-            for c in range(rows[0].shape[0]):
-                rows[0][c, :, lanes(t)] = row_sum[c * tiles + t]
-
-
-def image_kernel(paired, mine, theirs, x_ref, p_ref, q_ref, own, other, ship):
-    width = x_ref.shape[-1]
-    if paired:
-        y = mine[:, :width] + theirs[:, width : 2 * width]
-        other[...] = theirs[:, :width] + mine[:, width : 2 * width]
-    else:
-        y = mine[...] + theirs[...]
-        other[...] = jnp.zeros_like(other)
-    own[...] = y
+            mine[:, lanes(t)] = total
+            for c in range(rows.shape[0]):
+                rows[c, :, lanes(t)] = row_sum[c * tiles + t]
+
+
+def base_kernel(mine, rows, their_mine, their_rows, own, other):
+    width = own.shape[-1]
+    own[...] = mine[...] + their_rows[:, :width]
+    other[...] = their_mine[...] + rows[:, :width]
+
+
+def image_kernel(base, received, x_ref, p_ref, q_ref, image, ship):
+    tiles = image.shape[-1] // LANES
+    y = base[...] + jnp.concatenate([received[t] for t in range(tiles)], axis=1)
+    image[...] = y
     x, p, q = x_ref[...], p_ref[...], q_ref[...]
     outer = times_transpose(
         jnp.concatenate([x, y, p], axis=0), jnp.concatenate([x, y, p, q], axis=0), highest
     )
-    tiles = width // LANES
     for t in range(tiles):
         ship[t] = y[:, lanes(t)]
     ship[tiles] = jnp.concatenate(
@@ -293,13 +339,18 @@
 
 
 def transposed_image_kernel(
-    paired, places, held, own, other, p_ref, p_other, column_sum, sum_halves, row_halves
+    paired, counts, rows, columns, held, own, base_other, sums_other, p_ref, p_other,
+    column_sum, sum_halves,
+    row_halves,
 ):
-    places = Places(places, held.shape[0], row_halves.shape[0], column_sum.shape[0], paired)
+    refs = counts, rows, columns
+    places = Places(refs, held.shape[0], row_halves.shape[0], column_sum.shape[0], paired)
     width = own.shape[-1]
     tiles = width // LANES
+    other = base_other
     if paired:
-        p_other = p_other[:, 2 * width :]
+        other = base_other[...] + jnp.concatenate([sums_other[t] for t in range(tiles)], axis=1)
+        p_other = p_other[:, width:]
     for t in range(tiles):
         for (c, values), (_, previous) in zip(
             row_block_tiles(t, own, other, paired), row_block_tiles(t, p_ref, p_other, paired)
@@ -317,7 +368,7 @@
         sum_halves[j] = stacked_halves(column_sum[j])
 
 
-def inner_kernel(parts, sum_halves, diagonal, y_ref, p_ref, received, spread, sums, gram):
+def inner_kernel(parts, sum_halves, diagonal, y_ref, p_ref, for_partner, first_received, spread):
     near = parts.shape[0]
     tiles = y_ref.shape[-1] // LANES
     column_set = [
@@ -332,19 +383,11 @@
     )
     stored = cross[0:8, 0:16] + cross[8:16, 0:16] + cross[0:8, 16:32]
     scaled = diagonal[...] * y_ref[...]
-
-    def summed(tile):
-        return balanced_sum([parts[n, tile] for n in range(near)])
-
-    for_partner = [summed(3 * tiles + t) for t in range(tiles)]
-    for t in range(tiles):
-        sums[t] = for_partner[t]
-    gram[...] = summed(4 * tiles)
-    for_own = jnp.concatenate([summed(2 * tiles + t) for t in range(tiles)], axis=1)
+    halved = jnp.concatenate([half_result(t, parts, diagonal, y_ref) for t in range(tiles)], axis=1)
     yz = times_transpose(scaled, 0.5 * y_ref[...], highest)
     zp = times_transpose(
-        jnp.concatenate([scaled + for_own, *for_partner], axis=1),
-        jnp.concatenate([p_ref[...]] + [received[tiles + t] for t in range(tiles)], axis=1),
+        jnp.concatenate([halved] + [for_partner[t] for t in range(tiles)], axis=1),
+        jnp.concatenate([p_ref[...]] + [first_received[tiles + t] for t in range(tiles)], axis=1),
         highest,
     )
     total = stored + jnp.concatenate([yz, zp], axis=1)
@@ -386,26 +429,41 @@
         axis=0,
     )
     row_ids = lax.broadcasted_iota(jnp.int32, (24, 1), 0)
-    for k in range(23):
+    for k in range(0, 24, 2):
         if k == 8:
             ritz[...] = work[8:16, 24:32]
-        pivot_row = work[k : k + 1, :] / work[k : k + 1, k : k + 1]
-        factor = jnp.where(row_ids > k, work[:, k : k + 1], 0.0)
-        work = work - factor * pivot_row
+        row, next_row = work[k : k + 1, :], work[k + 1 : k + 2, :]
+        column = jnp.broadcast_to(work[:, k : k + 1], work.shape)
+        next_column = jnp.broadcast_to(work[:, k + 1 : k + 2], work.shape)
+        first, cross, second = column[k : k + 1], column[k + 1 : k + 2], next_column[k + 1 : k + 2]
+        scale = 1.0 / first
+        next_scale = first / (first * second - cross * cross)
+        ratio = cross * scale
+        work = (
+            work
+            - jnp.where(row_ids > k, column, 0.0) * (row * scale)
+            - jnp.where(row_ids > k + 1, next_column - column * ratio, 0.0)
+            * ((next_row - ratio * row) * next_scale)
+        )
     inverse[...] = work[:, 24:48] * lax.rsqrt(jnp.sum(work[:, 0:24] * unit, axis=1, keepdims=True))
 
 
-def residual_kernel(paired, ritz, x_ref, y_ref, mine, theirs, image, residual, residual_image):
-    width = x_ref.shape[-1]
-    r = y_ref[...]
-    image[...] = r
-    s = mine[:, :width] + (theirs[:, width : 2 * width] if paired else theirs[...])
-    for j in range(8):
-        factor = ritz[:, j : j + 1]
-        r = r + factor * x_ref[j : j + 1, :]
-        s = s + factor * y_ref[j : j + 1, :]
-    residual[...] = r
-    residual_image[...] = s
+def residual_kernel(
+    paired, ritz, x_ref, y_ref, parts, received, row_sum, theirs, diagonal,
+    image, residual, residual_image,
+):
+    image[...] = y_ref[...]
+    for t in range(theirs.shape[0]):
+        r = y_ref[:, lanes(t)]
+        s = half_result(t, parts, diagonal, y_ref) + received[t] + theirs[t]
+        if paired:
+            s = s + row_sum[t]
+        for j in range(8):
+            factor = ritz[:, j : j + 1]
+            r = r + factor * x_ref[j : j + 1, lanes(t)]
+            s = s + factor * y_ref[j : j + 1, lanes(t)]
+        residual[:, lanes(t)] = r
+        residual_image[:, lanes(t)] = s
 
 
 def reduce_kernel(inverse, pencil, parts, reduced):
@@ -435,18 +493,8 @@
     paired = n_col == 2
     row_tiles = n_col * tiles
     column_tiles = 2 * near * tiles
-    blocks = pltpu.with_memory_space_constraint(
-        tile_values.reshape(slots, side, side), pltpu.HBM
-    )
-    places = jnp.concatenate(
-        [
-            counts.reshape(1),
-            lax.axis_index("col").reshape(1).astype(jnp.int32),
-            lax.axis_index("half").reshape(1).astype(jnp.int32),
-            tile_row.reshape(slots),
-            tile_col.reshape(slots),
-        ]
-    )
+    blocks = kept_in_hbm(tile_values.reshape(slots, side, side))
+    places = [counts, tile_row, tile_col]
     diagonal = diagonal.reshape(1, width)
 
     def swap(values, axis="col"):
@@ -461,28 +509,21 @@
     def from_columns(values):
         return swap(values) if paired else lax.all_gather(values, "col", axis=0)
 
-    def row_sums_shared(parts, received, row_sum, vectors):
-        operands = [parts, received, row_sum, diagonal, vectors, previous]
-        specs = [in_vmem] * 6
-        kernel = functools.partial(combine_kernel, paired)
-        if paired:
-            mine = call(kernel, "combine", shape(8, 3 * width), operands, specs)
-            return mine, swap(mine)
-        mine, rows = call(
-            kernel, "combine", [shape(8, width), shape(n_col, 8, width)], operands, specs
-        )
-        return mine, jnp.sum(lax.all_to_all(rows, "col", 0, 0, tiled=True), axis=0)
-
     other = from_columns(current)
     partner = to_partner(current)
-    column_sum, held = call(
+    *held_places, column_sum, held = call(
         functools.partial(transposed_current_kernel, paired),
         "transposed_current",
-        [shape(column_tiles, 8, side), shape(slots, side, 2 * side, dtype=bf16)],
-        [places, blocks, current, other],
-        [in_smem, in_hbm] + [in_vmem] * 2,
-        stream_scratch(slots, side) + [pltpu.VMEM((row_tiles, 16, side), bf16)],
-    )
+        [pltpu.SMEM(part.shape, part.dtype) for part in places[1:]]
+        + [shape(column_tiles, 8, side), shape(slots, side, 2 * side, dtype=bf16)],
+        [counts, *map(kept_in_hbm, places[1:]), blocks, kept_in_hbm(current), other],
+        [in_smem] + [in_hbm] * 4 + [in_vmem],
+        [pltpu.VMEM((8, width), f32), pltpu.SemaphoreType.DMA((3,))]
+        + stream_scratch(slots, side)
+        + [pltpu.VMEM((row_tiles, 16, side), bf16)],
+        micros=3.0,
+    )
+    places[1:] = [pltpu.with_memory_space_constraint(part, pltpu.SMEM) for part in held_places]
     payload = call(
         assemble_kernel,
         "assemble_current",
@@ -492,37 +533,61 @@
     )
     parts = to_near(payload)
     sums = call(
-        partner_sums_kernel, "partner_sums", shape(2 * tiles, 8, side), [parts, previous], [in_vmem] * 2
-    )
-    received = to_partner(sums)
+        first_partner_sums_kernel,
+        "partner_sums",
+        shape(2 * tiles + 1, 8, side),
+        [parts, previous],
+        [in_vmem] * 2,
+    )
+    first_received = to_partner(sums)
     row_sum = call(
         functools.partial(direct_held_kernel, paired),
         "direct_current",
         shape(row_tiles, 8, side),
-        [places, held, parts],
-        [in_smem] + [in_vmem] * 2,
+        [*places, held, parts],
+        [in_smem] * 3 + [in_vmem] * 2,
         [pltpu.VMEM((column_tiles, 16, side), bf16)],
-    )
-    mine, theirs = row_sums_shared(parts, received, row_sum, current)
-    own, other, ship = call(
-        functools.partial(image_kernel, paired),
+        micros=2.2,
+    )
+    mine, rows = call(
+        functools.partial(combine_kernel, paired),
+        "combine",
+        [shape(8, width), shape(8, 2 * width) if paired else shape(n_col, 8, width)],
+        [parts, row_sum, diagonal, current, previous],
+        [in_vmem] * 5,
+    )
+    if paired:
+        previous_other = swap(rows)
+        base, base_other = call(
+            base_kernel,
+            "base",
+            [shape(8, width)] * 2,
+            [mine, rows, swap(mine), previous_other],
+            [in_vmem] * 4,
+        )
+        sums_other = swap(first_received[:tiles])
+    else:
+        base = mine + jnp.sum(lax.all_to_all(rows, "col", 0, 0, tiled=True), axis=0)
+        sums_other = first_received
+        previous_other = lax.all_gather(previous, "col", axis=0)
+    image, ship = call(
+        image_kernel,
         "image",
-        [shape(8, width), shape(8, width), shape(tiles + 1, 8, side)],
-        [mine, theirs, current, previous, previous_image],
+        [shape(8, width), shape(tiles + 1, 8, side)],
+        [base, first_received, current, previous, previous_image],
         [in_vmem] * 5,
     )
-    previous_other = theirs
+    partner_ship = to_partner(ship)
     if not paired:
-        other = lax.all_gather(own, "col", axis=0)
-        previous_other = lax.all_gather(previous, "col", axis=0)
-    partner_ship = to_partner(ship)
+        base_other = lax.all_gather(image, "col", axis=0)
     column_sum, sum_halves = call(
         functools.partial(transposed_image_kernel, paired),
         "transposed_image",
         [shape(column_tiles, 16, side), shape(column_tiles, 32, side, dtype=bf16)],
-        [places, held, own, other, previous, previous_other],
-        [in_smem] + [in_vmem] * 5,
+        [*places, held, image, base_other, sums_other, previous, previous_other],
+        [in_smem] * 3 + [in_vmem] * 6,
         [pltpu.VMEM((row_tiles, 32, side), bf16)],
+        micros=1.8,
     )
     payload = call(
         assemble_image_kernel,
@@ -532,41 +597,61 @@
         [in_vmem] * 3,
     )
     parts = to_near(payload)
-    spread, sums, gram = call(
+    for_partner, gram = call(
+        partner_sums_kernel,
+        "partner_sums",
+        [shape(tiles, 8, side), shape(8, LANES)],
+        [parts],
+        [in_vmem],
+    )
+    received = to_partner(for_partner)
+    their_gram = swap(gram) if paired else lax.psum(gram, "col") - gram
+    spread = call(
         inner_kernel,
         "inner_products",
-        [shape(2 * near * n_col, 8, LANES), shape(tiles, 8, side), shape(8, LANES)],
-        [parts, sum_halves, diagonal, own, previous, received],
-        [in_vmem] * 6,
+        shape(2 * near * n_col, 8, LANES),
+        [parts, sum_halves, diagonal, image, previous, for_partner, first_received],
+        [in_vmem] * 7,
+        micros=1.1,
     )
     inner_parts = lax.all_to_all(spread, ("half", "near", "col"), 0, 0, tiled=True)
-    received = to_partner(sums)
-    their_gram = swap(gram) if paired else lax.psum(gram, "col") - gram
-    row_sum = call(
+    row_sum, rest = call(
         functools.partial(direct_kernel, paired),
         "direct_image",
-        shape(row_tiles, 8, side),
-        [places, blocks, parts],
-        [in_smem, in_hbm, in_vmem],
+        [shape(row_tiles, 8, side), shape(tiles if paired else row_tiles, 8, side)],
+        [*places, blocks, parts],
+        [in_smem] * 3 + [in_hbm, in_vmem],
         stream_scratch(slots, side) + [pltpu.VMEM((column_tiles, 16, side), bf16)],
-    )
+        micros=3.4,
+    )
+    if paired:
+        theirs = swap(rest)
+    else:
+        rest = rest.reshape(n_col, tiles, 8, side)
+        theirs = jnp.sum(lax.all_to_all(rest, "col", 0, 0, tiled=True), axis=0)
     ritz, inverse, pencil = call(
         eliminate_kernel,
         "eliminate",
         [shape(8, 8), shape(24, 24), shape(24, 24)],
         [gram, their_gram],
         [in_vmem] * 2,
-    )
-    mine, theirs = row_sums_shared(parts, received, row_sum, own)
+        micros=2.1,
+    )
     image, residual, residual_image = call(
         functools.partial(residual_kernel, paired),
         "residuals",
         [shape(8, width)] * 3,
-        [ritz, current, own, mine, theirs],
-        [in_vmem] * 5,
+        [ritz, current, image, parts, received, row_sum, theirs, diagonal],
+        [in_vmem] * 8,
+        micros=0.7,
     )
     reduced = call(
-        reduce_kernel, "reduce", shape(24, 24), [inverse, pencil, inner_parts], [in_vmem] * 3
+        reduce_kernel,
+        "reduce",
+        shape(24, 24),
+        [inverse, pencil, inner_parts],
+        [in_vmem] * 3,
+        micros=1.0,
     )
     return (image, residual, residual_image, reduced)
 

time: 63.7 us -> 57.5 us (0.903)
  waiting for transfers between devices: 10.2 us -> 7.09 us
  Pallas kernels: 13 us -> 10.6 us
  local copies, waits for them, and re-layouts: 1.48 us -> 0.02 us
  starting transfers between devices: 10.9 us -> 12.2 us
    ppermute x8 -> x10, waiting for transfers between devices: 10.2 us -> 7.09 us  [swap(): return lax.ppermute(values, axis, [(0, 1), (1, 0)])]
    pallas_call x14 -> x15, Pallas kernels: 13 us -> 10.6 us  [call(): pl.pallas_call(kernel, out_shape=out_shape, in_specs=specs, out_specs=jax...]
    ppermute x8 -> x10, starting transfers between devices: 8.29 us -> 9.62 us  [swap(): return lax.ppermute(values, axis, [(0, 1), (1, 0)])]
    concatenate x1 -> x0, local copies, waits for them, and re-layouts: 0.75 us -> none  [local(): jnp.concatenate([counts.reshape(1), lax.axis_index('col').reshape(1).asty...]
    unnamed x10 -> x8, local copies, waits for them, and re-layouts: 0.74 us -> 0.02 us
  transfers between devices with their start and end apart: 9 -> 11, of which waited for: 5 -> 5; matrix products, arithmetic and copies ran while one was open for 1% -> 0% of each run, Pallas kernels for 17% -> 14%
where the time goes in v3:
time: 57.5 us
  blocking collectives  26.1 us (45%)
  starting transfers between devices  12.2 us (21%)
  Pallas kernels  10.6 us (18%)
  waiting for transfers between devices  7.09 us (12%)
  between operations  1.44 us (3%)
    all_to_all x2, blocking collectives, to_near(): return lax.all_to_all(values, 'near', 0, 0, tiled=True)  26.1 us
    pallas_call x15, Pallas kernels, call(): pl.pallas_call(kernel, out_shape=out_shape, in_specs=specs, out_specs=jax...  10.6 us
    ppermute x10, starting transfers between devices, swap(): return lax.ppermute(values, axis, [(0, 1), (1, 0)])  9.62 us
    ppermute x10, waiting for transfers between devices, swap(): return lax.ppermute(values, axis, [(0, 1), (1, 0)])  7.09 us
    all_to_all x1, starting transfers between devices, local(): lax.all_to_all(spread, ('half', 'near', 'col'), 0, 0, tiled=True)  2.56 us
  transfers between devices with their start and end apart: 11, of which 5 were waited for; matrix products, arithmetic and copies ran while one was open for 0% of the time, Pallas kernels for 14%

profile of v3, /device:TPU:0, one launch (start us, length us, event | category | flops | bytes accessed | tf_op | source)
XLA Modules:
  0.0 57.5 jit_solution(7731665046055142701)
XLA Ops:
  0.6 0.0 copy-start.1
  0.6 0.0 copy-start
  0.7 0.5 collective-permute-start.1
  1.2 3.7 %collective-permute-start = (f32[8,512]{1,0:T(8,128)}, f32[8,512]{1,0:T(8,128)S(1)}, u32[]{:S(2)}, u32[]{:S(2)}) collective-permute-start(f32[8,512]{1,0:T(8,128)} %x_ref.3), channel_id=1, source_target_pairs={{0,16},{16,0},{1,17},{17,1},{2,18},{18,2},{3,19},{19,3},{4,20},{20... | collective-permute-start | bytes 49160 | tf_op jit(solution)/shard_map/ppermute | solution.py:501
  5.5 0.0 collective-permute-done.1.refs_5_
  5.5 2.3 %transposed_current.1 = (s32[1,1,64]{2,1,0:T(1,128)S(4)}, s32[1,1,64]{2,1,0:T(1,128)S(4)}, f32[64,8,128]{2,1,0:T(8,128)S(1)}, bf16[64,128,256]{2,1,0:T(8,128)(2,1)S(1)}) custom-call(s32[1,1]{1,0:T(1,128)S(6)} %copy.12.refs_0_.counts, s32[1,1,64]{2,1,0:T(1,128)} %refs_1_.1, s32[1,1,64]{2,1,0:T(1,128)} %refs_2_.1, f32[64,128,128]{2,1,0:T(8,128)} %bitcast.5, ...), custom_call_target="tpu_custom_call" | custom-call | bytes 1 | tf_op jit(solution)/shard_map/transposed_current/pallas_call | solution.py:26
  7.8 0.0 copy-start.2
  7.9 0.0 copy-start.3
  7.9 0.0 collective-permute-done.partner
  7.9 0.0 copy-done.1
  7.9 14.6 %all_to_all.15.parts = f32[8,16,8,128]{3,2,1,0:T(8,128)S(1)} all-to-all(f32[8,16,8,128]{3,2,1,0:T(8,128)S(1)} %assemble_current.1), channel_id=1, replica_groups=mesh['half'=2,'near'=8,'col'=2] {'near'}, dimensions={0} | all-to-all | bytes 1048576 | tf_op jit(solution)/shard_map/all_to_all | solution.py:507
  22.5 0.0 copy-done
  22.5 0.8 %collective-permute-start.4 = (f32[9,8,128]{2,1,0:T(8,128)S(1)}, f32[9,8,128]{2,1,0:T(8,128)S(1)}, u32[]{:S(2)}, u32[]{:S(2)}) collective-permute-start(f32[9,8,128]{2,1,0:T(8,128)S(1)} %partner_sums.2), channel_id=1, source_target_pairs={{0,16},{16,0},{1,17},{17,1},{2,18},{18,2},{3,19},{19,3},{4,20},{20... | collective-permute-start | bytes 110600 | tf_op jit(solution)/shard_map/ppermute | solution.py:501
  23.3 0.8 %direct_current.1.row_sum = f32[8,8,128]{2,1,0:T(8,128)S(1)} custom-call(s32[1,1]{1,0:T(1,128)S(6)} %copy.12.refs_0_.counts, s32[1,1,64]{2,1,0:T(1,128)S(4)} %get-tuple-element.27.rows, s32[1,1,64]{2,1,0:T(1,128)S(4)} %get-tuple-element.28.columns, bf16[64,128,256]{2,1,0:T(8,128)(2,1)S(1)} %get-tuple-element.29.held, f32[8,16,8,128]{3,2,1,0:T(8,128)S(1)} %all_to_all.15.parts), custom_call_target="tpu_custom_call" | custom-call | bytes 1 | tf_op jit(solution)/shard_map/direct_current/pallas_call | solution.py:26
  24.1 0.0 copy-done.2
  24.2 0.1 collective-permute-start.3
  24.3 0.5 collective-permute-start.2
  24.8 0.8 %collective-permute-done.2.their_mine = f32[8,512]{1,0:T(8,128)S(1)} collective-permute-done((f32[8,512]{1,0:T(8,128)S(1)}, f32[8,512]{1,0:T(8,128)S(1)}, u32[]{:S(2)}, u32[]{:S(2)}) %collective-permute-start.2) | collective-permute-done | bytes 16416 | tf_op jit(solution)/shard_map/ppermute | solution.py:501
  25.6 0.0 collective-permute-done.3.their_rows.p_other
  25.6 1.8 %collective-permute-done.4.received.first_received = f32[9,8,128]{2,1,0:T(8,128)S(1)} collective-permute-done((f32[9,8,128]{2,1,0:T(8,128)S(1)}, f32[9,8,128]{2,1,0:T(8,128)S(1)}, u32[]{:S(2)}, u32[]{:S(2)}) %collective-permute-start.4) | collective-permute-done | bytes 36896 | tf_op jit(solution)/shard_map/ppermute | solution.py:501
  27.5 0.0 copy-done.3
  27.5 0.2 image.1
  27.7 0.7 %collective-permute-start.5 = (f32[5,8,128]{2,1,0:T(8,128)S(1)}, f32[5,8,128]{2,1,0:T(8,128)S(1)}, u32[]{:S(2)}, u32[]{:S(2)}) collective-permute-start(f32[5,8,128]{2,1,0:T(8,128)S(1)} %get-tuple-element.33.own), channel_id=1, source_target_pairs={{0,16},{16,0},{1,17},{17,1},{2,18},{18,2},{3,19},{19,3},{4,20},{20... | collective-permute-start | bytes 61448 | tf_op jit(solution)/shard_map/ppermute | solution.py:501
  28.4 0.0 collective-permute-start.6
  28.4 1.2 %collective-permute-done.6.sums_other = f32[4,8,128]{2,1,0:T(8,128)S(1)} collective-permute-done((f32[4,8,128]{2,1,0:T(8,128)S(1)}, f32[4,8,128]{2,1,0:T(8,128)S(1)}, u32[]{:S(2)}, u32[]{:S(2)}) %collective-permute-start.6) | collective-permute-done | bytes 16416 | tf_op jit(solution)/shard_map/ppermute | solution.py:501
  29.6 0.7 %transposed_image.1 = (f32[64,16,128]{2,1,0:T(8,128)S(1)}, bf16[64,32,128]{2,1,0:T(8,128)(2,1)S(1)}) custom-call(s32[1,1]{1,0:T(1,128)S(6)} %copy.12.refs_0_.counts, s32[1,1,64]{2,1,0:T(1,128)S(4)} %get-tuple-element.27.rows, s32[1,1,64]{2,1,0:T(1,128)S(4)} %get-tuple-element.28.columns, bf16[64,128,256]{2,1,0:T(8,128)(2,1)S(1)} %get-tuple-element.29.held, ...), custom_call_target="tpu_custom_call" | custom-call | bytes 1 | tf_op jit(solution)/shard_map/transposed_image/pallas_call | solution.py:26
  30.3 2.1 %collective-permute-done.5.partner = f32[5,8,128]{2,1,0:T(8,128)S(1)} collective-permute-done((f32[5,8,128]{2,1,0:T(8,128)S(1)}, f32[5,8,128]{2,1,0:T(8,128)S(1)}, u32[]{:S(2)}, u32[]{:S(2)}) %collective-permute-start.5) | collective-permute-done | bytes 20512 | tf_op jit(solution)/shard_map/ppermute | solution.py:501
  32.4 11.5 %all_to_all.16.parts = f32[8,17,8,128]{3,2,1,0:T(8,128)S(1)} all-to-all(f32[8,17,8,128]{3,2,1,0:T(8,128)S(1)} %assemble_image.1), channel_id=1, replica_groups=mesh['half'=2,'near'=8,'col'=2] {'near'}, dimensions={0} | all-to-all | bytes 1114112 | tf_op jit(solution)/shard_map/all_to_all | solution.py:507
  44.0 1.1 %inner_products.1 = f32[32,8,128]{2,1,0:T(8,128)} custom-call(f32[8,17,8,128]{3,2,1,0:T(8,128)S(1)} %all_to_all.16.parts, bf16[64,32,128]{2,1,0:T(8,128)(2,1)S(1)} %get-tuple-element.47.sum_halves, f32[1,512]{1,0:T(1,128)S(1)} %bitcast.3, f32[8,512]{1,0:T(8,128)S(1)} %get-tuple-element.34.own.y_ref, f32[8,512]{1,0:T(8,128)S(1)} %copy-done, ...), custom_call_target="tpu_custom_call" | custom-call | bytes 1 | tf_op jit(solution)/shard_map/inner_products/pallas_call | solution.py:26
  45.1 2.6 %all-to-all-start.2 = ((f32[32,8,128]{2,1,0:T(8,128)}), f32[32,8,128]{2,1,0:T(8,128)S(1)}, u32[]{:S(2)}, u32[]{:S(2)}) async-start(f32[32,8,128]{2,1,0:T(8,128)} %inner_products.1), calls=%async_computation.2 | async-start | bytes 262144 | tf_op jit(solution)/shard_map/all_to_all | solution.py:617
  47.6 2.7 %collective-permute-start.8 = (f32[4,8,128]{2,1,0:T(8,128)S(1)}, f32[4,8,128]{2,1,0:T(8,128)S(1)}, u32[]{:S(2)}, u32[]{:S(2)}) collective-permute-start(f32[4,8,128]{2,1,0:T(8,128)S(1)} %get-tuple-element.39.for_partner), channel_id=1, source_target_pairs={{0,16},{16,0},{1,17},{17,1},{2,18},{18,2},{3,19},{19,3},{4,20},{20... | collective-permute-start | bytes 49160 | tf_op jit(solution)/shard_map/ppermute | solution.py:501
  50.3 2.2 %direct_image.1 = (f32[8,8,128]{2,1,0:T(8,128)S(1)}, f32[4,8,128]{2,1,0:T(8,128)S(1)}) custom-call(s32[1,1]{1,0:T(1,128)S(6)} %copy.12.refs_0_.counts, s32[1,1,64]{2,1,0:T(1,128)S(4)} %get-tuple-element.27.rows, s32[1,1,64]{2,1,0:T(1,128)S(4)} %get-tuple-element.28.columns, f32[64,128,128]{2,1,0:T(8,128)} %bitcast.6, f32[8,17,8,128]{3,2,1,0:T(8,128)S(1)} %all_to_all.16.parts), custom_call_target="tpu_custom_call" | custom-call | bytes 1 | tf_op jit(solution)/shard_map/direct_image/pallas_call | solution.py:26
  52.6 0.6 %collective-permute-start.9 = (f32[4,8,128]{2,1,0:T(8,128)S(1)}, f32[4,8,128]{2,1,0:T(8,128)S(1)}, u32[]{:S(2)}, u32[]{:S(2)}) collective-permute-start(f32[4,8,128]{2,1,0:T(8,128)S(1)} %get-tuple-element.41), channel_id=1, source_target_pairs={{0,1},{1,0},{2,3},{3,2},{4,5},{5,4},{6,7},{7,6},{8,9},{9,8},{10,11... | collective-permute-start | bytes 49160 | tf_op jit(solution)/shard_map/ppermute | solution.py:501
  53.1 0.1 collective-permute-start.7
  53.2 1.1 %collective-permute-done.7.theirs = f32[8,128]{1,0:T(8,128)S(1)} collective-permute-done((f32[8,128]{1,0:T(8,128)S(1)}, f32[8,128]{1,0:T(8,128)S(1)}, u32[]{:S(2)}, u32[]{:S(2)}) %collective-permute-start.7) | collective-permute-done | bytes 4128 | tf_op jit(solution)/shard_map/ppermute | solution.py:501
  54.3 1.3 %eliminate.1 = (f32[8,8]{1,0:T(8,128)S(1)}, f32[24,24]{1,0:T(8,128)S(1)}, f32[24,24]{1,0:T(8,128)S(1)}) custom-call(f32[8,128]{1,0:T(8,128)S(1)} %get-tuple-element.37.mine, f32[8,128]{1,0:T(8,128)S(1)} %collective-permute-done.7.theirs), custom_call_target="tpu_custom_call" | custom-call | bytes 1 | tf_op jit(solution)/shard_map/eliminate/pallas_call | solution.py:26
  55.6 0.0 collective-permute-done.8.received
  55.6 0.0 collective-permute-done.9.theirs
  55.7 0.7 %residuals.1 = (f32[8,512]{1,0:T(8,128)}, f32[8,512]{1,0:T(8,128)}, f32[8,512]{1,0:T(8,128)}) custom-call(f32[8,8]{1,0:T(8,128)S(1)} %get-tuple-element.38.ritz, f32[8,512]{1,0:T(8,128)S(1)} %copy-done.1, f32[8,512]{1,0:T(8,128)S(1)} %get-tuple-element.34.own.y_ref, f32[8,17,8,128]{3,2,1,0:T(8,128)S(1)} %all_to_all.16.parts, ...), custom_call_target="tpu_custom_call" | custom-call | bytes 1 | tf_op jit(solution)/shard_map/residuals/pallas_call | solution.py:26
  56.4 0.0 all-to-all-done.2.parts
  56.4 1.1 %reduce.1 = f32[24,24]{1,0:T(8,128)} custom-call(f32[24,24]{1,0:T(8,128)S(1)} %get-tuple-element.45.inverse, f32[24,24]{1,0:T(8,128)S(1)} %get-tuple-element.46.pencil, f32[32,8,128]{2,1,0:T(8,128)S(1)} %all-to-all-done.2.parts), custom_call_target="tpu_custom_call" | custom-call | bytes 1 | tf_op jit(solution)/shard_map/reduce/pallas_call | solution.py:26
  (7 shorter events, 0.1 us)
Async XLA Ops:
  0.6 7.2 %copy-start.1 = (f32[8,512]{1,0:T(8,128)S(1)}, f32[8,512]{1,0:T(8,128)}, u32[]{:S(2)}) copy-start(f32[8,512]{1,0:T(8,128)} %x_ref.3) | copy-start | bytes 49156
  0.6 21.9 %copy-start = (f32[8,512]{1,0:T(8,128)S(1)}, f32[8,512]{1,0:T(8,128)}, u32[]{:S(2)}) copy-start(f32[8,512]{1,0:T(8,128)} %p_ref.5) | copy-start | bytes 49156
  0.7 4.8 %collective-permute-start.1 = (f32[8,512]{1,0:T(8,128)}, f32[8,512]{1,0:T(8,128)S(1)}, u32[]{:S(2)}, u32[]{:S(2)}) collective-permute-start(f32[8,512]{1,0:T(8,128)} %x_ref.3), channel_id=1, source_target_pairs={{0,1},{1,0},{2,3},{3,2},{4,5},{5,4},{6,7},{7,6},{8,9},{9,8},{10,11... | collective-permute-start | bytes 49160 | tf_op jit(solution)/shard_map/ppermute | solution.py:501
  1.2 6.7 %collective-permute-start = (f32[8,512]{1,0:T(8,128)}, f32[8,512]{1,0:T(8,128)S(1)}, u32[]{:S(2)}, u32[]{:S(2)}) collective-permute-start(f32[8,512]{1,0:T(8,128)} %x_ref.3), channel_id=1, source_target_pairs={{0,16},{16,0},{1,17},{17,1},{2,18},{18,2},{3,19},{19,3},{4,20},{20... | collective-permute-start | bytes 49160 | tf_op jit(solution)/shard_map/ppermute | solution.py:501
  7.8 16.3 %copy-start.2 = (f32[512]{0:T(512)S(1)}, f32[512]{0:T(512)}, u32[]{:S(2)}) copy-start(f32[512]{0:T(512)} %param.12) | copy-start | bytes 6148
  7.9 19.6 %copy-start.3 = (f32[8,512]{1,0:T(8,128)S(1)}, f32[8,512]{1,0:T(8,128)}, u32[]{:S(2)}) copy-start(f32[8,512]{1,0:T(8,128)} %q_ref.1) | copy-start | bytes 49156
  22.5 4.9 %collective-permute-start.4 = (f32[9,8,128]{2,1,0:T(8,128)S(1)}, f32[9,8,128]{2,1,0:T(8,128)S(1)}, u32[]{:S(2)}, u32[]{:S(2)}) collective-permute-start(f32[9,8,128]{2,1,0:T(8,128)S(1)} %partner_sums.2), channel_id=1, source_target_pairs={{0,16},{16,0},{1,17},{17,1},{2,18},{18,2},{3,19},{19,3},{4,20},{20... | collective-permute-start | bytes 110600 | tf_op jit(solution)/shard_map/ppermute | solution.py:501
  24.2 1.4 %collective-permute-start.3 = (f32[8,1024]{1,0:T(8,128)S(1)}, f32[8,1024]{1,0:T(8,128)S(1)}, u32[]{:S(2)}, u32[]{:S(2)}) collective-permute-start(f32[8,1024]{1,0:T(8,128)S(1)} %get-tuple-element.31.rows), channel_id=1, source_target_pairs={{0,1},{1,0},{2,3},{3,2},{4,5},{5,4},{6,7},{7,6},{8,9},{9,8},{10,11... | collective-permute-start | bytes 98312 | tf_op jit(solution)/shard_map/ppermute | solution.py:501
  24.3 1.3 %collective-permute-start.2 = (f32[8,512]{1,0:T(8,128)S(1)}, f32[8,512]{1,0:T(8,128)S(1)}, u32[]{:S(2)}, u32[]{:S(2)}) collective-permute-start(f32[8,512]{1,0:T(8,128)S(1)} %get-tuple-element.30.mine), channel_id=1, source_target_pairs={{0,1},{1,0},{2,3},{3,2},{4,5},{5,4},{6,7},{7,6},{8,9},{9,8},{10,11... | collective-permute-start | bytes 49160 | tf_op jit(solution)/shard_map/ppermute | solution.py:501
  27.7 4.7 %collective-permute-start.5 = (f32[5,8,128]{2,1,0:T(8,128)S(1)}, f32[5,8,128]{2,1,0:T(8,128)S(1)}, u32[]{:S(2)}, u32[]{:S(2)}) collective-permute-start(f32[5,8,128]{2,1,0:T(8,128)S(1)} %get-tuple-element.33.own), channel_id=1, source_target_pairs={{0,16},{16,0},{1,17},{17,1},{2,18},{18,2},{3,19},{19,3},{4,20},{20... | collective-permute-start | bytes 61448 | tf_op jit(solution)/shard_map/ppermute | solution.py:501
  28.4 1.2 %collective-permute-start.6 = (f32[4,8,128]{2,1,0:T(8,128)S(1)}, f32[4,8,128]{2,1,0:T(8,128)S(1)}, u32[]{:S(2)}, u32[]{:S(2)}) collective-permute-start(f32[4,8,128]{2,1,0:T(8,128)S(1)} %slice.4), channel_id=1, source_target_pairs={{0,1},{1,0},{2,3},{3,2},{4,5},{5,4},{6,7},{7,6},{8,9},{9,8},{10,11... | collective-permute-start | bytes 49160 | tf_op jit(solution)/shard_map/ppermute | solution.py:501
  45.1 11.3 %all-to-all-start.2 = ((f32[32,8,128]{2,1,0:T(8,128)}), f32[32,8,128]{2,1,0:T(8,128)S(1)}, u32[]{:S(2)}, u32[]{:S(2)}) async-start(f32[32,8,128]{2,1,0:T(8,128)} %inner_products.1), calls=%async_computation.2 | async-start | bytes 262144 | tf_op jit(solution)/shard_map/all_to_all | solution.py:617
  47.6 8.0 %collective-permute-start.8 = (f32[4,8,128]{2,1,0:T(8,128)S(1)}, f32[4,8,128]{2,1,0:T(8,128)S(1)}, u32[]{:S(2)}, u32[]{:S(2)}) collective-permute-start(f32[4,8,128]{2,1,0:T(8,128)S(1)} %get-tuple-element.39.for_partner), channel_id=1, source_target_pairs={{0,16},{16,0},{1,17},{17,1},{2,18},{18,2},{3,19},{19,3},{4,20},{20... | collective-permute-start | bytes 49160 | tf_op jit(solution)/shard_map/ppermute | solution.py:501
  52.6 3.1 %collective-permute-start.9 = (f32[4,8,128]{2,1,0:T(8,128)S(1)}, f32[4,8,128]{2,1,0:T(8,128)S(1)}, u32[]{:S(2)}, u32[]{:S(2)}) collective-permute-start(f32[4,8,128]{2,1,0:T(8,128)S(1)} %get-tuple-element.41), channel_id=1, source_target_pairs={{0,1},{1,0},{2,3},{3,2},{4,5},{5,4},{6,7},{7,6},{8,9},{9,8},{10,11... | collective-permute-start | bytes 49160 | tf_op jit(solution)/shard_map/ppermute | solution.py:501
  53.1 1.2 %collective-permute-start.7 = (f32[8,128]{1,0:T(8,128)S(1)}, f32[8,128]{1,0:T(8,128)S(1)}, u32[]{:S(2)}, u32[]{:S(2)}) collective-permute-start(f32[8,128]{1,0:T(8,128)S(1)} %get-tuple-element.37.mine), channel_id=1, source_target_pairs={{0,1},{1,0},{2,3},{3,2},{4,5},{5,4},{6,7},{7,6},{8,9},{9,8},{10,11... | collective-permute-start | bytes 12296 | tf_op jit(solution)/shard_map/ppermute | solution.py:501

commit v4 on v3

--- a/solution.py
+++ b/solution.py
@@ -51,7 +51,8 @@
 
 
 def stacked_halves(values):
-    return jnp.concatenate(halves(values), axis=0)
+    high = values.astype(bf16).astype(f32)
+    return jnp.concatenate([high, values - high], axis=0).astype(bf16)
 
 
 def times_transpose(left, right, precision=None):
@@ -83,18 +84,20 @@
 
 
 class Places:
-    def __init__(self, refs, slots, row_tiles, column_tiles, paired):
+    def __init__(self, refs, row_tiles, column_tiles, tiles, paired):
         counts, self.rows, self.columns = refs
         self.live = counts[0, 0]
-        self.row_tiles, self.column_tiles = row_tiles, column_tiles
-        self.row_shift = lax.axis_index("col") * (row_tiles // 2) if paired else 0
-        self.column_shift = lax.axis_index("half") * (column_tiles // 2)
+        here = lax.axis_index("col")
+        self.row_mask = here * tiles if paired else 0
+        self.column_mask = lax.axis_index("half") * (column_tiles // 2) + lax.rem(here, 2) * (
+            column_tiles // 4
+        )
 
     def row(self, slot):
-        return lax.rem(self.rows[0, 0, slot] + self.row_shift, self.row_tiles)
+        return lax.bitwise_xor(self.rows[0, 0, slot], self.row_mask)
 
     def column(self, slot):
-        return lax.rem(self.columns[0, 0, slot] + self.column_shift, self.column_tiles)
+        return lax.bitwise_xor(self.columns[0, 0, slot], self.column_mask)
 
     def weight(self, slot):
         return jnp.where(slot < self.live, 1.0, 0.0).astype(f32)
@@ -107,8 +110,9 @@
 class Stream:
     def __init__(self, blocks, staged, semaphores):
         self.blocks, self.staged, self.semaphores = blocks, staged, semaphores
-        self.group = group_of(blocks.shape[0])
-        for index in range(blocks.shape[0] // self.group):
+        self.group = group_of(staged.shape[0])
+        self.groups = staged.shape[0] // self.group
+        for index in range(self.groups):
             self.copy(index).start()
 
     def copy(self, index):
@@ -127,9 +131,9 @@
             self.copy(index).wait()
             return 0
 
-        groups = (live + self.group - 1) // self.group
+        groups = jnp.minimum((live + self.group - 1) // self.group, self.groups)
         lax.fori_loop(0, groups, step, 0)
-        lax.fori_loop(groups, self.blocks.shape[0] // self.group, leave, 0)
+        lax.fori_loop(groups, self.groups, leave, 0)
 
 
 def stream_scratch(slots, side):
@@ -166,14 +170,14 @@
     return lambda slot: jnp.concatenate(halves(staged[slot]), axis=1)
 
 
-def loop_held(places, held, visit):
-    group = group_of(held.shape[0])
+def loop_held(places, held, visit, first=0):
+    group = math.gcd(held.shape[0], 32)
 
     def step(index, _):
-        visit([index * group + s for s in range(group)])
+        visit([first + index * group + s for s in range(group)])
         return 0
 
-    lax.fori_loop(0, (places.live + group - 1) // group, step, 0)
+    lax.fori_loop(0, (jnp.maximum(places.live - first, 0) + group - 1) // group, step, 0)
 
 
 def transposed_current_kernel(
@@ -193,7 +197,7 @@
     for copy in copies:
         copy.wait()
     refs = counts, rows_held, columns_held
-    places = Places(refs, blocks.shape[0], row_halves.shape[0], column_sum.shape[0], paired)
+    places = Places(refs, row_halves.shape[0], column_sum.shape[0], own.shape[-1] // LANES, paired)
     tiles = own.shape[-1] // LANES
     for t in range(tiles):
         for c, values in row_block_tiles(t, own, other, paired):
@@ -219,13 +223,29 @@
             payload[n, 3 * tiles + t] = column_sum[(near + n) * tiles + t]
 
 
-def assemble_image_kernel(own, partner, column_sum, payload):
-    tiles = own.shape[0] - 1
+def assemble_image_kernel(
+    own, base_partner, sums, received, column_sum, x_ref, x_partner, p_ref, payload, partner_image
+):
+    tiles = own.shape[-1] // LANES
     near = payload.shape[0]
-    gram = own[tiles] + partner[tiles]
+    partner = [base_partner[t] + sums[t] for t in range(tiles)]
+    basis = jnp.concatenate(
+        [
+            jnp.concatenate([x_ref[...], x_partner[...]], axis=1),
+            jnp.concatenate([own[...]] + partner, axis=1),
+            jnp.concatenate([p_ref[...]] + [received[tiles + t] for t in range(tiles)], axis=1),
+        ],
+        axis=0,
+    )
+    for t in range(tiles):
+        partner_image[:, lanes(t)] = partner[t]
+    outer = times_transpose(basis, basis, highest)
+    gram = jnp.concatenate(
+        [outer[0:8], outer[8:16, 8:24], outer[16:24, 16:24], jnp.zeros((8, LANES - 48), f32)], axis=1
+    )
     for n in range(near):
         for t in range(tiles):
-            payload[n, t] = own[t]
+            payload[n, t] = own[:, lanes(t)]
             payload[n, tiles + t] = partner[t]
             payload[n, 2 * tiles + t] = column_sum[n * tiles + t, 0:8]
             payload[n, 3 * tiles + t] = column_sum[(near + n) * tiles + t, 0:8]
@@ -238,8 +258,7 @@
     for t in range(tiles):
         sums[t] = balanced_sum([parts[n, 3 * tiles + t] for n in range(near)])
         sums[tiles + t] = previous[:, lanes(t)]
-    for t in range(2 * tiles, sums.shape[0]):
-        sums[t] = jnp.zeros_like(sums[t])
+    sums[2 * tiles] = jnp.zeros_like(sums[2 * tiles])
 
 
 def partner_sums_kernel(parts, sums, gram):
@@ -261,7 +280,7 @@
 
 def direct_held_kernel(paired, counts, rows, columns, held, parts, row_sum, column_halves):
     refs = counts, rows, columns
-    places = Places(refs, held.shape[0], row_sum.shape[0], column_halves.shape[0], paired)
+    places = Places(refs, row_sum.shape[0], column_halves.shape[0], parts.shape[1] // 4, paired)
     fill_column_set(column_halves, parts)
     row_sum[...] = jnp.zeros_like(row_sum)
     loop_held(
@@ -272,17 +291,28 @@
 
 
 def direct_kernel(
-    paired, counts, rows, columns, blocks, parts,
-    row_sum, rest,
+    paired, counts, rows, columns, blocks, parts, kept, mine, theirs,
+    row_sum, rest, gram,
     staged, semaphores, column_halves,
 ):
     refs = counts, rows, columns
-    places = Places(refs, blocks.shape[0], row_sum.shape[0], column_halves.shape[0], paired)
+    places = Places(refs, row_sum.shape[0], column_halves.shape[0], parts.shape[1] // 4, paired)
     stream = Stream(blocks, staged, semaphores)
+    gram[...] = mine[...] + theirs[...]
     fill_column_set(column_halves, parts)
     row_sum[...] = jnp.zeros_like(row_sum)
+    first = staged.shape[0]
+    loop_held(
+        places,
+        kept,
+        lambda slots: visit_direct(
+            slots, places, lambda slot: kept[slot - first], column_halves, row_sum
+        ),
+        first,
+    )
     stream.loop(
-        places.live, lambda slots: visit_direct(slots, places, tile_from(staged), column_halves, row_sum)
+        places.live,
+        lambda slots: visit_direct(slots, places, tile_from(staged), column_halves, row_sum),
     )
     for t in range(rest.shape[0]):
         rest[t] = row_sum[row_sum.shape[0] - rest.shape[0] + t]
@@ -296,61 +326,45 @@
     )
 
 
-def combine_kernel(paired, parts, row_sum, diagonal, vectors, previous, mine, rows):
+def combine_kernel(paired, parts, row_sum, diagonal, vectors, mine, *rows):
     tiles = parts.shape[1] // 4
     for t in range(tiles):
         total = half_result(t, parts, diagonal, vectors)
         if paired:
-            mine[:, lanes(t)] = total + row_sum[t]
-            rows[:, lanes(t)] = row_sum[tiles + t]
-            rows[:, lanes(tiles + t)] = previous[:, lanes(t)]
+            mine[t] = total + row_sum[t]
+            mine[tiles + t] = row_sum[tiles + t]
         else:
             mine[:, lanes(t)] = total
-            for c in range(rows.shape[0]):
-                rows[c, :, lanes(t)] = row_sum[c * tiles + t]
-
-
-def base_kernel(mine, rows, their_mine, their_rows, own, other):
-    width = own.shape[-1]
-    own[...] = mine[...] + their_rows[:, :width]
-    other[...] = their_mine[...] + rows[:, :width]
-
-
-def image_kernel(base, received, x_ref, p_ref, q_ref, image, ship):
-    tiles = image.shape[-1] // LANES
-    y = base[...] + jnp.concatenate([received[t] for t in range(tiles)], axis=1)
-    image[...] = y
-    x, p, q = x_ref[...], p_ref[...], q_ref[...]
-    outer = times_transpose(
-        jnp.concatenate([x, y, p], axis=0), jnp.concatenate([x, y, p, q], axis=0), highest
-    )
+            for c in range(rows[0].shape[0]):
+                rows[0][c, :, lanes(t)] = row_sum[c * tiles + t]
+
+
+def base_kernel(mine, theirs, own, other):
+    tiles = own.shape[0] - 1
     for t in range(tiles):
-        ship[t] = y[:, lanes(t)]
-    ship[tiles] = jnp.concatenate(
-        [
-            outer[0:8, 0:24],
-            outer[0:8, 24:32] + outer[8:16, 16:24],
-            outer[8:16, 8:32],
-            outer[16:24, 16:32],
-            jnp.zeros((8, LANES - 72), f32),
-        ],
-        axis=1,
-    )
+        own[t] = mine[t] + theirs[tiles + t]
+        other[:, lanes(t)] = theirs[t] + mine[tiles + t]
+    own[tiles] = jnp.zeros_like(own[tiles])
+
+
+def image_kernel(base, received, image):
+    for t in range(image.shape[-1] // LANES):
+        image[:, lanes(t)] = base[t] + received[t]
 
 
 def transposed_image_kernel(
-    paired, counts, rows, columns, held, own, base_other, sums_other, p_ref, p_other,
-    column_sum, sum_halves,
+    paired, counts, rows, columns, held, own, base_other, sums_other, p_ref, p_other, diagonal,
+    x_ref, q_ref,
+    column_sum, sum_halves, late, kept,
     row_halves,
 ):
     refs = counts, rows, columns
-    places = Places(refs, held.shape[0], row_halves.shape[0], column_sum.shape[0], paired)
+    places = Places(refs, row_halves.shape[0], column_sum.shape[0], own.shape[-1] // LANES, paired)
     width = own.shape[-1]
     tiles = width // LANES
     other = base_other
     if paired:
         other = base_other[...] + jnp.concatenate([sums_other[t] for t in range(tiles)], axis=1)
-        p_other = p_other[:, width:]
     for t in range(tiles):
         for (c, values), (_, previous) in zip(
             row_block_tiles(t, own, other, paired), row_block_tiles(t, p_ref, p_other, paired)
@@ -365,39 +379,89 @@
         ),
     )
     for j in range(column_sum.shape[0]):
-        sum_halves[j] = stacked_halves(column_sum[j])
-
-
-def inner_kernel(parts, sum_halves, diagonal, y_ref, p_ref, for_partner, first_received, spread):
+        sum_halves[j] = stacked_halves(column_sum[j, 8:16])
+
+    def keep(index, _):
+        part = pl.ds(index * 8, 8)
+        kept[part] = held[pl.ds(kept.shape[0] + index * 8, 8)]
+        return 0
+
+    lax.fori_loop(0, kept.shape[0] // 8, keep, 0)
+    y, p, q = own[...], p_ref[...], q_ref[...]
+    rows = jnp.concatenate([x_ref[...], y, p], axis=0)
+    terms = times_transpose(
+        rows, jnp.concatenate([0.5 * q, 0.5 * diagonal[...] * y], axis=0), highest
+    )
+    image_previous = times_transpose(0.5 * diagonal[...] * y, p, highest)
+    nothing = jnp.zeros((8, 16), f32)
+    late[...] = jnp.concatenate(
+        [
+            nothing,
+            terms[0:8, 0:8],
+            nothing[:, 0:8],
+            terms[8:16, 8:16],
+            terms[8:16, 0:8] + image_previous,
+            nothing,
+            terms[16:24, 0:8],
+            jnp.zeros((8, LANES - 72), f32),
+        ],
+        axis=1,
+    )
+
+
+def three_products(left, right):
+    rows, columns = left.shape[0] // 2, right.shape[0] // 2
+    cross = times_transpose(left, right)
+    return cross[:rows, :columns] + cross[rows:, :columns] + cross[:rows, columns:]
+
+
+def inner_kernel(
+    parts, sum_halves, late, y_ref, y_partner, p_ref, for_partner, first_received, spread
+):
     near = parts.shape[0]
-    tiles = y_ref.shape[-1] // LANES
+    tiles = parts.shape[1] // 4
     column_set = [
         stacked_halves(parts[n, first + t])
         for first in (0, tiles)
         for n in range(near)
         for t in range(tiles)
     ]
-    cross = times_transpose(
+    gathered = three_products(
         jnp.concatenate(column_set, axis=1),
         jnp.concatenate([sum_halves[j] for j in range(sum_halves.shape[0])], axis=1),
     )
-    stored = cross[0:8, 0:16] + cross[8:16, 0:16] + cross[0:8, 16:32]
-    scaled = diagonal[...] * y_ref[...]
-    halved = jnp.concatenate([half_result(t, parts, diagonal, y_ref) for t in range(tiles)], axis=1)
-    yz = times_transpose(scaled, 0.5 * y_ref[...], highest)
-    zp = times_transpose(
-        jnp.concatenate([halved] + [for_partner[t] for t in range(tiles)], axis=1),
-        jnp.concatenate([p_ref[...]] + [first_received[tiles + t] for t in range(tiles)], axis=1),
-        highest,
-    )
-    total = stored + jnp.concatenate([yz, zp], axis=1)
-    total = jnp.concatenate([total, jnp.zeros((8, LANES - 16), f32)], axis=1)
+    own = [balanced_sum([parts[n, 2 * tiles + t] for n in range(near)]) for t in range(tiles)]
+    pair = three_products(
+        stacked_halves(jnp.concatenate(own + [for_partner[t] for t in range(tiles)], axis=1)),
+        stacked_halves(
+            jnp.concatenate(
+                [
+                    jnp.concatenate([y_ref[...], y_partner[...]], axis=1),
+                    0.5
+                    * jnp.concatenate(
+                        [p_ref[...]] + [first_received[tiles + t] for t in range(tiles)], axis=1
+                    ),
+                ],
+                axis=0,
+            )
+        ),
+    )
+    total = late[...] + jnp.concatenate(
+        [
+            jnp.zeros((8, 32), f32),
+            pair[:, 0:8],
+            pair[:, 8:16] + 0.5 * gathered,
+            jnp.zeros((8, LANES - 48), f32),
+        ],
+        axis=1,
+    )
     for n in range(spread.shape[0]):
         spread[n] = total
 
 
-def eliminate_kernel(mine, theirs, ritz, inverse, pencil):
-    gram = mine[...] + theirs[...]
+def eliminate_kernel(gram, x_ref, y_ref, ritz, inverse, pencil, image, residual):
+    image[...] = y_ref[...]
+    gram = gram[...]
     turned = gram.T
 
     def block(n):
@@ -406,7 +470,7 @@
     def flipped(n):
         return turned[8 * n : 8 * n + 8, :]
 
-    xx, xy, xp, mixed, yy, yp, yq, pp, pq = range(9)
+    xx, xy, xp, yy, yp, pp = range(6)
     nothing = jnp.zeros((8, 8), f32)
     unit = (
         lax.broadcasted_iota(jnp.int32, (24, 24), 0) == lax.broadcasted_iota(jnp.int32, (24, 24), 1)
@@ -422,16 +486,21 @@
     work = jnp.concatenate([work, unit, jnp.zeros((24, LANES - 48), f32)], axis=1)
     pencil[...] = 0.5 * jnp.concatenate(
         [
-            jnp.concatenate([block(xy) + flipped(xy), 2.0 * block(yy), block(mixed)], axis=1),
-            jnp.concatenate([2.0 * block(yy), nothing, block(yq)], axis=1),
-            jnp.concatenate([flipped(mixed), flipped(yq), block(pq) + flipped(pq)], axis=1),
+            jnp.concatenate([block(xy) + flipped(xy), 2.0 * block(yy), block(yp)], axis=1),
+            jnp.concatenate([2.0 * block(yy), nothing, nothing], axis=1),
+            jnp.concatenate([flipped(yp), nothing, nothing], axis=1),
         ],
         axis=0,
     )
     row_ids = lax.broadcasted_iota(jnp.int32, (24, 1), 0)
     for k in range(0, 24, 2):
         if k == 8:
-            ritz[...] = work[8:16, 24:32]
+            factors = work[8:16, 24:32]
+            ritz[...] = factors
+            r = y_ref[...]
+            for j in range(8):
+                r = r + factors[:, j : j + 1] * x_ref[j : j + 1, :]
+            residual[...] = r
         row, next_row = work[k : k + 1, :], work[k + 1 : k + 2, :]
         column = jnp.broadcast_to(work[:, k : k + 1], work.shape)
         next_column = jnp.broadcast_to(work[:, k + 1 : k + 2], work.shape)
@@ -448,41 +517,22 @@
     inverse[...] = work[:, 24:48] * lax.rsqrt(jnp.sum(work[:, 0:24] * unit, axis=1, keepdims=True))
 
 
-def residual_kernel(
-    paired, ritz, x_ref, y_ref, parts, received, row_sum, theirs, diagonal,
-    image, residual, residual_image,
+def finish_kernel(
+    paired, inverse, pencil, inner_parts, ritz, y_ref, parts, received, row_sum, theirs, diagonal,
+    residual_image, reduced,
 ):
-    image[...] = y_ref[...]
+    total = balanced_sum([inner_parts[n] for n in range(inner_parts.shape[0])])
+    late = jnp.concatenate([total[:, 0:24], total[:, 24:48], total[:, 48:72]], axis=0)
+    lower = inverse[...]
+    left = times(lower, pencil[...] + late, highest) + times_transpose(lower, late, highest)
+    reduced[...] = times_transpose(left, lower, highest)
     for t in range(theirs.shape[0]):
-        r = y_ref[:, lanes(t)]
         s = half_result(t, parts, diagonal, y_ref) + received[t] + theirs[t]
         if paired:
             s = s + row_sum[t]
         for j in range(8):
-            factor = ritz[:, j : j + 1]
-            r = r + factor * x_ref[j : j + 1, lanes(t)]
-            s = s + factor * y_ref[j : j + 1, lanes(t)]
-        residual[:, lanes(t)] = r
+            s = s + ritz[:, j : j + 1] * y_ref[j : j + 1, lanes(t)]
         residual_image[:, lanes(t)] = s
-
-
-def reduce_kernel(inverse, pencil, parts, reduced):
-    total = balanced_sum([parts[n] for n in range(parts.shape[0])])
-    turned = total.T
-    yz = total[:, 0:8] + turned[0:8, :]
-    zp = 0.5 * total[:, 8:16]
-    pz = 0.5 * turned[8:16, :]
-    nothing = jnp.zeros((8, 8), f32)
-    full = pencil[...] + jnp.concatenate(
-        [
-            jnp.zeros((8, 24), f32),
-            jnp.concatenate([nothing, yz, zp], axis=1),
-            jnp.concatenate([nothing, pz, nothing], axis=1),
-        ],
-        axis=0,
-    )
-    lower = inverse[...]
-    reduced[...] = times_transpose(times(lower, full, highest), lower, highest)
 
 
 def local(tile_values, tile_row, tile_col, counts, diagonal, current, previous, previous_image, *, sizes):
@@ -503,8 +553,15 @@
     def to_partner(values):
         return swap(values, "half")
 
+    devices = ("half", "near", "col")
+
     def to_near(values):
-        return lax.all_to_all(values, "near", 0, 0, tiled=True)
+        groups = [
+            [(h * near + (p + c % 2 * (near // 2)) % near) * n_col + c for p in range(near)]
+            for h in range(2)
+            for c in range(n_col)
+        ]
+        return lax.all_to_all(values, devices, 0, 0, tiled=True, axis_index_groups=groups)
 
     def from_columns(values):
         return swap(values) if paired else lax.all_gather(values, "col", axis=0)
@@ -549,52 +606,59 @@
         [pltpu.VMEM((column_tiles, 16, side), bf16)],
         micros=2.2,
     )
-    mine, rows = call(
+    combine = functools.partial(
+        call,
         functools.partial(combine_kernel, paired),
         "combine",
-        [shape(8, width), shape(8, 2 * width) if paired else shape(n_col, 8, width)],
-        [parts, row_sum, diagonal, current, previous],
-        [in_vmem] * 5,
+        operands=[parts, row_sum, diagonal, current],
+        specs=[in_vmem] * 4,
     )
     if paired:
-        previous_other = swap(rows)
+        previous_other = swap(previous)
+        mine = combine(out_shape=shape(2 * tiles, 8, side))
         base, base_other = call(
             base_kernel,
             "base",
-            [shape(8, width)] * 2,
-            [mine, rows, swap(mine), previous_other],
-            [in_vmem] * 4,
+            [shape(tiles + 1, 8, side), shape(8, width)],
+            [mine, swap(mine)],
+            [in_vmem] * 2,
         )
         sums_other = swap(first_received[:tiles])
     else:
+        mine, rows = combine(out_shape=[shape(8, width), shape(n_col, 8, width)])
         base = mine + jnp.sum(lax.all_to_all(rows, "col", 0, 0, tiled=True), axis=0)
+        base = base.reshape(8, tiles, side).transpose(1, 0, 2)
         sums_other = first_received
         previous_other = lax.all_gather(previous, "col", axis=0)
-    image, ship = call(
-        image_kernel,
-        "image",
-        [shape(8, width), shape(tiles + 1, 8, side)],
-        [base, first_received, current, previous, previous_image],
-        [in_vmem] * 5,
-    )
-    partner_ship = to_partner(ship)
+    base_partner = to_partner(base)
+    image = call(image_kernel, "image", shape(8, width), [base, first_received], [in_vmem] * 2)
     if not paired:
         base_other = lax.all_gather(image, "col", axis=0)
-    column_sum, sum_halves = call(
+    column_sum, sum_halves, late, kept = call(
         functools.partial(transposed_image_kernel, paired),
         "transposed_image",
-        [shape(column_tiles, 16, side), shape(column_tiles, 32, side, dtype=bf16)],
-        [*places, held, image, base_other, sums_other, previous, previous_other],
-        [in_smem] * 3 + [in_vmem] * 6,
+        [
+            shape(column_tiles, 16, side),
+            shape(column_tiles, 16, side, dtype=bf16),
+            shape(8, LANES),
+            shape(slots // 2, side, 2 * side, dtype=bf16),
+        ],
+        [
+            *places, held, image, base_other, sums_other, previous, previous_other, diagonal,
+            current, previous_image,
+        ],
+        [in_smem] * 3 + [in_vmem] * 9,
         [pltpu.VMEM((row_tiles, 32, side), bf16)],
         micros=1.8,
     )
-    payload = call(
+    payload, partner_image = call(
         assemble_image_kernel,
         "assemble_image",
-        shape(near, 4 * tiles + 1, 8, side),
-        [ship, partner_ship, column_sum],
-        [in_vmem] * 3,
+        [shape(near, 4 * tiles + 1, 8, side), shape(8, width)],
+        [
+            image, base_partner, sums, first_received, column_sum, current, partner, previous,
+        ],
+        [in_vmem] * 8,
     )
     parts = to_near(payload)
     for_partner, gram = call(
@@ -604,24 +668,31 @@
         [parts],
         [in_vmem],
     )
-    received = to_partner(for_partner)
     their_gram = swap(gram) if paired else lax.psum(gram, "col") - gram
     spread = call(
         inner_kernel,
         "inner_products",
         shape(2 * near * n_col, 8, LANES),
-        [parts, sum_halves, diagonal, image, previous, for_partner, first_received],
-        [in_vmem] * 7,
+        [
+            parts, sum_halves, late, image, partner_image, previous, for_partner, first_received,
+        ],
+        [in_vmem] * 8,
         micros=1.1,
     )
-    inner_parts = lax.all_to_all(spread, ("half", "near", "col"), 0, 0, tiled=True)
-    row_sum, rest = call(
+    everyone = [list(range(2 * near * n_col))[::-1]]
+    inner_parts = lax.all_to_all(spread, devices, 0, 0, tiled=True, axis_index_groups=everyone)
+    received = to_partner(for_partner)
+    row_sum, rest, gram = call(
         functools.partial(direct_kernel, paired),
         "direct_image",
-        [shape(row_tiles, 8, side), shape(tiles if paired else row_tiles, 8, side)],
-        [*places, blocks, parts],
-        [in_smem] * 3 + [in_hbm, in_vmem],
-        stream_scratch(slots, side) + [pltpu.VMEM((column_tiles, 16, side), bf16)],
+        [
+            shape(row_tiles, 8, side),
+            shape(tiles if paired else row_tiles, 8, side),
+            shape(8, LANES),
+        ],
+        [*places, blocks, parts, kept, gram, their_gram],
+        [in_smem] * 3 + [in_hbm] + [in_vmem] * 4,
+        stream_scratch(slots // 2, side) + [pltpu.VMEM((column_tiles, 16, side), bf16)],
         micros=3.4,
     )
     if paired:
@@ -629,31 +700,25 @@
     else:
         rest = rest.reshape(n_col, tiles, 8, side)
         theirs = jnp.sum(lax.all_to_all(rest, "col", 0, 0, tiled=True), axis=0)
-    ritz, inverse, pencil = call(
+    ritz, inverse, pencil, image_out, residual = call(
         eliminate_kernel,
         "eliminate",
-        [shape(8, 8), shape(24, 24), shape(24, 24)],
-        [gram, their_gram],
-        [in_vmem] * 2,
-        micros=2.1,
-    )
-    image, residual, residual_image = call(
-        functools.partial(residual_kernel, paired),
-        "residuals",
-        [shape(8, width)] * 3,
-        [ritz, current, image, parts, received, row_sum, theirs, diagonal],
-        [in_vmem] * 8,
-        micros=0.7,
-    )
-    reduced = call(
-        reduce_kernel,
-        "reduce",
-        shape(24, 24),
-        [inverse, pencil, inner_parts],
+        [shape(8, 8), shape(24, 24), shape(24, 24), shape(8, width), shape(8, width)],
+        [gram, current, image],
         [in_vmem] * 3,
+        micros=1.3,
+    )
+    residual_image, reduced = call(
+        functools.partial(finish_kernel, paired),
+        "finish",
+        [shape(8, width), shape(24, 24)],
+        [
+            inverse, pencil, inner_parts, ritz, image, parts, received, row_sum, theirs, diagonal,
+        ],
+        [in_vmem] * 10,
         micros=1.0,
     )
-    return (image, residual, residual_image, reduced)
+    return (image_out, residual, residual_image, reduced)
 
 
 def solution(mesh):

time: 57.5 us -> 55.6 us (0.967)
  waiting for transfers between devices: 7.09 us -> 3.49 us
  starting transfers between devices: 12.2 us -> 13.3 us
    ppermute x10, waiting for transfers between devices: 7.09 us -> 2.83 us  [swap(): return lax.ppermute(values, axis, [(0, 1), (1, 0)])]
    ppermute x10, starting transfers between devices: 9.62 us -> 10.8 us  [swap(): return lax.ppermute(values, axis, [(0, 1), (1, 0)])]
    all_to_all x1, waiting for transfers between devices: 0.01 us -> 0.65 us  [local(): lax.all_to_all(spread, devices, 0, 0, tiled=True, axis_index_groups=every...]
    pallas_call x15 -> x14, Pallas kernels: 10.6 us -> 10.4 us  [call(): pl.pallas_call(kernel, out_shape=out_shape, in_specs=specs, out_specs=jax...]
  transfers between devices with their start and end apart: 11 -> 11, of which waited for: 5 -> 6; matrix products, arithmetic and copies ran while one was open for 0% -> 0% of each run, Pallas kernels for 14% -> 14%
where the time goes in v4:
time: 55.6 us; the launch traced here: 55.3 us
  blocking collectives  26.6 us (48%)
  starting transfers between devices  13.3 us (24%)
  Pallas kernels  10.4 us (19%)
  waiting for transfers between devices  3.49 us (6%)
  between operations  1.42 us (3%)
    all_to_all x2, blocking collectives, to_near(): lax.all_to_all(values, devices, 0, 0, tiled=True, axis_index_groups=groups)  26.6 us
    ppermute x10, starting transfers between devices, swap(): return lax.ppermute(values, axis, [(0, 1), (1, 0)])  10.8 us
    pallas_call x14, Pallas kernels, call(): pl.pallas_call(kernel, out_shape=out_shape, in_specs=specs, out_specs=jax...  10.4 us
    ppermute x10, waiting for transfers between devices, swap(): return lax.ppermute(values, axis, [(0, 1), (1, 0)])  2.83 us
    all_to_all x1, starting transfers between devices, local(): lax.all_to_all(spread, devices, 0, 0, tiled=True, axis_index_groups=every...  2.57 us
  transfers between devices with their start and end apart: 11, of which 6 were waited for; matrix products, arithmetic and copies ran while one was open for 0% of the time, Pallas kernels for 14%

profile of v4, /device:TPU:0, one launch (start us, length us, event | category | flops | bytes accessed | tf_op | source)
XLA Modules:
  0.0 55.3 jit_solution(4029264594486670154)
XLA Ops:
  0.6 0.0 copy-start
  0.6 0.0 copy-start.1
  0.7 0.5 collective-permute-start
  1.2 3.7 %collective-permute-start.1 = (f32[8,512]{1,0:T(8,128)}, f32[8,512]{1,0:T(8,128)S(1)}, u32[]{:S(2)}, u32[]{:S(2)}) collective-permute-start(f32[8,512]{1,0:T(8,128)} %x_ref.5), channel_id=1, source_target_pairs={{0,16},{16,0},{1,17},{17,1},{2,18},{18,2},{3,19},{19,3},{4,20},{20... | collective-permute-start | bytes 49160 | tf_op jit(solution)/shard_map/ppermute | solution.py:551
  5.5 0.0 collective-permute-done.refs_5_
  5.5 2.3 %transposed_current.1 = (s32[1,1,64]{2,1,0:T(1,128)S(4)}, s32[1,1,64]{2,1,0:T(1,128)S(4)}, f32[64,8,128]{2,1,0:T(8,128)S(1)}, bf16[64,128,256]{2,1,0:T(8,128)(2,1)S(1)}) custom-call(s32[1,1]{1,0:T(1,128)S(6)} %copy.12.refs_0_.counts, s32[1,1,64]{2,1,0:T(1,128)} %refs_1_.1, s32[1,1,64]{2,1,0:T(1,128)} %refs_2_.1, f32[64,128,128]{2,1,0:T(8,128)} %bitcast.5, ...), custom_call_target="tpu_custom_call" | custom-call | bytes 1 | tf_op jit(solution)/shard_map/transposed_current/pallas_call | solution.py:26
  7.8 0.0 copy-start.2
  7.9 0.0 copy-start.3
  7.9 0.0 collective-permute-done.1.partner.x_partner
  7.9 0.0 copy-done
  7.9 13.7 %all_to_all.15.parts = f32[8,16,8,128]{3,2,1,0:T(8,128)S(1)} all-to-all(f32[8,16,8,128]{3,2,1,0:T(8,128)S(1)} %assemble_current.1), channel_id=1, replica_groups={{0,2,4,6,8,10,12,14},{9,11,13,15,1,3,5,7},{16,18,20,22,24,26,28,30},{25..., dimensions={0} | all-to-all | bytes 1048576 | tf_op jit(solution)/shard_map/all_to_all | solution.py:564
  21.7 0.0 copy-done.1
  21.7 1.1 %collective-permute-start.3 = (f32[9,8,128]{2,1,0:T(8,128)S(1)}, f32[9,8,128]{2,1,0:T(8,128)S(1)}, u32[]{:S(2)}, u32[]{:S(2)}) collective-permute-start(f32[9,8,128]{2,1,0:T(8,128)S(1)} %partner_sums.2.sums), channel_id=1, source_target_pairs={{0,16},{16,0},{1,17},{17,1},{2,18},{18,2},{3,19},{19,3},{4,20},{20... | collective-permute-start | bytes 110600 | tf_op jit(solution)/shard_map/ppermute | solution.py:551
  22.7 0.7 %direct_current.1.row_sum = f32[8,8,128]{2,1,0:T(8,128)S(1)} custom-call(s32[1,1]{1,0:T(1,128)S(6)} %copy.12.refs_0_.counts, s32[1,1,64]{2,1,0:T(1,128)S(4)} %get-tuple-element.28.rows, s32[1,1,64]{2,1,0:T(1,128)S(4)} %get-tuple-element.29.columns, bf16[64,128,256]{2,1,0:T(8,128)(2,1)S(1)} %get-tuple-element.31.held, f32[8,16,8,128]{3,2,1,0:T(8,128)S(1)} %all_to_all.15.parts), custom_call_target="tpu_custom_call" | custom-call | bytes 1 | tf_op jit(solution)/shard_map/direct_current/pallas_call | solution.py:26
  23.4 0.0 copy-done.2
  23.5 0.1 collective-permute-start.2
  23.6 1.2 %collective-permute-done.2.theirs = f32[8,8,128]{2,1,0:T(8,128)S(1)} collective-permute-done((f32[8,8,128]{2,1,0:T(8,128)S(1)}, f32[8,8,128]{2,1,0:T(8,128)S(1)}, u32[]{:S(2)}, u32[]{:S(2)}) %collective-permute-start.2) | collective-permute-done | bytes 32800 | tf_op jit(solution)/shard_map/ppermute | solution.py:551
  24.8 1.9 %collective-permute-start.4 = (f32[5,8,128]{2,1,0:T(8,128)S(1)}, f32[5,8,128]{2,1,0:T(8,128)S(1)}, u32[]{:S(2)}, u32[]{:S(2)}) collective-permute-start(f32[5,8,128]{2,1,0:T(8,128)S(1)} %get-tuple-element.32.base), channel_id=1, source_target_pairs={{0,16},{16,0},{1,17},{17,1},{2,18},{18,2},{3,19},{19,3},{4,20},{20... | collective-permute-start | bytes 61448 | tf_op jit(solution)/shard_map/ppermute | solution.py:551
  26.7 0.0 collective-permute-start.6
  26.7 0.0 collective-permute-done.3.received.first_received
  26.7 0.5 collective-permute-start.5
  27.2 0.7 %collective-permute-done.6.p_other = f32[8,512]{1,0:T(8,128)S(1)} collective-permute-done((f32[8,512]{1,0:T(8,128)S(1)}, f32[8,512]{1,0:T(8,128)S(1)}, u32[]{:S(2)}, u32[]{:S(2)}) %collective-permute-start.6) | collective-permute-done | bytes 16416 | tf_op jit(solution)/shard_map/ppermute | solution.py:551
  27.9 0.2 collective-permute-done.5.sums_other
  28.1 0.0 copy-done.3
  28.1 0.9 %transposed_image.1 = (f32[64,16,128]{2,1,0:T(8,128)S(1)}, bf16[64,16,128]{2,1,0:T(8,128)(2,1)S(1)}, f32[8,128]{1,0:T(8,128)S(1)}, bf16[32,128,256]{2,1,0:T(8,128)(2,1)S(1)}) custom-call(s32[1,1]{1,0:T(1,128)S(6)} %copy.12.refs_0_.counts, s32[1,1,64]{2,1,0:T(1,128)S(4)} %get-tuple-element.28.rows, s32[1,1,64]{2,1,0:T(1,128)S(4)} %get-tuple-element.29.columns, ...), custom_call_target="tpu_custom_call" | custom-call | bytes 1 | tf_op jit(solution)/shard_map/transposed_image/pallas_call | solution.py:26
  29.0 0.5 collective-permute-done.4.base_partner
  29.4 0.3 assemble_image.1
  29.7 12.9 %all_to_all.16.parts = f32[8,17,8,128]{3,2,1,0:T(8,128)S(1)} all-to-all(f32[8,17,8,128]{3,2,1,0:T(8,128)S(1)} %get-tuple-element.35), channel_id=1, replica_groups={{0,2,4,6,8,10,12,14},{9,11,13,15,1,3,5,7},{16,18,20,22,24,26,28,30},{25..., dimensions={0} | all-to-all | bytes 1114112 | tf_op jit(solution)/shard_map/all_to_all | solution.py:564
  42.6 1.1 %inner_products.1 = f32[32,8,128]{2,1,0:T(8,128)} custom-call(f32[8,17,8,128]{3,2,1,0:T(8,128)S(1)} %all_to_all.16.parts, bf16[64,16,128]{2,1,0:T(8,128)(2,1)S(1)} %get-tuple-element.43.sum_halves, f32[8,128]{1,0:T(8,128)S(1)} %get-tuple-element.44.late, f32[8,512]{1,0:T(8,128)S(1)} %image.1.own.y_ref, f32[8,512]{1,0:T(8,128)S(1)} %get-tuple-element.45.y_partner, ...), custom_call_target="tpu_custom_call" | custom-call | bytes 1 | tf_op jit(solution)/shard_map/inner_products/pallas_call | solution.py:26
  43.7 2.6 %all-to-all-start.2 = ((f32[32,8,128]{2,1,0:T(8,128)}), f32[32,8,128]{2,1,0:T(8,128)S(1)}, u32[]{:S(2)}, u32[]{:S(2)}) async-start(f32[32,8,128]{2,1,0:T(8,128)} %inner_products.1), calls=%async_computation.2 | async-start | bytes 262144 | tf_op jit(solution)/shard_map/all_to_all | solution.py:683
  46.3 0.2 collective-permute-start.7
  46.5 2.7 %collective-permute-start.8 = (f32[4,8,128]{2,1,0:T(8,128)S(1)}, f32[4,8,128]{2,1,0:T(8,128)S(1)}, u32[]{:S(2)}, u32[]{:S(2)}) collective-permute-start(f32[4,8,128]{2,1,0:T(8,128)S(1)} %get-tuple-element.46.for_partner), channel_id=1, source_target_pairs={{0,16},{16,0},{1,17},{17,1},{2,18},{18,2},{3,19},{19,3},{4,20},{20... | collective-permute-start | bytes 49160 | tf_op jit(solution)/shard_map/ppermute | solution.py:551
  49.2 0.0 collective-permute-done.7.theirs
  49.2 2.0 %direct_image.1 = (f32[8,8,128]{2,1,0:T(8,128)S(1)}, f32[4,8,128]{2,1,0:T(8,128)S(1)}, f32[8,128]{1,0:T(8,128)S(1)}) custom-call(s32[1,1]{1,0:T(1,128)S(6)} %copy.12.refs_0_.counts, s32[1,1,64]{2,1,0:T(1,128)S(4)} %get-tuple-element.28.rows, s32[1,1,64]{2,1,0:T(1,128)S(4)} %get-tuple-element.29.columns, f32[64,128,128]{2,1,0:T(8,128)} %bitcast.6, ...), custom_call_target="tpu_custom_call" | custom-call | bytes 1 | tf_op jit(solution)/shard_map/direct_image/pallas_call | solution.py:26
  51.2 0.1 collective-permute-start.9
  51.4 1.9 %eliminate.1 = (f32[8,8]{1,0:T(8,128)S(1)}, f32[24,24]{1,0:T(8,128)S(1)}, f32[24,24]{1,0:T(8,128)S(1)}, f32[8,512]{1,0:T(8,128)}, f32[8,512]{1,0:T(8,128)}) custom-call(f32[8,128]{1,0:T(8,128)S(1)} %get-tuple-element.38.gram, f32[8,512]{1,0:T(8,128)S(1)} %copy-done, f32[8,512]{1,0:T(8,128)S(1)} %image.1.own.y_ref), custom_call_target="tpu_custom_call" | custom-call | bytes 1 | tf_op jit(solution)/shard_map/eliminate/pallas_call | solution.py:26
  53.2 0.3 collective-permute-done.8.received
  53.6 0.0 collective-permute-done.9.theirs
  53.6 0.7 %all-to-all-done.2.inner_parts = f32[32,8,128]{2,1,0:T(8,128)S(1)} async-done(((f32[32,8,128]{2,1,0:T(8,128)}), f32[32,8,128]{2,1,0:T(8,128)S(1)}, u32[]{:S(2)}, u32[]{:S(2)}) %all-to-all-start.2) | async-done | bytes 131104 | tf_op jit(solution)/shard_map/all_to_all | solution.py:683
  54.2 1.0 %finish.1 = (f32[8,512]{1,0:T(8,128)}, f32[24,24]{1,0:T(8,128)}) custom-call(f32[24,24]{1,0:T(8,128)S(1)} %get-tuple-element.41.inverse, f32[24,24]{1,0:T(8,128)S(1)} %get-tuple-element.42.pencil, f32[32,8,128]{2,1,0:T(8,128)S(1)} %all-to-all-done.2.inner_parts, f32[8,8]{1,0:T(8,128)S(1)} %get-tuple-element.47.ritz, f32[8,512]{1,0:T(8,128)S(1)} %image.1.own.y_ref, ...), custom_call_target="tpu_custom_call" | custom-call | bytes 1 | tf_op jit(solution)/shard_map/finish/pallas_call | solution.py:26
  (7 shorter events, 0.1 us)
Async XLA Ops:
  0.6 7.2 %copy-start = (f32[8,512]{1,0:T(8,128)S(1)}, f32[8,512]{1,0:T(8,128)}, u32[]{:S(2)}) copy-start(f32[8,512]{1,0:T(8,128)} %x_ref.5) | copy-start | bytes 49156
  0.6 21.0 %copy-start.1 = (f32[8,512]{1,0:T(8,128)S(1)}, f32[8,512]{1,0:T(8,128)}, u32[]{:S(2)}) copy-start(f32[8,512]{1,0:T(8,128)} %p_ref.5) | copy-start | bytes 49156
  0.7 4.8 %collective-permute-start = (f32[8,512]{1,0:T(8,128)}, f32[8,512]{1,0:T(8,128)S(1)}, u32[]{:S(2)}, u32[]{:S(2)}) collective-permute-start(f32[8,512]{1,0:T(8,128)} %x_ref.5), channel_id=1, source_target_pairs={{0,1},{1,0},{2,3},{3,2},{4,5},{5,4},{6,7},{7,6},{8,9},{9,8},{10,11... | collective-permute-start | bytes 49160 | tf_op jit(solution)/shard_map/ppermute | solution.py:551
  1.2 6.7 %collective-permute-start.1 = (f32[8,512]{1,0:T(8,128)}, f32[8,512]{1,0:T(8,128)S(1)}, u32[]{:S(2)}, u32[]{:S(2)}) collective-permute-start(f32[8,512]{1,0:T(8,128)} %x_ref.5), channel_id=1, source_target_pairs={{0,16},{16,0},{1,17},{17,1},{2,18},{18,2},{3,19},{19,3},{4,20},{20... | collective-permute-start | bytes 49160 | tf_op jit(solution)/shard_map/ppermute | solution.py:551
  7.8 15.6 %copy-start.2 = (f32[512]{0:T(512)S(1)}, f32[512]{0:T(512)}, u32[]{:S(2)}) copy-start(f32[512]{0:T(512)} %param.12) | copy-start | bytes 6148
  7.9 20.2 %copy-start.3 = (f32[8,512]{1,0:T(8,128)S(1)}, f32[8,512]{1,0:T(8,128)}, u32[]{:S(2)}) copy-start(f32[8,512]{1,0:T(8,128)} %q_ref.1) | copy-start | bytes 49156
  21.7 5.0 %collective-permute-start.3 = (f32[9,8,128]{2,1,0:T(8,128)S(1)}, f32[9,8,128]{2,1,0:T(8,128)S(1)}, u32[]{:S(2)}, u32[]{:S(2)}) collective-permute-start(f32[9,8,128]{2,1,0:T(8,128)S(1)} %partner_sums.2.sums), channel_id=1, source_target_pairs={{0,16},{16,0},{1,17},{17,1},{2,18},{18,2},{3,19},{19,3},{4,20},{20... | collective-permute-start | bytes 110600 | tf_op jit(solution)/shard_map/ppermute | solution.py:551
  23.5 1.3 %collective-permute-start.2 = (f32[8,8,128]{2,1,0:T(8,128)S(1)}, f32[8,8,128]{2,1,0:T(8,128)S(1)}, u32[]{:S(2)}, u32[]{:S(2)}) collective-permute-start(f32[8,8,128]{2,1,0:T(8,128)S(1)} %combine.1.mine), channel_id=1, source_target_pairs={{0,1},{1,0},{2,3},{3,2},{4,5},{5,4},{6,7},{7,6},{8,9},{9,8},{10,11... | collective-permute-start | bytes 98312 | tf_op jit(solution)/shard_map/ppermute | solution.py:551
  24.8 4.7 %collective-permute-start.4 = (f32[5,8,128]{2,1,0:T(8,128)S(1)}, f32[5,8,128]{2,1,0:T(8,128)S(1)}, u32[]{:S(2)}, u32[]{:S(2)}) collective-permute-start(f32[5,8,128]{2,1,0:T(8,128)S(1)} %get-tuple-element.32.base), channel_id=1, source_target_pairs={{0,16},{16,0},{1,17},{17,1},{2,18},{18,2},{3,19},{19,3},{4,20},{20... | collective-permute-start | bytes 61448 | tf_op jit(solution)/shard_map/ppermute | solution.py:551
  26.7 1.2 %collective-permute-start.6 = (f32[8,512]{1,0:T(8,128)S(1)}, f32[8,512]{1,0:T(8,128)S(1)}, u32[]{:S(2)}, u32[]{:S(2)}) collective-permute-start(f32[8,512]{1,0:T(8,128)S(1)} %copy-done.1), channel_id=1, source_target_pairs={{0,1},{1,0},{2,3},{3,2},{4,5},{5,4},{6,7},{7,6},{8,9},{9,8},{10,11... | collective-permute-start | bytes 49160 | tf_op jit(solution)/shard_map/ppermute | solution.py:551
  26.7 1.3 %collective-permute-start.5 = (f32[4,8,128]{2,1,0:T(8,128)S(1)}, f32[4,8,128]{2,1,0:T(8,128)S(1)}, u32[]{:S(2)}, u32[]{:S(2)}) collective-permute-start(f32[4,8,128]{2,1,0:T(8,128)S(1)} %slice.4), channel_id=1, source_target_pairs={{0,1},{1,0},{2,3},{3,2},{4,5},{5,4},{6,7},{7,6},{8,9},{9,8},{10,11... | collective-permute-start | bytes 49160 | tf_op jit(solution)/shard_map/ppermute | solution.py:551
  43.7 10.5 %all-to-all-start.2 = ((f32[32,8,128]{2,1,0:T(8,128)}), f32[32,8,128]{2,1,0:T(8,128)S(1)}, u32[]{:S(2)}, u32[]{:S(2)}) async-start(f32[32,8,128]{2,1,0:T(8,128)} %inner_products.1), calls=%async_computation.2 | async-start | bytes 262144 | tf_op jit(solution)/shard_map/all_to_all | solution.py:683
  46.3 2.9 %collective-permute-start.7 = (f32[8,128]{1,0:T(8,128)S(1)}, f32[8,128]{1,0:T(8,128)S(1)}, u32[]{:S(2)}, u32[]{:S(2)}) collective-permute-start(f32[8,128]{1,0:T(8,128)S(1)} %get-tuple-element.37.mine), channel_id=1, source_target_pairs={{0,1},{1,0},{2,3},{3,2},{4,5},{5,4},{6,7},{7,6},{8,9},{9,8},{10,11... | collective-permute-start | bytes 12296 | tf_op jit(solution)/shard_map/ppermute | solution.py:551
  46.5 7.1 %collective-permute-start.8 = (f32[4,8,128]{2,1,0:T(8,128)S(1)}, f32[4,8,128]{2,1,0:T(8,128)S(1)}, u32[]{:S(2)}, u32[]{:S(2)}) collective-permute-start(f32[4,8,128]{2,1,0:T(8,128)S(1)} %get-tuple-element.46.for_partner), channel_id=1, source_target_pairs={{0,16},{16,0},{1,17},{17,1},{2,18},{18,2},{3,19},{19,3},{4,20},{20... | collective-permute-start | bytes 49160 | tf_op jit(solution)/shard_map/ppermute | solution.py:551
  51.2 2.3 %collective-permute-start.9 = (f32[4,8,128]{2,1,0:T(8,128)S(1)}, f32[4,8,128]{2,1,0:T(8,128)S(1)}, u32[]{:S(2)}, u32[]{:S(2)}) collective-permute-start(f32[4,8,128]{2,1,0:T(8,128)S(1)} %get-tuple-element.49), channel_id=1, source_target_pairs={{0,1},{1,0},{2,3},{3,2},{4,5},{5,4},{6,7},{7,6},{8,9},{9,8},{10,11... | collective-permute-start | bytes 49160 | tf_op jit(solution)/shard_map/ppermute | solution.py:551

commit v5 on v4

--- a/solution.py
+++ b/solution.py
@@ -87,6 +87,8 @@
     def __init__(self, refs, row_tiles, column_tiles, tiles, paired):
         counts, self.rows, self.columns = refs
         self.live = counts[0, 0]
+        loop_step = step_of(self.rows.shape[-1])
+        self.reach = (self.live + loop_step - 1) // loop_step * loop_step
         here = lax.axis_index("col")
         self.row_mask = here * tiles if paired else 0
         self.column_mask = lax.axis_index("half") * (column_tiles // 2) + lax.rem(here, 2) * (
@@ -101,6 +103,10 @@
 
     def weight(self, slot):
         return jnp.where(slot < self.live, 1.0, 0.0).astype(f32)
+
+
+def step_of(slots):
+    return math.gcd(slots, 32)
 
 
 def group_of(slots):
@@ -121,7 +127,7 @@
             self.blocks.at[part], self.staged.at[part], self.semaphores.at[index]
         )
 
-    def loop(self, live, visit):
+    def loop(self, reach, visit):
         def step(index, _):
             self.copy(index).wait()
             visit([index * self.group + s for s in range(self.group)])
@@ -131,7 +137,7 @@
             self.copy(index).wait()
             return 0
 
-        groups = jnp.minimum((live + self.group - 1) // self.group, self.groups)
+        groups = jnp.minimum(reach // self.group, self.groups)
         lax.fori_loop(0, groups, step, 0)
         lax.fori_loop(groups, self.groups, leave, 0)
 
@@ -171,33 +177,30 @@
 
 
 def loop_held(places, held, visit, first=0):
-    group = math.gcd(held.shape[0], 32)
+    group = step_of(held.shape[0])
 
     def step(index, _):
         visit([first + index * group + s for s in range(group)])
         return 0
 
-    lax.fori_loop(0, (jnp.maximum(places.live - first, 0) + group - 1) // group, step, 0)
+    lax.fori_loop(0, jnp.maximum(places.reach - first, 0) // group, step, 0)
 
 
 def transposed_current_kernel(
     paired, *refs
 ):
-    counts, rows, columns, blocks, x_ref, other, *refs = refs
-    rows_held, columns_held, column_sum, held, own, semaphore, staged, semaphores, row_halves = refs
+    inputs, (blocks, x_ref, other), outputs, refs = refs[:3], refs[3:6], refs[6:9], refs[9:]
+    column_sum, held, own, semaphore, staged, semaphores, row_halves = refs
     copies = [
         pltpu.make_async_copy(source, target, semaphore.at[n])
-        for n, (source, target) in enumerate(
-            [(rows, rows_held), (columns, columns_held), (x_ref, own)]
-        )
+        for n, (source, target) in enumerate(zip((*inputs, x_ref), (*outputs, own)))
     ]
     for copy in copies:
         copy.start()
     stream = Stream(blocks, staged, semaphores)
     for copy in copies:
         copy.wait()
-    refs = counts, rows_held, columns_held
-    places = Places(refs, row_halves.shape[0], column_sum.shape[0], own.shape[-1] // LANES, paired)
+    places = Places(outputs, row_halves.shape[0], column_sum.shape[0], own.shape[-1] // LANES, paired)
     tiles = own.shape[-1] // LANES
     for t in range(tiles):
         for c, values in row_block_tiles(t, own, other, paired):
@@ -209,7 +212,7 @@
         held[slot] = pair
         return pair
 
-    stream.loop(places.live, lambda slots: visit_transposed(slots, places, split, row_halves, column_sum))
+    stream.loop(places.reach, lambda slots: visit_transposed(slots, places, split, row_halves, column_sum))
 
 
 def assemble_kernel(own, partner, column_sum, payload):
@@ -224,7 +227,7 @@
 
 
 def assemble_image_kernel(
-    own, base_partner, sums, received, column_sum, x_ref, x_partner, p_ref, payload, partner_image
+    own, base_partner, sums, received, column_sum, x_ref, x_partner, p_ref, payload
 ):
     tiles = own.shape[-1] // LANES
     near = payload.shape[0]
@@ -237,8 +240,6 @@
         ],
         axis=0,
     )
-    for t in range(tiles):
-        partner_image[:, lanes(t)] = partner[t]
     outer = times_transpose(basis, basis, highest)
     gram = jnp.concatenate(
         [outer[0:8], outer[8:16, 8:24], outer[16:24, 16:24], jnp.zeros((8, LANES - 48), f32)], axis=1
@@ -311,7 +312,7 @@
         first,
     )
     stream.loop(
-        places.live,
+        places.reach,
         lambda slots: visit_direct(slots, places, tile_from(staged), column_halves, row_sum),
     )
     for t in range(rest.shape[0]):
@@ -354,7 +355,7 @@
 
 def transposed_image_kernel(
     paired, counts, rows, columns, held, own, base_other, sums_other, p_ref, p_other, diagonal,
-    x_ref, q_ref,
+    x_ref, q_ref, received,
     column_sum, sum_halves, late, kept,
     row_halves,
 ):
@@ -378,8 +379,15 @@
             slots, places, lambda slot: held[slot], row_halves, column_sum
         ),
     )
-    for j in range(column_sum.shape[0]):
-        sum_halves[j] = stacked_halves(column_sum[j, 8:16])
+    scale = jnp.where(lax.broadcasted_iota(jnp.int32, (16, 1), 0) < 8, 1.0, 0.5).astype(f32)
+    count = column_sum.shape[0]
+    for j in range(count):
+        sum_halves[j] = stacked_halves(column_sum[j] * scale)
+    for t in range(tiles):
+        for n, previous in enumerate((p_ref[:, lanes(t)], received[tiles + t])):
+            sum_halves[count + n * tiles + t] = stacked_halves(
+                jnp.concatenate([jnp.zeros_like(previous), 0.5 * previous], axis=0)
+            )
 
     def keep(index, _):
         part = pl.ds(index * 8, 8)
@@ -409,51 +417,26 @@
     )
 
 
-def three_products(left, right):
-    rows, columns = left.shape[0] // 2, right.shape[0] // 2
-    cross = times_transpose(left, right)
-    return cross[:rows, :columns] + cross[rows:, :columns] + cross[:rows, columns:]
-
-
-def inner_kernel(
-    parts, sum_halves, late, y_ref, y_partner, p_ref, for_partner, first_received, spread
-):
+def inner_kernel(parts, sum_halves, late, for_partner, spread):
     near = parts.shape[0]
     tiles = parts.shape[1] // 4
-    column_set = [
+    left = [
         stacked_halves(parts[n, first + t])
         for first in (0, tiles)
         for n in range(near)
         for t in range(tiles)
     ]
-    gathered = three_products(
-        jnp.concatenate(column_set, axis=1),
+    for t in range(tiles):
+        left.append(stacked_halves(balanced_sum([parts[n, 2 * tiles + t] for n in range(near)])))
+    for t in range(tiles):
+        left.append(stacked_halves(for_partner[t]))
+    cross = times_transpose(
+        jnp.concatenate(left, axis=1),
         jnp.concatenate([sum_halves[j] for j in range(sum_halves.shape[0])], axis=1),
     )
-    own = [balanced_sum([parts[n, 2 * tiles + t] for n in range(near)]) for t in range(tiles)]
-    pair = three_products(
-        stacked_halves(jnp.concatenate(own + [for_partner[t] for t in range(tiles)], axis=1)),
-        stacked_halves(
-            jnp.concatenate(
-                [
-                    jnp.concatenate([y_ref[...], y_partner[...]], axis=1),
-                    0.5
-                    * jnp.concatenate(
-                        [p_ref[...]] + [first_received[tiles + t] for t in range(tiles)], axis=1
-                    ),
-                ],
-                axis=0,
-            )
-        ),
-    )
+    terms = cross[0:8, 0:16] + cross[8:16, 0:16] + cross[0:8, 16:32]
     total = late[...] + jnp.concatenate(
-        [
-            jnp.zeros((8, 32), f32),
-            pair[:, 0:8],
-            pair[:, 8:16] + 0.5 * gathered,
-            jnp.zeros((8, LANES - 48), f32),
-        ],
-        axis=1,
+        [jnp.zeros((8, 32), f32), terms, jnp.zeros((8, LANES - 48), f32)], axis=1
     )
     for n in range(spread.shape[0]):
         spread[n] = total
@@ -568,19 +551,19 @@
 
     other = from_columns(current)
     partner = to_partner(current)
-    *held_places, column_sum, held = call(
+    *places, column_sum, held = call(
         functools.partial(transposed_current_kernel, paired),
         "transposed_current",
-        [pltpu.SMEM(part.shape, part.dtype) for part in places[1:]]
+        [pltpu.SMEM(part.shape, part.dtype) for part in places]
         + [shape(column_tiles, 8, side), shape(slots, side, 2 * side, dtype=bf16)],
         [counts, *map(kept_in_hbm, places[1:]), blocks, kept_in_hbm(current), other],
-        [in_smem] + [in_hbm] * 4 + [in_vmem],
-        [pltpu.VMEM((8, width), f32), pltpu.SemaphoreType.DMA((3,))]
+        [pl.BlockSpec(memory_space=pl.ANY)] + [in_hbm] * 4 + [in_vmem],
+        [pltpu.VMEM((8, width), f32), pltpu.SemaphoreType.DMA((4,))]
         + stream_scratch(slots, side)
         + [pltpu.VMEM((row_tiles, 16, side), bf16)],
         micros=3.0,
     )
-    places[1:] = [pltpu.with_memory_space_constraint(part, pltpu.SMEM) for part in held_places]
+    places = [pltpu.with_memory_space_constraint(part, pltpu.SMEM) for part in places]
     payload = call(
         assemble_kernel,
         "assemble_current",
@@ -639,22 +622,22 @@
         "transposed_image",
         [
             shape(column_tiles, 16, side),
-            shape(column_tiles, 16, side, dtype=bf16),
+            shape(column_tiles + 2 * tiles, 32, side, dtype=bf16),
             shape(8, LANES),
             shape(slots // 2, side, 2 * side, dtype=bf16),
         ],
         [
             *places, held, image, base_other, sums_other, previous, previous_other, diagonal,
-            current, previous_image,
-        ],
-        [in_smem] * 3 + [in_vmem] * 9,
+            current, previous_image, first_received,
+        ],
+        [in_smem] * 3 + [in_vmem] * 10,
         [pltpu.VMEM((row_tiles, 32, side), bf16)],
         micros=1.8,
     )
-    payload, partner_image = call(
+    payload = call(
         assemble_image_kernel,
         "assemble_image",
-        [shape(near, 4 * tiles + 1, 8, side), shape(8, width)],
+        shape(near, 4 * tiles + 1, 8, side),
         [
             image, base_partner, sums, first_received, column_sum, current, partner, previous,
         ],
@@ -673,10 +656,8 @@
         inner_kernel,
         "inner_products",
         shape(2 * near * n_col, 8, LANES),
-        [
-            parts, sum_halves, late, image, partner_image, previous, for_partner, first_received,
-        ],
-        [in_vmem] * 8,
+        [parts, sum_halves, late, for_partner],
+        [in_vmem] * 4,
         micros=1.1,
     )
     everyone = [list(range(2 * near * n_col))[::-1]]

time: 55.6 us -> 56.3 us (1.013)
  starting transfers between devices: 13.3 us -> 14.3 us
  blocking collectives: 26.6 us -> 26 us
    all_to_all x1, starting transfers between devices: 2.57 us -> 3.57 us  [local(): lax.all_to_all(spread, devices, 0, 0, tiled=True, axis_index_groups=every...]
    all_to_all x2, blocking collectives: 26.6 us -> 26 us  [to_near(): lax.all_to_all(values, devices, 0, 0, tiled=True, axis_index_groups=groups)]
where the time goes in v5:
time: 56.3 us; the launch traced here: 55.9 us
  blocking collectives  26 us (46%)
  starting transfers between devices  14.3 us (25%)
  Pallas kernels  10.4 us (18%)
  waiting for transfers between devices  3.66 us (7%)
  between operations  1.42 us (3%)
    all_to_all x2, blocking collectives, to_near(): lax.all_to_all(values, devices, 0, 0, tiled=True, axis_index_groups=groups)  26 us
    ppermute x10, starting transfers between devices, swap(): return lax.ppermute(values, axis, [(0, 1), (1, 0)])  10.8 us
    pallas_call x14, Pallas kernels, call(): pl.pallas_call(kernel, out_shape=out_shape, in_specs=specs, out_specs=jax...  10.4 us
    all_to_all x1, starting transfers between devices, local(): lax.all_to_all(spread, devices, 0, 0, tiled=True, axis_index_groups=every...  3.57 us
    ppermute x10, waiting for transfers between devices, swap(): return lax.ppermute(values, axis, [(0, 1), (1, 0)])  3.02 us
  transfers between devices with their start and end apart: 11, of which 6 were waited for; matrix products, arithmetic and copies ran while one was open for 0% of the time, Pallas kernels for 14%

profile of v5, /device:TPU:0, one launch (start us, length us, event | category | flops | bytes accessed | tf_op | source)
XLA Modules:
  0.0 55.9 jit_solution(14432089769169445351)
XLA Ops:
  0.6 0.0 copy-start
  0.6 0.0 copy-start.1
  0.7 0.5 collective-permute-start
  1.2 3.7 %collective-permute-start.1 = (f32[8,512]{1,0:T(8,128)}, f32[8,512]{1,0:T(8,128)S(1)}, u32[]{:S(2)}, u32[]{:S(2)}) collective-permute-start(f32[8,512]{1,0:T(8,128)} %x_ref.5), channel_id=1, source_target_pairs={{0,16},{16,0},{1,17},{17,1},{2,18},{18,2},{3,19},{19,3},{4,20},{20... | collective-permute-start | bytes 49160 | tf_op jit(solution)/shard_map/ppermute | solution.py:534
  5.5 0.0 collective-permute-done.refs_5_
  5.5 2.3 %transposed_current.1 = (s32[1,1]{1,0:T(1,128)S(4)}, s32[1,1,64]{2,1,0:T(1,128)S(4)}, s32[1,1,64]{2,1,0:T(1,128)S(4)}, f32[64,8,128]{2,1,0:T(8,128)S(1)}, bf16[64,128,256]{2,1,0:T(8,128)(2,1)S(1)}) custom-call(s32[1,1]{1,0:T(1,128)S(6)} %copy.12.refs_0_, s32[1,1,64]{2,1,0:T(1,128)} %refs_1_.1, s32[1,1,64]{2,1,0:T(1,128)} %refs_2_.1, ...), custom_call_target="tpu_custom_call" | custom-call | bytes 1 | tf_op jit(solution)/shard_map/transposed_current/pallas_call | solution.py:26
  7.8 0.0 copy-start.2
  7.9 0.0 copy-start.3
  7.9 0.0 collective-permute-done.1.partner.x_partner
  7.9 0.0 copy-done
  7.9 13.7 %all_to_all.15.parts = f32[8,16,8,128]{3,2,1,0:T(8,128)S(1)} all-to-all(f32[8,16,8,128]{3,2,1,0:T(8,128)S(1)} %assemble_current.1), channel_id=1, replica_groups={{0,2,4,6,8,10,12,14},{9,11,13,15,1,3,5,7},{16,18,20,22,24,26,28,30},{25..., dimensions={0} | all-to-all | bytes 1048576 | tf_op jit(solution)/shard_map/all_to_all | solution.py:547
  21.7 0.0 copy-done.1
  21.7 1.3 %collective-permute-start.3 = (f32[9,8,128]{2,1,0:T(8,128)S(1)}, f32[9,8,128]{2,1,0:T(8,128)S(1)}, u32[]{:S(2)}, u32[]{:S(2)}) collective-permute-start(f32[9,8,128]{2,1,0:T(8,128)S(1)} %partner_sums.2.sums), channel_id=1, source_target_pairs={{0,16},{16,0},{1,17},{17,1},{2,18},{18,2},{3,19},{19,3},{4,20},{20... | collective-permute-start | bytes 110600 | tf_op jit(solution)/shard_map/ppermute | solution.py:534
  23.0 0.7 %direct_current.1.row_sum = f32[8,8,128]{2,1,0:T(8,128)S(1)} custom-call(s32[1,1]{1,0:T(1,128)S(4)} %get-tuple-element.27.counts, s32[1,1,64]{2,1,0:T(1,128)S(4)} %get-tuple-element.28.rows, s32[1,1,64]{2,1,0:T(1,128)S(4)} %get-tuple-element.29.columns, bf16[64,128,256]{2,1,0:T(8,128)(2,1)S(1)} %get-tuple-element.31.held, f32[8,16,8,128]{3,2,1,0:T(8,128)S(1)} %all_to_all.15.parts), custom_call_target="tpu_custom_call" | custom-call | bytes 1 | tf_op jit(solution)/shard_map/direct_current/pallas_call | solution.py:26
  23.7 0.0 copy-done.2
  23.7 0.1 collective-permute-start.2
  23.8 1.2 %collective-permute-done.2.theirs = f32[8,8,128]{2,1,0:T(8,128)S(1)} collective-permute-done((f32[8,8,128]{2,1,0:T(8,128)S(1)}, f32[8,8,128]{2,1,0:T(8,128)S(1)}, u32[]{:S(2)}, u32[]{:S(2)}) %collective-permute-start.2) | collective-permute-done | bytes 32800 | tf_op jit(solution)/shard_map/ppermute | solution.py:534
  25.0 1.7 %collective-permute-start.4 = (f32[5,8,128]{2,1,0:T(8,128)S(1)}, f32[5,8,128]{2,1,0:T(8,128)S(1)}, u32[]{:S(2)}, u32[]{:S(2)}) collective-permute-start(f32[5,8,128]{2,1,0:T(8,128)S(1)} %get-tuple-element.32.base), channel_id=1, source_target_pairs={{0,16},{16,0},{1,17},{17,1},{2,18},{18,2},{3,19},{19,3},{4,20},{20... | collective-permute-start | bytes 61448 | tf_op jit(solution)/shard_map/ppermute | solution.py:534
  26.7 0.0 collective-permute-start.6
  26.7 0.0 collective-permute-done.3.received
  26.7 0.5 collective-permute-start.5
  27.2 0.7 %collective-permute-done.6.p_other = f32[8,512]{1,0:T(8,128)S(1)} collective-permute-done((f32[8,512]{1,0:T(8,128)S(1)}, f32[8,512]{1,0:T(8,128)S(1)}, u32[]{:S(2)}, u32[]{:S(2)}) %collective-permute-start.6) | collective-permute-done | bytes 16416 | tf_op jit(solution)/shard_map/ppermute | solution.py:534
  27.9 0.2 collective-permute-done.5.sums_other
  28.1 0.0 copy-done.3
  28.1 0.9 %transposed_image.1 = (f32[64,16,128]{2,1,0:T(8,128)S(1)}, bf16[72,32,128]{2,1,0:T(8,128)(2,1)S(1)}, f32[8,128]{1,0:T(8,128)S(1)}, bf16[32,128,256]{2,1,0:T(8,128)(2,1)S(1)}) custom-call(s32[1,1]{1,0:T(1,128)S(4)} %get-tuple-element.27.counts, s32[1,1,64]{2,1,0:T(1,128)S(4)} %get-tuple-element.28.rows, s32[1,1,64]{2,1,0:T(1,128)S(4)} %get-tuple-element.29.columns, ...), custom_call_target="tpu_custom_call" | custom-call | bytes 1 | tf_op jit(solution)/shard_map/transposed_image/pallas_call | solution.py:26
  29.0 0.7 %collective-permute-done.4.base_partner = f32[5,8,128]{2,1,0:T(8,128)S(1)} collective-permute-done((f32[5,8,128]{2,1,0:T(8,128)S(1)}, f32[5,8,128]{2,1,0:T(8,128)S(1)}, u32[]{:S(2)}, u32[]{:S(2)}) %collective-permute-start.4) | collective-permute-done | bytes 20512 | tf_op jit(solution)/shard_map/ppermute | solution.py:534
  29.7 0.3 assemble_image.1
  30.0 12.3 %all_to_all.16.parts = f32[8,17,8,128]{3,2,1,0:T(8,128)S(1)} all-to-all(f32[8,17,8,128]{3,2,1,0:T(8,128)S(1)} %assemble_image.1), channel_id=1, replica_groups={{0,2,4,6,8,10,12,14},{9,11,13,15,1,3,5,7},{16,18,20,22,24,26,28,30},{25..., dimensions={0} | all-to-all | bytes 1114112 | tf_op jit(solution)/shard_map/all_to_all | solution.py:547
  42.3 1.1 %inner_products.1 = f32[32,8,128]{2,1,0:T(8,128)} custom-call(f32[8,17,8,128]{3,2,1,0:T(8,128)S(1)} %all_to_all.16.parts, bf16[72,32,128]{2,1,0:T(8,128)(2,1)S(1)} %get-tuple-element.42.sum_halves, f32[8,128]{1,0:T(8,128)S(1)} %get-tuple-element.43.late, f32[4,8,128]{2,1,0:T(8,128)S(1)} %get-tuple-element.44.for_partner), custom_call_target="tpu_custom_call" | custom-call | bytes 1 | tf_op jit(solution)/shard_map/inner_products/pallas_call | solution.py:26
  43.3 3.6 %all-to-all-start.2 = ((f32[32,8,128]{2,1,0:T(8,128)}), f32[32,8,128]{2,1,0:T(8,128)S(1)}, u32[]{:S(2)}, u32[]{:S(2)}) async-start(f32[32,8,128]{2,1,0:T(8,128)} %inner_products.1), calls=%async_computation.2 | async-start | bytes 262144 | tf_op jit(solution)/shard_map/all_to_all | solution.py:664
  46.9 0.3 collective-permute-start.7
  47.2 2.6 %collective-permute-start.8 = (f32[4,8,128]{2,1,0:T(8,128)S(1)}, f32[4,8,128]{2,1,0:T(8,128)S(1)}, u32[]{:S(2)}, u32[]{:S(2)}) collective-permute-start(f32[4,8,128]{2,1,0:T(8,128)S(1)} %get-tuple-element.44.for_partner), channel_id=1, source_target_pairs={{0,16},{16,0},{1,17},{17,1},{2,18},{18,2},{3,19},{19,3},{4,20},{20... | collective-permute-start | bytes 49160 | tf_op jit(solution)/shard_map/ppermute | solution.py:534
  49.8 0.0 collective-permute-done.7.theirs
  49.8 2.0 %direct_image.1 = (f32[8,8,128]{2,1,0:T(8,128)S(1)}, f32[4,8,128]{2,1,0:T(8,128)S(1)}, f32[8,128]{1,0:T(8,128)S(1)}) custom-call(s32[1,1]{1,0:T(1,128)S(4)} %get-tuple-element.27.counts, s32[1,1,64]{2,1,0:T(1,128)S(4)} %get-tuple-element.28.rows, s32[1,1,64]{2,1,0:T(1,128)S(4)} %get-tuple-element.29.columns, f32[64,128,128]{2,1,0:T(8,128)} %bitcast.6, ...), custom_call_target="tpu_custom_call" | custom-call | bytes 1 | tf_op jit(solution)/shard_map/direct_image/pallas_call | solution.py:26
  51.9 0.1 collective-permute-start.9
  52.0 1.9 %eliminate.1 = (f32[8,8]{1,0:T(8,128)S(1)}, f32[24,24]{1,0:T(8,128)S(1)}, f32[24,24]{1,0:T(8,128)S(1)}, f32[8,512]{1,0:T(8,128)}, f32[8,512]{1,0:T(8,128)}) custom-call(f32[8,128]{1,0:T(8,128)S(1)} %get-tuple-element.37.gram, f32[8,512]{1,0:T(8,128)S(1)} %copy-done, f32[8,512]{1,0:T(8,128)S(1)} %image.1.own.y_ref), custom_call_target="tpu_custom_call" | custom-call | bytes 1 | tf_op jit(solution)/shard_map/eliminate/pallas_call | solution.py:26
  53.9 0.3 collective-permute-done.8.received
  54.2 0.0 collective-permute-done.9.theirs
  54.2 0.6 %all-to-all-done.2.inner_parts = f32[32,8,128]{2,1,0:T(8,128)S(1)} async-done(((f32[32,8,128]{2,1,0:T(8,128)}), f32[32,8,128]{2,1,0:T(8,128)S(1)}, u32[]{:S(2)}, u32[]{:S(2)}) %all-to-all-start.2) | async-done | bytes 131104 | tf_op jit(solution)/shard_map/all_to_all | solution.py:664
  54.8 1.0 %finish.1 = (f32[8,512]{1,0:T(8,128)}, f32[24,24]{1,0:T(8,128)}) custom-call(f32[24,24]{1,0:T(8,128)S(1)} %get-tuple-element.40.inverse, f32[24,24]{1,0:T(8,128)S(1)} %get-tuple-element.41.pencil, f32[32,8,128]{2,1,0:T(8,128)S(1)} %all-to-all-done.2.inner_parts, f32[8,8]{1,0:T(8,128)S(1)} %get-tuple-element.45.ritz, f32[8,512]{1,0:T(8,128)S(1)} %image.1.own.y_ref, ...), custom_call_target="tpu_custom_call" | custom-call | bytes 1 | tf_op jit(solution)/shard_map/finish/pallas_call | solution.py:26
  (7 shorter events, 0.1 us)
Async XLA Ops:
  0.6 7.3 %copy-start = (f32[8,512]{1,0:T(8,128)S(1)}, f32[8,512]{1,0:T(8,128)}, u32[]{:S(2)}) copy-start(f32[8,512]{1,0:T(8,128)} %x_ref.5) | copy-start | bytes 49156
  0.6 21.0 %copy-start.1 = (f32[8,512]{1,0:T(8,128)S(1)}, f32[8,512]{1,0:T(8,128)}, u32[]{:S(2)}) copy-start(f32[8,512]{1,0:T(8,128)} %p_ref.3) | copy-start | bytes 49156
  0.7 4.8 %collective-permute-start = (f32[8,512]{1,0:T(8,128)}, f32[8,512]{1,0:T(8,128)S(1)}, u32[]{:S(2)}, u32[]{:S(2)}) collective-permute-start(f32[8,512]{1,0:T(8,128)} %x_ref.5), channel_id=1, source_target_pairs={{0,1},{1,0},{2,3},{3,2},{4,5},{5,4},{6,7},{7,6},{8,9},{9,8},{10,11... | collective-permute-start | bytes 49160 | tf_op jit(solution)/shard_map/ppermute | solution.py:534
  1.2 6.7 %collective-permute-start.1 = (f32[8,512]{1,0:T(8,128)}, f32[8,512]{1,0:T(8,128)S(1)}, u32[]{:S(2)}, u32[]{:S(2)}) collective-permute-start(f32[8,512]{1,0:T(8,128)} %x_ref.5), channel_id=1, source_target_pairs={{0,16},{16,0},{1,17},{17,1},{2,18},{18,2},{3,19},{19,3},{4,20},{20... | collective-permute-start | bytes 49160 | tf_op jit(solution)/shard_map/ppermute | solution.py:534
  7.8 15.8 %copy-start.2 = (f32[512]{0:T(512)S(1)}, f32[512]{0:T(512)}, u32[]{:S(2)}) copy-start(f32[512]{0:T(512)} %param.12) | copy-start | bytes 6148
  7.9 20.2 %copy-start.3 = (f32[8,512]{1,0:T(8,128)S(1)}, f32[8,512]{1,0:T(8,128)}, u32[]{:S(2)}) copy-start(f32[8,512]{1,0:T(8,128)} %q_ref.1) | copy-start | bytes 49156
  21.7 5.0 %collective-permute-start.3 = (f32[9,8,128]{2,1,0:T(8,128)S(1)}, f32[9,8,128]{2,1,0:T(8,128)S(1)}, u32[]{:S(2)}, u32[]{:S(2)}) collective-permute-start(f32[9,8,128]{2,1,0:T(8,128)S(1)} %partner_sums.2.sums), channel_id=1, source_target_pairs={{0,16},{16,0},{1,17},{17,1},{2,18},{18,2},{3,19},{19,3},{4,20},{20... | collective-permute-start | bytes 110600 | tf_op jit(solution)/shard_map/ppermute | solution.py:534
  23.7 1.3 %collective-permute-start.2 = (f32[8,8,128]{2,1,0:T(8,128)S(1)}, f32[8,8,128]{2,1,0:T(8,128)S(1)}, u32[]{:S(2)}, u32[]{:S(2)}) collective-permute-start(f32[8,8,128]{2,1,0:T(8,128)S(1)} %combine.1.mine), channel_id=1, source_target_pairs={{0,1},{1,0},{2,3},{3,2},{4,5},{5,4},{6,7},{7,6},{8,9},{9,8},{10,11... | collective-permute-start | bytes 98312 | tf_op jit(solution)/shard_map/ppermute | solution.py:534
  25.0 4.7 %collective-permute-start.4 = (f32[5,8,128]{2,1,0:T(8,128)S(1)}, f32[5,8,128]{2,1,0:T(8,128)S(1)}, u32[]{:S(2)}, u32[]{:S(2)}) collective-permute-start(f32[5,8,128]{2,1,0:T(8,128)S(1)} %get-tuple-element.32.base), channel_id=1, source_target_pairs={{0,16},{16,0},{1,17},{17,1},{2,18},{18,2},{3,19},{19,3},{4,20},{20... | collective-permute-start | bytes 61448 | tf_op jit(solution)/shard_map/ppermute | solution.py:534
  26.7 1.2 %collective-permute-start.6 = (f32[8,512]{1,0:T(8,128)S(1)}, f32[8,512]{1,0:T(8,128)S(1)}, u32[]{:S(2)}, u32[]{:S(2)}) collective-permute-start(f32[8,512]{1,0:T(8,128)S(1)} %copy-done.1), channel_id=1, source_target_pairs={{0,1},{1,0},{2,3},{3,2},{4,5},{5,4},{6,7},{7,6},{8,9},{9,8},{10,11... | collective-permute-start | bytes 49160 | tf_op jit(solution)/shard_map/ppermute | solution.py:534
  26.7 1.3 %collective-permute-start.5 = (f32[4,8,128]{2,1,0:T(8,128)S(1)}, f32[4,8,128]{2,1,0:T(8,128)S(1)}, u32[]{:S(2)}, u32[]{:S(2)}) collective-permute-start(f32[4,8,128]{2,1,0:T(8,128)S(1)} %slice.4), channel_id=1, source_target_pairs={{0,1},{1,0},{2,3},{3,2},{4,5},{5,4},{6,7},{7,6},{8,9},{9,8},{10,11... | collective-permute-start | bytes 49160 | tf_op jit(solution)/shard_map/ppermute | solution.py:534
  43.3 11.5 %all-to-all-start.2 = ((f32[32,8,128]{2,1,0:T(8,128)}), f32[32,8,128]{2,1,0:T(8,128)S(1)}, u32[]{:S(2)}, u32[]{:S(2)}) async-start(f32[32,8,128]{2,1,0:T(8,128)} %inner_products.1), calls=%async_computation.2 | async-start | bytes 262144 | tf_op jit(solution)/shard_map/all_to_all | solution.py:664
  46.9 2.9 %collective-permute-start.7 = (f32[8,128]{1,0:T(8,128)S(1)}, f32[8,128]{1,0:T(8,128)S(1)}, u32[]{:S(2)}, u32[]{:S(2)}) collective-permute-start(f32[8,128]{1,0:T(8,128)S(1)} %get-tuple-element.36.mine), channel_id=1, source_target_pairs={{0,1},{1,0},{2,3},{3,2},{4,5},{5,4},{6,7},{7,6},{8,9},{9,8},{10,11... | collective-permute-start | bytes 12296 | tf_op jit(solution)/shard_map/ppermute | solution.py:534
  47.2 7.0 %collective-permute-start.8 = (f32[4,8,128]{2,1,0:T(8,128)S(1)}, f32[4,8,128]{2,1,0:T(8,128)S(1)}, u32[]{:S(2)}, u32[]{:S(2)}) collective-permute-start(f32[4,8,128]{2,1,0:T(8,128)S(1)} %get-tuple-element.44.for_partner), channel_id=1, source_target_pairs={{0,16},{16,0},{1,17},{17,1},{2,18},{18,2},{3,19},{19,3},{4,20},{20... | collective-permute-start | bytes 49160 | tf_op jit(solution)/shard_map/ppermute | solution.py:534
  51.9 2.3 %collective-permute-start.9 = (f32[4,8,128]{2,1,0:T(8,128)S(1)}, f32[4,8,128]{2,1,0:T(8,128)S(1)}, u32[]{:S(2)}, u32[]{:S(2)}) collective-permute-start(f32[4,8,128]{2,1,0:T(8,128)S(1)} %get-tuple-element.47), channel_id=1, source_target_pairs={{0,1},{1,0},{2,3},{3,2},{4,5},{5,4},{6,7},{7,6},{8,9},{9,8},{10,11... | collective-permute-start | bytes 49160 | tf_op jit(solution)/shard_map/ppermute | solution.py:534

commit v6 on v5

--- a/solution.py
+++ b/solution.py
@@ -227,7 +227,7 @@
 
 
 def assemble_image_kernel(
-    own, base_partner, sums, received, column_sum, x_ref, x_partner, p_ref, payload
+    own, base_partner, sums, column_sum, x_ref, x_partner, p_ref, payload, previous_halves
 ):
     tiles = own.shape[-1] // LANES
     near = payload.shape[0]
@@ -236,10 +236,15 @@
         [
             jnp.concatenate([x_ref[...], x_partner[...]], axis=1),
             jnp.concatenate([own[...]] + partner, axis=1),
-            jnp.concatenate([p_ref[...]] + [received[tiles + t] for t in range(tiles)], axis=1),
+            jnp.concatenate([p_ref[...]] + [base_partner[tiles + t] for t in range(tiles)], axis=1),
         ],
         axis=0,
     )
+    for t in range(tiles):
+        for n, previous in enumerate((p_ref[:, lanes(t)], base_partner[tiles + t])):
+            previous_halves[n * tiles + t] = stacked_halves(
+                jnp.concatenate([jnp.zeros_like(previous), 0.5 * previous], axis=0)
+            )
     outer = times_transpose(basis, basis, highest)
     gram = jnp.concatenate(
         [outer[0:8], outer[8:16, 8:24], outer[16:24, 16:24], jnp.zeros((8, LANES - 48), f32)], axis=1
@@ -253,13 +258,11 @@
         payload[n, 4 * tiles] = gram
 
 
-def first_partner_sums_kernel(parts, previous, sums):
+def first_partner_sums_kernel(parts, sums):
     near = parts.shape[0]
     tiles = parts.shape[1] // 4
     for t in range(tiles):
         sums[t] = balanced_sum([parts[n, 3 * tiles + t] for n in range(near)])
-        sums[tiles + t] = previous[:, lanes(t)]
-    sums[2 * tiles] = jnp.zeros_like(sums[2 * tiles])
 
 
 def partner_sums_kernel(parts, sums, gram):
@@ -327,9 +330,11 @@
     )
 
 
-def combine_kernel(paired, parts, row_sum, diagonal, vectors, mine, *rows):
+def combine_kernel(paired, parts, row_sum, diagonal, vectors, sums, other_sums, mine, shipped, *rows):
     tiles = parts.shape[1] // 4
     for t in range(tiles):
+        shipped[t] = sums[t]
+        shipped[tiles + t] = other_sums[t]
         total = half_result(t, parts, diagonal, vectors)
         if paired:
             mine[t] = total + row_sum[t]
@@ -340,12 +345,12 @@
                 rows[0][c, :, lanes(t)] = row_sum[c * tiles + t]
 
 
-def base_kernel(mine, theirs, own, other):
-    tiles = own.shape[0] - 1
+def base_kernel(mine, theirs, previous, own, other):
+    tiles = own.shape[0] // 2
     for t in range(tiles):
         own[t] = mine[t] + theirs[tiles + t]
+        own[tiles + t] = previous[:, lanes(t)]
         other[:, lanes(t)] = theirs[t] + mine[tiles + t]
-    own[tiles] = jnp.zeros_like(own[tiles])
 
 
 def image_kernel(base, received, image):
@@ -355,7 +360,7 @@
 
 def transposed_image_kernel(
     paired, counts, rows, columns, held, own, base_other, sums_other, p_ref, p_other, diagonal,
-    x_ref, q_ref, received,
+    x_ref, q_ref,
     column_sum, sum_halves, late, kept,
     row_halves,
 ):
@@ -365,7 +370,9 @@
     tiles = width // LANES
     other = base_other
     if paired:
-        other = base_other[...] + jnp.concatenate([sums_other[t] for t in range(tiles)], axis=1)
+        other = base_other[...] + jnp.concatenate(
+            [sums_other[tiles + t] for t in range(tiles)], axis=1
+        )
     for t in range(tiles):
         for (c, values), (_, previous) in zip(
             row_block_tiles(t, own, other, paired), row_block_tiles(t, p_ref, p_other, paired)
@@ -380,14 +387,8 @@
         ),
     )
     scale = jnp.where(lax.broadcasted_iota(jnp.int32, (16, 1), 0) < 8, 1.0, 0.5).astype(f32)
-    count = column_sum.shape[0]
-    for j in range(count):
+    for j in range(column_sum.shape[0]):
         sum_halves[j] = stacked_halves(column_sum[j] * scale)
-    for t in range(tiles):
-        for n, previous in enumerate((p_ref[:, lanes(t)], received[tiles + t])):
-            sum_halves[count + n * tiles + t] = stacked_halves(
-                jnp.concatenate([jnp.zeros_like(previous), 0.5 * previous], axis=0)
-            )
 
     def keep(index, _):
         part = pl.ds(index * 8, 8)
@@ -417,7 +418,7 @@
     )
 
 
-def inner_kernel(parts, sum_halves, late, for_partner, spread):
+def inner_kernel(parts, sum_halves, previous_halves, late, for_partner, spread):
     near = parts.shape[0]
     tiles = parts.shape[1] // 4
     left = [
@@ -432,7 +433,9 @@
         left.append(stacked_halves(for_partner[t]))
     cross = times_transpose(
         jnp.concatenate(left, axis=1),
-        jnp.concatenate([sum_halves[j] for j in range(sum_halves.shape[0])], axis=1),
+        jnp.concatenate(
+            [ref[j] for ref in (sum_halves, previous_halves) for j in range(ref.shape[0])], axis=1
+        ),
     )
     terms = cross[0:8, 0:16] + cross[8:16, 0:16] + cross[0:8, 16:32]
     total = late[...] + jnp.concatenate(
@@ -573,13 +576,9 @@
     )
     parts = to_near(payload)
     sums = call(
-        first_partner_sums_kernel,
-        "partner_sums",
-        shape(2 * tiles + 1, 8, side),
-        [parts, previous],
-        [in_vmem] * 2,
-    )
-    first_received = to_partner(sums)
+        first_partner_sums_kernel, "partner_sums", shape(tiles, 8, side), [parts], [in_vmem]
+    )
+    other_sums = swap(sums) if paired else sums
     row_sum = call(
         functools.partial(direct_held_kernel, paired),
         "direct_current",
@@ -593,26 +592,28 @@
         call,
         functools.partial(combine_kernel, paired),
         "combine",
-        operands=[parts, row_sum, diagonal, current],
-        specs=[in_vmem] * 4,
+        operands=[parts, row_sum, diagonal, current, sums, other_sums],
+        specs=[in_vmem] * 6,
     )
     if paired:
         previous_other = swap(previous)
-        mine = combine(out_shape=shape(2 * tiles, 8, side))
+        mine, shipped = combine(out_shape=[shape(2 * tiles, 8, side)] * 2)
         base, base_other = call(
             base_kernel,
             "base",
-            [shape(tiles + 1, 8, side), shape(8, width)],
-            [mine, swap(mine)],
-            [in_vmem] * 2,
+            [shape(2 * tiles, 8, side), shape(8, width)],
+            [mine, swap(mine), previous],
+            [in_vmem] * 3,
         )
-        sums_other = swap(first_received[:tiles])
     else:
-        mine, rows = combine(out_shape=[shape(8, width), shape(n_col, 8, width)])
+        mine, shipped, rows = combine(
+            out_shape=[shape(8, width), shape(2 * tiles, 8, side), shape(n_col, 8, width)]
+        )
         base = mine + jnp.sum(lax.all_to_all(rows, "col", 0, 0, tiled=True), axis=0)
-        base = base.reshape(8, tiles, side).transpose(1, 0, 2)
-        sums_other = first_received
+        base = jnp.concatenate([base, previous], axis=1)
+        base = base.reshape(8, 2 * tiles, side).transpose(1, 0, 2)
         previous_other = lax.all_gather(previous, "col", axis=0)
+    first_received = to_partner(shipped)
     base_partner = to_partner(base)
     image = call(image_kernel, "image", shape(8, width), [base, first_received], [in_vmem] * 2)
     if not paired:
@@ -622,26 +623,27 @@
         "transposed_image",
         [
             shape(column_tiles, 16, side),
-            shape(column_tiles + 2 * tiles, 32, side, dtype=bf16),
+            shape(column_tiles, 32, side, dtype=bf16),
             shape(8, LANES),
             shape(slots // 2, side, 2 * side, dtype=bf16),
         ],
         [
-            *places, held, image, base_other, sums_other, previous, previous_other, diagonal,
-            current, previous_image, first_received,
-        ],
-        [in_smem] * 3 + [in_vmem] * 10,
+            *places, held, image, base_other, first_received, previous, previous_other, diagonal,
+            current, previous_image,
+        ],
+        [in_smem] * 3 + [in_vmem] * 9,
         [pltpu.VMEM((row_tiles, 32, side), bf16)],
         micros=1.8,
     )
-    payload = call(
+    payload, previous_halves = call(
         assemble_image_kernel,
         "assemble_image",
-        shape(near, 4 * tiles + 1, 8, side),
-        [
-            image, base_partner, sums, first_received, column_sum, current, partner, previous,
-        ],
-        [in_vmem] * 8,
+        [
+            shape(near, 4 * tiles + 1, 8, side),
+            shape(2 * tiles, 32, side, dtype=bf16),
+        ],
+        [image, base_partner, sums, column_sum, current, partner, previous],
+        [in_vmem] * 7,
     )
     parts = to_near(payload)
     for_partner, gram = call(
@@ -656,8 +658,8 @@
         inner_kernel,
         "inner_products",
         shape(2 * near * n_col, 8, LANES),
-        [parts, sum_halves, late, for_partner],
-        [in_vmem] * 4,
+        [parts, sum_halves, previous_halves, late, for_partner],
+        [in_vmem] * 5,
         micros=1.1,
     )
     everyone = [list(range(2 * near * n_col))[::-1]]

time: 56.3 us -> 55.6 us (0.988)
  starting transfers between devices: 14.3 us -> 13 us
  waiting for transfers between devices: 3.66 us -> 4.56 us
    all_to_all x1, starting transfers between devices: 3.57 us -> 2.56 us  [local(): lax.all_to_all(spread, devices, 0, 0, tiled=True, axis_index_groups=every...]
    ppermute x10, waiting for transfers between devices: 3.02 us -> 3.9 us  [swap(): return lax.ppermute(values, axis, [(0, 1), (1, 0)])]
  transfers between devices with their start and end apart: 11 -> 11, of which waited for: 6 -> 4; matrix products, arithmetic and copies ran while one was open for 0% -> 0% of each run, Pallas kernels for 14% -> 14%
where the time goes in v6:
time: 55.6 us; the launch traced here: 55.2 us
  blocking collectives  25.8 us (46%)
  starting transfers between devices  13 us (23%)
  Pallas kernels  10.4 us (19%)
  waiting for transfers between devices  4.56 us (8%)
  between operations  1.43 us (3%)
    all_to_all x2, blocking collectives, to_near(): lax.all_to_all(values, devices, 0, 0, tiled=True, axis_index_groups=groups)  25.8 us
    ppermute x10, starting transfers between devices, swap(): return lax.ppermute(values, axis, [(0, 1), (1, 0)])  10.5 us
    pallas_call x14, Pallas kernels, call(): pl.pallas_call(kernel, out_shape=out_shape, in_specs=specs, out_specs=jax...  10.4 us
    ppermute x10, waiting for transfers between devices, swap(): return lax.ppermute(values, axis, [(0, 1), (1, 0)])  3.9 us
    all_to_all x1, starting transfers between devices, local(): lax.all_to_all(spread, devices, 0, 0, tiled=True, axis_index_groups=every...  2.56 us
  transfers between devices with their start and end apart: 11, of which 4 were waited for; matrix products, arithmetic and copies ran while one was open for 0% of the time, Pallas kernels for 14%

profile of v6, /device:TPU:0, one launch (start us, length us, event | category | flops | bytes accessed | tf_op | source)
XLA Modules:
  0.0 55.2 jit_solution(4514705517090149204)
XLA Ops:
  0.6 0.0 copy-start
  0.6 0.5 collective-permute-start
  1.2 3.7 %collective-permute-start.1 = (f32[8,512]{1,0:T(8,128)}, f32[8,512]{1,0:T(8,128)S(1)}, u32[]{:S(2)}, u32[]{:S(2)}) collective-permute-start(f32[8,512]{1,0:T(8,128)} %x_ref.5), channel_id=1, source_target_pairs={{0,16},{16,0},{1,17},{17,1},{2,18},{18,2},{3,19},{19,3},{4,20},{20... | collective-permute-start | bytes 49160 | tf_op jit(solution)/shard_map/ppermute | solution.py:537
  5.5 0.0 collective-permute-done.refs_5_
  5.5 2.3 %transposed_current.1 = (s32[1,1]{1,0:T(1,128)S(4)}, s32[1,1,64]{2,1,0:T(1,128)S(4)}, s32[1,1,64]{2,1,0:T(1,128)S(4)}, f32[64,8,128]{2,1,0:T(8,128)S(1)}, bf16[64,128,256]{2,1,0:T(8,128)(2,1)S(1)}) custom-call(s32[1,1]{1,0:T(1,128)S(6)} %copy.12.refs_0_, s32[1,1,64]{2,1,0:T(1,128)} %refs_1_.1, s32[1,1,64]{2,1,0:T(1,128)} %refs_2_.1, ...), custom_call_target="tpu_custom_call" | custom-call | bytes 1 | tf_op jit(solution)/shard_map/transposed_current/pallas_call | solution.py:26
  7.8 0.0 copy-start.2
  7.9 0.0 copy-start.1
  7.9 0.0 copy-start.3
  7.9 0.0 collective-permute-done.1.partner.x_partner
  7.9 0.0 copy-done
  7.9 14.3 %all_to_all.15.parts = f32[8,16,8,128]{3,2,1,0:T(8,128)S(1)} all-to-all(f32[8,16,8,128]{3,2,1,0:T(8,128)S(1)} %assemble_current.1), channel_id=1, replica_groups={{0,2,4,6,8,10,12,14},{9,11,13,15,1,3,5,7},{16,18,20,22,24,26,28,30},{25..., dimensions={0} | all-to-all | bytes 1048576 | tf_op jit(solution)/shard_map/all_to_all | solution.py:550
  22.2 0.1 collective-permute-start.2
  22.3 0.7 %direct_current.1.row_sum = f32[8,8,128]{2,1,0:T(8,128)S(1)} custom-call(s32[1,1]{1,0:T(1,128)S(4)} %get-tuple-element.31.counts, s32[1,1,64]{2,1,0:T(1,128)S(4)} %get-tuple-element.32.rows, s32[1,1,64]{2,1,0:T(1,128)S(4)} %get-tuple-element.33.columns, bf16[64,128,256]{2,1,0:T(8,128)(2,1)S(1)} %get-tuple-element.35.held, f32[8,16,8,128]{3,2,1,0:T(8,128)S(1)} %all_to_all.15.parts), custom_call_target="tpu_custom_call" | custom-call | bytes 1 | tf_op jit(solution)/shard_map/direct_current/pallas_call | solution.py:26
  23.0 0.5 collective-permute-done.2.other_sums
  23.5 0.0 copy-done.2
  23.5 0.2 collective-permute-start.3
  23.8 1.2 %collective-permute-start.4 = (f32[8,8,128]{2,1,0:T(8,128)S(1)}, f32[8,8,128]{2,1,0:T(8,128)S(1)}, u32[]{:S(2)}, u32[]{:S(2)}) collective-permute-start(f32[8,8,128]{2,1,0:T(8,128)S(1)} %get-tuple-element.38), channel_id=1, source_target_pairs={{0,16},{16,0},{1,17},{17,1},{2,18},{18,2},{3,19},{19,3},{4,20},{20... | collective-permute-start | bytes 98312 | tf_op jit(solution)/shard_map/ppermute | solution.py:537
  24.9 0.0 collective-permute-done.3.theirs
  24.9 0.0 copy-done.1
  25.0 1.8 %collective-permute-start.5 = (f32[8,8,128]{2,1,0:T(8,128)S(1)}, f32[8,8,128]{2,1,0:T(8,128)S(1)}, u32[]{:S(2)}, u32[]{:S(2)}) collective-permute-start(f32[8,8,128]{2,1,0:T(8,128)S(1)} %get-tuple-element.37.base), channel_id=1, source_target_pairs={{0,16},{16,0},{1,17},{17,1},{2,18},{18,2},{3,19},{19,3},{4,20},{20... | collective-permute-start | bytes 98312 | tf_op jit(solution)/shard_map/ppermute | solution.py:537
  26.8 0.0 collective-permute-start.6
  26.8 3.1 %collective-permute-done.4.received.sums_other = f32[8,8,128]{2,1,0:T(8,128)S(1)} collective-permute-done((f32[8,8,128]{2,1,0:T(8,128)S(1)}, f32[8,8,128]{2,1,0:T(8,128)S(1)}, u32[]{:S(2)}, u32[]{:S(2)}) %collective-permute-start.4) | collective-permute-done | bytes 32800 | tf_op jit(solution)/shard_map/ppermute | solution.py:537
  29.9 0.0 collective-permute-done.6.p_other
  29.9 0.0 copy-done.3
  29.9 0.9 %transposed_image.1 = (f32[64,16,128]{2,1,0:T(8,128)S(1)}, bf16[64,32,128]{2,1,0:T(8,128)(2,1)S(1)}, f32[8,128]{1,0:T(8,128)S(1)}, bf16[32,128,256]{2,1,0:T(8,128)(2,1)S(1)}) custom-call(s32[1,1]{1,0:T(1,128)S(4)} %get-tuple-element.31.counts, s32[1,1,64]{2,1,0:T(1,128)S(4)} %get-tuple-element.32.rows, s32[1,1,64]{2,1,0:T(1,128)S(4)} %get-tuple-element.33.columns, ...), custom_call_target="tpu_custom_call" | custom-call | bytes 1 | tf_op jit(solution)/shard_map/transposed_image/pallas_call | solution.py:26
  30.8 0.0 collective-permute-done.5.base_partner
  30.8 0.3 assemble_image.1
  31.1 11.5 %all_to_all.16.parts = f32[8,17,8,128]{3,2,1,0:T(8,128)S(1)} all-to-all(f32[8,17,8,128]{3,2,1,0:T(8,128)S(1)} %get-tuple-element.41), channel_id=1, replica_groups={{0,2,4,6,8,10,12,14},{9,11,13,15,1,3,5,7},{16,18,20,22,24,26,28,30},{25..., dimensions={0} | all-to-all | bytes 1114112 | tf_op jit(solution)/shard_map/all_to_all | solution.py:550
  42.6 1.1 %inner_products.1 = f32[32,8,128]{2,1,0:T(8,128)} custom-call(f32[8,17,8,128]{3,2,1,0:T(8,128)S(1)} %all_to_all.16.parts, bf16[64,32,128]{2,1,0:T(8,128)(2,1)S(1)} %get-tuple-element.49.sum_halves, bf16[8,32,128]{2,1,0:T(8,128)(2,1)S(1)} %get-tuple-element.50.previous_halves, f32[8,128]{1,0:T(8,128)S(1)} %get-tuple-element.51.late, ...), custom_call_target="tpu_custom_call" | custom-call | bytes 1 | tf_op jit(solution)/shard_map/inner_products/pallas_call | solution.py:26
  43.7 2.6 %all-to-all-start.2 = ((f32[32,8,128]{2,1,0:T(8,128)}), f32[32,8,128]{2,1,0:T(8,128)S(1)}, u32[]{:S(2)}, u32[]{:S(2)}) async-start(f32[32,8,128]{2,1,0:T(8,128)} %inner_products.1), calls=%async_computation.2 | async-start | bytes 262144 | tf_op jit(solution)/shard_map/all_to_all | solution.py:666
  46.3 0.2 collective-permute-start.7
  46.5 2.7 %collective-permute-start.8 = (f32[4,8,128]{2,1,0:T(8,128)S(1)}, f32[4,8,128]{2,1,0:T(8,128)S(1)}, u32[]{:S(2)}, u32[]{:S(2)}) collective-permute-start(f32[4,8,128]{2,1,0:T(8,128)S(1)} %get-tuple-element.52.for_partner), channel_id=1, source_target_pairs={{0,16},{16,0},{1,17},{17,1},{2,18},{18,2},{3,19},{19,3},{4,20},{20... | collective-permute-start | bytes 49160 | tf_op jit(solution)/shard_map/ppermute | solution.py:537
  49.2 0.0 collective-permute-done.7.theirs
  49.2 2.1 %direct_image.1 = (f32[8,8,128]{2,1,0:T(8,128)S(1)}, f32[4,8,128]{2,1,0:T(8,128)S(1)}, f32[8,128]{1,0:T(8,128)S(1)}) custom-call(s32[1,1]{1,0:T(1,128)S(4)} %get-tuple-element.31.counts, s32[1,1,64]{2,1,0:T(1,128)S(4)} %get-tuple-element.32.rows, s32[1,1,64]{2,1,0:T(1,128)S(4)} %get-tuple-element.33.columns, f32[64,128,128]{2,1,0:T(8,128)} %bitcast.6, ...), custom_call_target="tpu_custom_call" | custom-call | bytes 1 | tf_op jit(solution)/shard_map/direct_image/pallas_call | solution.py:26
  51.2 0.1 collective-permute-start.9
  51.3 1.9 %eliminate.1 = (f32[8,8]{1,0:T(8,128)S(1)}, f32[24,24]{1,0:T(8,128)S(1)}, f32[24,24]{1,0:T(8,128)S(1)}, f32[8,512]{1,0:T(8,128)}, f32[8,512]{1,0:T(8,128)}) custom-call(f32[8,128]{1,0:T(8,128)S(1)} %get-tuple-element.44.gram, f32[8,512]{1,0:T(8,128)S(1)} %copy-done, f32[8,512]{1,0:T(8,128)S(1)} %image.1.own.y_ref), custom_call_target="tpu_custom_call" | custom-call | bytes 1 | tf_op jit(solution)/shard_map/eliminate/pallas_call | solution.py:26
  53.2 0.3 collective-permute-done.8.received
  53.5 0.0 collective-permute-done.9.theirs
  53.5 0.7 %all-to-all-done.2.inner_parts = f32[32,8,128]{2,1,0:T(8,128)S(1)} async-done(((f32[32,8,128]{2,1,0:T(8,128)}), f32[32,8,128]{2,1,0:T(8,128)S(1)}, u32[]{:S(2)}, u32[]{:S(2)}) %all-to-all-start.2) | async-done | bytes 131104 | tf_op jit(solution)/shard_map/all_to_all | solution.py:666
  54.2 1.0 %finish.1 = (f32[8,512]{1,0:T(8,128)}, f32[24,24]{1,0:T(8,128)}) custom-call(f32[24,24]{1,0:T(8,128)S(1)} %get-tuple-element.47.inverse, f32[24,24]{1,0:T(8,128)S(1)} %get-tuple-element.48.pencil, f32[32,8,128]{2,1,0:T(8,128)S(1)} %all-to-all-done.2.inner_parts, f32[8,8]{1,0:T(8,128)S(1)} %get-tuple-element.53.ritz, f32[8,512]{1,0:T(8,128)S(1)} %image.1.own.y_ref, ...), custom_call_target="tpu_custom_call" | custom-call | bytes 1 | tf_op jit(solution)/shard_map/finish/pallas_call | solution.py:26
  (6 shorter events, 0.1 us)
Async XLA Ops:
  0.6 7.3 %copy-start = (f32[8,512]{1,0:T(8,128)S(1)}, f32[8,512]{1,0:T(8,128)}, u32[]{:S(2)}) copy-start(f32[8,512]{1,0:T(8,128)} %x_ref.5) | copy-start | bytes 49156
  0.6 4.8 %collective-permute-start = (f32[8,512]{1,0:T(8,128)}, f32[8,512]{1,0:T(8,128)S(1)}, u32[]{:S(2)}, u32[]{:S(2)}) collective-permute-start(f32[8,512]{1,0:T(8,128)} %x_ref.5), channel_id=1, source_target_pairs={{0,1},{1,0},{2,3},{3,2},{4,5},{5,4},{6,7},{7,6},{8,9},{9,8},{10,11... | collective-permute-start | bytes 49160 | tf_op jit(solution)/shard_map/ppermute | solution.py:537
  1.2 6.7 %collective-permute-start.1 = (f32[8,512]{1,0:T(8,128)}, f32[8,512]{1,0:T(8,128)S(1)}, u32[]{:S(2)}, u32[]{:S(2)}) collective-permute-start(f32[8,512]{1,0:T(8,128)} %x_ref.5), channel_id=1, source_target_pairs={{0,16},{16,0},{1,17},{17,1},{2,18},{18,2},{3,19},{19,3},{4,20},{20... | collective-permute-start | bytes 49160 | tf_op jit(solution)/shard_map/ppermute | solution.py:537
  7.8 15.7 %copy-start.2 = (f32[512]{0:T(512)S(1)}, f32[512]{0:T(512)}, u32[]{:S(2)}) copy-start(f32[512]{0:T(512)} %param.12) | copy-start | bytes 6148
  7.9 17.1 %copy-start.1 = (f32[8,512]{1,0:T(8,128)S(1)}, f32[8,512]{1,0:T(8,128)}, u32[]{:S(2)}) copy-start(f32[8,512]{1,0:T(8,128)} %p_ref.3) | copy-start | bytes 49156
  7.9 22.0 %copy-start.3 = (f32[8,512]{1,0:T(8,128)S(1)}, f32[8,512]{1,0:T(8,128)}, u32[]{:S(2)}) copy-start(f32[8,512]{1,0:T(8,128)} %q_ref.1) | copy-start | bytes 49156
  22.2 1.2 %collective-permute-start.2 = (f32[4,8,128]{2,1,0:T(8,128)S(1)}, f32[4,8,128]{2,1,0:T(8,128)S(1)}, u32[]{:S(2)}, u32[]{:S(2)}) collective-permute-start(f32[4,8,128]{2,1,0:T(8,128)S(1)} %partner_sums.2.sums), channel_id=1, source_target_pairs={{0,1},{1,0},{2,3},{3,2},{4,5},{5,4},{6,7},{7,6},{8,9},{9,8},{10,11... | collective-permute-start | bytes 49160 | tf_op jit(solution)/shard_map/ppermute | solution.py:537
  23.5 1.4 %collective-permute-start.3 = (f32[8,8,128]{2,1,0:T(8,128)S(1)}, f32[8,8,128]{2,1,0:T(8,128)S(1)}, u32[]{:S(2)}, u32[]{:S(2)}) collective-permute-start(f32[8,8,128]{2,1,0:T(8,128)S(1)} %get-tuple-element.36.mine), channel_id=1, source_target_pairs={{0,1},{1,0},{2,3},{3,2},{4,5},{5,4},{6,7},{7,6},{8,9},{9,8},{10,11... | collective-permute-start | bytes 98312 | tf_op jit(solution)/shard_map/ppermute | solution.py:537
  23.8 6.1 %collective-permute-start.4 = (f32[8,8,128]{2,1,0:T(8,128)S(1)}, f32[8,8,128]{2,1,0:T(8,128)S(1)}, u32[]{:S(2)}, u32[]{:S(2)}) collective-permute-start(f32[8,8,128]{2,1,0:T(8,128)S(1)} %get-tuple-element.38), channel_id=1, source_target_pairs={{0,16},{16,0},{1,17},{17,1},{2,18},{18,2},{3,19},{19,3},{4,20},{20... | collective-permute-start | bytes 98312 | tf_op jit(solution)/shard_map/ppermute | solution.py:537
  25.0 5.8 %collective-permute-start.5 = (f32[8,8,128]{2,1,0:T(8,128)S(1)}, f32[8,8,128]{2,1,0:T(8,128)S(1)}, u32[]{:S(2)}, u32[]{:S(2)}) collective-permute-start(f32[8,8,128]{2,1,0:T(8,128)S(1)} %get-tuple-element.37.base), channel_id=1, source_target_pairs={{0,16},{16,0},{1,17},{17,1},{2,18},{18,2},{3,19},{19,3},{4,20},{20... | collective-permute-start | bytes 98312 | tf_op jit(solution)/shard_map/ppermute | solution.py:537
  26.8 3.1 %collective-permute-start.6 = (f32[8,512]{1,0:T(8,128)S(1)}, f32[8,512]{1,0:T(8,128)S(1)}, u32[]{:S(2)}, u32[]{:S(2)}) collective-permute-start(f32[8,512]{1,0:T(8,128)S(1)} %copy-done.1), channel_id=1, source_target_pairs={{0,1},{1,0},{2,3},{3,2},{4,5},{5,4},{6,7},{7,6},{8,9},{9,8},{10,11... | collective-permute-start | bytes 49160 | tf_op jit(solution)/shard_map/ppermute | solution.py:537
  43.7 10.5 %all-to-all-start.2 = ((f32[32,8,128]{2,1,0:T(8,128)}), f32[32,8,128]{2,1,0:T(8,128)S(1)}, u32[]{:S(2)}, u32[]{:S(2)}) async-start(f32[32,8,128]{2,1,0:T(8,128)} %inner_products.1), calls=%async_computation.2 | async-start | bytes 262144 | tf_op jit(solution)/shard_map/all_to_all | solution.py:666
  46.3 2.9 %collective-permute-start.7 = (f32[8,128]{1,0:T(8,128)S(1)}, f32[8,128]{1,0:T(8,128)S(1)}, u32[]{:S(2)}, u32[]{:S(2)}) collective-permute-start(f32[8,128]{1,0:T(8,128)S(1)} %get-tuple-element.43.mine), channel_id=1, source_target_pairs={{0,1},{1,0},{2,3},{3,2},{4,5},{5,4},{6,7},{7,6},{8,9},{9,8},{10,11... | collective-permute-start | bytes 12296 | tf_op jit(solution)/shard_map/ppermute | solution.py:537
  46.5 7.1 %collective-permute-start.8 = (f32[4,8,128]{2,1,0:T(8,128)S(1)}, f32[4,8,128]{2,1,0:T(8,128)S(1)}, u32[]{:S(2)}, u32[]{:S(2)}) collective-permute-start(f32[4,8,128]{2,1,0:T(8,128)S(1)} %get-tuple-element.52.for_partner), channel_id=1, source_target_pairs={{0,16},{16,0},{1,17},{17,1},{2,18},{18,2},{3,19},{19,3},{4,20},{20... | collective-permute-start | bytes 49160 | tf_op jit(solution)/shard_map/ppermute | solution.py:537
  51.2 2.3 %collective-permute-start.9 = (f32[4,8,128]{2,1,0:T(8,128)S(1)}, f32[4,8,128]{2,1,0:T(8,128)S(1)}, u32[]{:S(2)}, u32[]{:S(2)}) collective-permute-start(f32[4,8,128]{2,1,0:T(8,128)S(1)} %get-tuple-element.55), channel_id=1, source_target_pairs={{0,1},{1,0},{2,3},{3,2},{4,5},{5,4},{6,7},{7,6},{8,9},{9,8},{10,11... | collective-permute-start | bytes 49160 | tf_op jit(solution)/shard_map/ppermute | solution.py:537

commit v7 on v6

--- a/solution.py
+++ b/solution.py
@@ -226,28 +226,29 @@
             payload[n, 3 * tiles + t] = column_sum[(near + n) * tiles + t]
 
 
+def early_products(x, y, p):
+    basis = jnp.concatenate([x, y, p], axis=0)
+    outer = times_transpose(basis, basis, highest)
+    return jnp.concatenate(
+        [outer[0:8], outer[8:16, 8:24], outer[16:24, 16:24], jnp.zeros((8, LANES - 48), f32)], axis=1
+    )
+
+
+def lower_halves(previous):
+    return stacked_halves(jnp.concatenate([jnp.zeros_like(previous), 0.5 * previous], axis=0))
+
+
 def assemble_image_kernel(
-    own, base_partner, sums, column_sum, x_ref, x_partner, p_ref, payload, previous_halves
+    own, base_partner, sums, column_sum, x_partner, own_gram, payload, partner_halves
 ):
     tiles = own.shape[-1] // LANES
     near = payload.shape[0]
     partner = [base_partner[t] + sums[t] for t in range(tiles)]
-    basis = jnp.concatenate(
-        [
-            jnp.concatenate([x_ref[...], x_partner[...]], axis=1),
-            jnp.concatenate([own[...]] + partner, axis=1),
-            jnp.concatenate([p_ref[...]] + [base_partner[tiles + t] for t in range(tiles)], axis=1),
-        ],
-        axis=0,
-    )
-    for t in range(tiles):
-        for n, previous in enumerate((p_ref[:, lanes(t)], base_partner[tiles + t])):
-            previous_halves[n * tiles + t] = stacked_halves(
-                jnp.concatenate([jnp.zeros_like(previous), 0.5 * previous], axis=0)
-            )
-    outer = times_transpose(basis, basis, highest)
-    gram = jnp.concatenate(
-        [outer[0:8], outer[8:16, 8:24], outer[16:24, 16:24], jnp.zeros((8, LANES - 48), f32)], axis=1
+    previous = [base_partner[tiles + t] for t in range(tiles)]
+    for t in range(tiles):
+        partner_halves[t] = lower_halves(previous[t])
+    gram = own_gram[...] + early_products(
+        x_partner[...], jnp.concatenate(partner, axis=1), jnp.concatenate(previous, axis=1)
     )
     for n in range(near):
         for t in range(tiles):
@@ -361,7 +362,7 @@
 def transposed_image_kernel(
     paired, counts, rows, columns, held, own, base_other, sums_other, p_ref, p_other, diagonal,
     x_ref, q_ref,
-    column_sum, sum_halves, late, kept,
+    column_sum, sum_halves, late, kept, gram, own_halves,
     row_halves,
 ):
     refs = counts, rows, columns
@@ -397,6 +398,9 @@
 
     lax.fori_loop(0, kept.shape[0] // 8, keep, 0)
     y, p, q = own[...], p_ref[...], q_ref[...]
+    gram[...] = early_products(x_ref[...], y, p)
+    for t in range(tiles):
+        own_halves[t] = lower_halves(p[:, lanes(t)])
     rows = jnp.concatenate([x_ref[...], y, p], axis=0)
     terms = times_transpose(
         rows, jnp.concatenate([0.5 * q, 0.5 * diagonal[...] * y], axis=0), highest
@@ -418,7 +422,7 @@
     )
 
 
-def inner_kernel(parts, sum_halves, previous_halves, late, for_partner, spread):
+def inner_kernel(parts, sum_halves, own_halves, partner_halves, late, for_partner, spread):
     near = parts.shape[0]
     tiles = parts.shape[1] // 4
     left = [
@@ -434,7 +438,12 @@
     cross = times_transpose(
         jnp.concatenate(left, axis=1),
         jnp.concatenate(
-            [ref[j] for ref in (sum_halves, previous_halves) for j in range(ref.shape[0])], axis=1
+            [
+                ref[j]
+                for ref in (sum_halves, own_halves, partner_halves)
+                for j in range(ref.shape[0])
+            ],
+            axis=1,
         ),
     )
     terms = cross[0:8, 0:16] + cross[8:16, 0:16] + cross[0:8, 16:32]
@@ -618,7 +627,7 @@
     image = call(image_kernel, "image", shape(8, width), [base, first_received], [in_vmem] * 2)
     if not paired:
         base_other = lax.all_gather(image, "col", axis=0)
-    column_sum, sum_halves, late, kept = call(
+    column_sum, sum_halves, late, kept, own_gram, own_halves = call(
         functools.partial(transposed_image_kernel, paired),
         "transposed_image",
         [
@@ -626,6 +635,8 @@
             shape(column_tiles, 32, side, dtype=bf16),
             shape(8, LANES),
             shape(slots // 2, side, 2 * side, dtype=bf16),
+            shape(8, LANES),
+            shape(tiles, 32, side, dtype=bf16),
         ],
         [
             *places, held, image, base_other, first_received, previous, previous_other, diagonal,
@@ -635,15 +646,15 @@
         [pltpu.VMEM((row_tiles, 32, side), bf16)],
         micros=1.8,
     )
-    payload, previous_halves = call(
+    payload, partner_halves = call(
         assemble_image_kernel,
         "assemble_image",
         [
             shape(near, 4 * tiles + 1, 8, side),
-            shape(2 * tiles, 32, side, dtype=bf16),
+            shape(tiles, 32, side, dtype=bf16),
         ],
-        [image, base_partner, sums, column_sum, current, partner, previous],
-        [in_vmem] * 7,
+        [image, base_partner, sums, column_sum, partner, own_gram],
+        [in_vmem] * 6,
     )
     parts = to_near(payload)
     for_partner, gram = call(
@@ -658,11 +669,13 @@
         inner_kernel,
         "inner_products",
         shape(2 * near * n_col, 8, LANES),
-        [parts, sum_halves, previous_halves, late, for_partner],
-        [in_vmem] * 5,
+        [parts, sum_halves, own_halves, partner_halves, late, for_partner],
+        [in_vmem] * 6,
         micros=1.1,
     )
-    everyone = [list(range(2 * near * n_col))[::-1]]
+    everyone = [
+        [(h * near + n) * n_col + c for n in range(near)[::-1] for c in range(n_col) for h in range(2)]
+    ]
     inner_parts = lax.all_to_all(spread, devices, 0, 0, tiled=True, axis_index_groups=everyone)
     received = to_partner(for_partner)
     row_sum, rest, gram = call(

time: 55.6 us -> 55.4 us (level)
  waiting for transfers between devices: 4.56 us -> 3.89 us
  transfers between devices with their start and end apart: 11 -> 11, of which waited for: 4 -> 5; matrix products, arithmetic and copies ran while one was open for 0% -> 0% of each run, Pallas kernels for 14% -> 15%
where the time goes in v7:
time: 55.4 us; the launch traced here: 54.8 us
  blocking collectives  25.6 us (46%)
  starting transfers between devices  13.5 us (24%)
  Pallas kernels  10.4 us (19%)
  waiting for transfers between devices  3.89 us (7%)
  between operations  1.41 us (3%)
    all_to_all x2, blocking collectives, to_near(): lax.all_to_all(values, devices, 0, 0, tiled=True, axis_index_groups=groups)  25.6 us
    ppermute x10, starting transfers between devices, swap(): return lax.ppermute(values, axis, [(0, 1), (1, 0)])  11 us
    pallas_call x14, Pallas kernels, call(): pl.pallas_call(kernel, out_shape=out_shape, in_specs=specs, out_specs=jax...  10.4 us
    ppermute x10, waiting for transfers between devices, swap(): return lax.ppermute(values, axis, [(0, 1), (1, 0)])  3.5 us
    all_to_all x1, starting transfers between devices, local(): lax.all_to_all(spread, devices, 0, 0, tiled=True, axis_index_groups=every...  2.57 us
  transfers between devices with their start and end apart: 11, of which 5 were waited for; matrix products, arithmetic and copies ran while one was open for 0% of the time, Pallas kernels for 15%

profile of v7, /device:TPU:0, one launch (start us, length us, event | category | flops | bytes accessed | tf_op | source)
XLA Modules:
  0.0 54.8 jit_solution(6633977997596971583)
XLA Ops:
  0.6 0.0 copy-start
  0.6 0.5 collective-permute-start
  1.2 3.7 %collective-permute-start.1 = (f32[8,512]{1,0:T(8,128)}, f32[8,512]{1,0:T(8,128)S(1)}, u32[]{:S(2)}, u32[]{:S(2)}) collective-permute-start(f32[8,512]{1,0:T(8,128)} %x_ref.3), channel_id=1, source_target_pairs={{0,16},{16,0},{1,17},{17,1},{2,18},{18,2},{3,19},{19,3},{4,20},{20... | collective-permute-start | bytes 49160 | tf_op jit(solution)/shard_map/ppermute | solution.py:546
  5.5 0.0 collective-permute-done.refs_5_
  5.5 2.3 %transposed_current.1 = (s32[1,1]{1,0:T(1,128)S(4)}, s32[1,1,64]{2,1,0:T(1,128)S(4)}, s32[1,1,64]{2,1,0:T(1,128)S(4)}, f32[64,8,128]{2,1,0:T(8,128)S(1)}, bf16[64,128,256]{2,1,0:T(8,128)(2,1)S(1)}) custom-call(s32[1,1]{1,0:T(1,128)S(6)} %copy.12.refs_0_, s32[1,1,64]{2,1,0:T(1,128)} %refs_1_.1, s32[1,1,64]{2,1,0:T(1,128)} %refs_2_.1, ...), custom_call_target="tpu_custom_call" | custom-call | bytes 1 | tf_op jit(solution)/shard_map/transposed_current/pallas_call | solution.py:26
  7.8 0.0 copy-start.2
  7.9 0.0 copy-start.1
  7.9 0.0 copy-start.3
  7.9 0.0 collective-permute-done.1.partner.x_partner
  7.9 0.0 copy-done
  8.0 13.7 %all_to_all.15.parts = f32[8,16,8,128]{3,2,1,0:T(8,128)S(1)} all-to-all(f32[8,16,8,128]{3,2,1,0:T(8,128)S(1)} %assemble_current.1), channel_id=1, replica_groups={{0,2,4,6,8,10,12,14},{9,11,13,15,1,3,5,7},{16,18,20,22,24,26,28,30},{25..., dimensions={0} | all-to-all | bytes 1048576 | tf_op jit(solution)/shard_map/all_to_all | solution.py:559
  21.7 0.1 collective-permute-start.2
  21.8 0.7 %direct_current.1.row_sum = f32[8,8,128]{2,1,0:T(8,128)S(1)} custom-call(s32[1,1]{1,0:T(1,128)S(4)} %get-tuple-element.33.counts, s32[1,1,64]{2,1,0:T(1,128)S(4)} %get-tuple-element.34.rows, s32[1,1,64]{2,1,0:T(1,128)S(4)} %get-tuple-element.35.columns, bf16[64,128,256]{2,1,0:T(8,128)(2,1)S(1)} %get-tuple-element.37.held, f32[8,16,8,128]{3,2,1,0:T(8,128)S(1)} %all_to_all.15.parts), custom_call_target="tpu_custom_call" | custom-call | bytes 1 | tf_op jit(solution)/shard_map/direct_current/pallas_call | solution.py:26
  22.5 0.5 collective-permute-done.2.other_sums
  22.9 0.0 copy-done.2
  23.0 0.8 %collective-permute-start.3 = (f32[8,8,128]{2,1,0:T(8,128)S(1)}, f32[8,8,128]{2,1,0:T(8,128)S(1)}, u32[]{:S(2)}, u32[]{:S(2)}) collective-permute-start(f32[8,8,128]{2,1,0:T(8,128)S(1)} %get-tuple-element.38.mine), channel_id=1, source_target_pairs={{0,1},{1,0},{2,3},{3,2},{4,5},{5,4},{6,7},{7,6},{8,9},{9,8},{10,11... | collective-permute-start | bytes 98312 | tf_op jit(solution)/shard_map/ppermute | solution.py:546
  23.8 0.8 %collective-permute-start.4 = (f32[8,8,128]{2,1,0:T(8,128)S(1)}, f32[8,8,128]{2,1,0:T(8,128)S(1)}, u32[]{:S(2)}, u32[]{:S(2)}) collective-permute-start(f32[8,8,128]{2,1,0:T(8,128)S(1)} %get-tuple-element.40), channel_id=1, source_target_pairs={{0,16},{16,0},{1,17},{17,1},{2,18},{18,2},{3,19},{19,3},{4,20},{20... | collective-permute-start | bytes 98312 | tf_op jit(solution)/shard_map/ppermute | solution.py:546
  24.5 0.1 collective-permute-done.3.theirs
  24.6 0.0 copy-done.1
  24.6 2.1 %collective-permute-start.5 = (f32[8,8,128]{2,1,0:T(8,128)S(1)}, f32[8,8,128]{2,1,0:T(8,128)S(1)}, u32[]{:S(2)}, u32[]{:S(2)}) collective-permute-start(f32[8,8,128]{2,1,0:T(8,128)S(1)} %get-tuple-element.39.base), channel_id=1, source_target_pairs={{0,16},{16,0},{1,17},{17,1},{2,18},{18,2},{3,19},{19,3},{4,20},{20... | collective-permute-start | bytes 98312 | tf_op jit(solution)/shard_map/ppermute | solution.py:546
  26.8 0.0 collective-permute-start.6
  26.8 2.6 %collective-permute-done.4.received.sums_other = f32[8,8,128]{2,1,0:T(8,128)S(1)} collective-permute-done((f32[8,8,128]{2,1,0:T(8,128)S(1)}, f32[8,8,128]{2,1,0:T(8,128)S(1)}, u32[]{:S(2)}, u32[]{:S(2)}) %collective-permute-start.4) | collective-permute-done | bytes 32800 | tf_op jit(solution)/shard_map/ppermute | solution.py:546
  29.4 0.0 collective-permute-done.6.p_other
  29.4 0.0 copy-done.3
  29.4 1.0 %transposed_image.1 = (f32[64,16,128]{2,1,0:T(8,128)S(1)}, bf16[64,32,128]{2,1,0:T(8,128)(2,1)S(1)}, f32[8,128]{1,0:T(8,128)S(1)}, bf16[32,128,256]{2,1,0:T(8,12...) custom-call(s32[1,1]{1,0:T(1,128)S(4)} %get-tuple-element.33.counts, ...), custom_call_target="tpu_custom_call" | custom-call | bytes 1 | tf_op jit(solution)/shard_map/transposed_image/pallas_call | solution.py:26
  30.4 0.0 collective-permute-done.5.base_partner
  30.4 0.3 assemble_image.1
  30.7 11.8 %all_to_all.16.parts = f32[8,17,8,128]{3,2,1,0:T(8,128)S(1)} all-to-all(f32[8,17,8,128]{3,2,1,0:T(8,128)S(1)} %get-tuple-element.44), channel_id=1, replica_groups={{0,2,4,6,8,10,12,14},{9,11,13,15,1,3,5,7},{16,18,20,22,24,26,28,30},{25..., dimensions={0} | all-to-all | bytes 1114112 | tf_op jit(solution)/shard_map/all_to_all | solution.py:559
  42.5 1.1 %inner_products.1 = f32[32,8,128]{2,1,0:T(8,128)} custom-call(f32[8,17,8,128]{3,2,1,0:T(8,128)S(1)} %all_to_all.16.parts, bf16[64,32,128]{2,1,0:T(8,128)(2,1)S(1)} %get-tuple-element.52.sum_halves, bf16[4,32,128]{2,1,0:T(8,128)(2,1)S(1)} %get-tuple-element.53.own_halves, bf16[4,32,128]{2,1,0:T(8,128)(2,1)S(1)} %get-tuple-element.54.partner_halves, ...), custom_call_target="tpu_custom_call" | custom-call | bytes 1 | tf_op jit(solution)/shard_map/inner_products/pallas_call | solution.py:26
  43.6 2.6 %all-to-all-start.2 = ((f32[32,8,128]{2,1,0:T(8,128)}), f32[32,8,128]{2,1,0:T(8,128)S(1)}, u32[]{:S(2)}, u32[]{:S(2)}) async-start(f32[32,8,128]{2,1,0:T(8,128)} %inner_products.1), calls=%async_computation.2 | async-start | bytes 262144 | tf_op jit(solution)/shard_map/all_to_all | solution.py:679
  46.1 0.2 collective-permute-start.7
  46.3 2.7 %collective-permute-start.8 = (f32[4,8,128]{2,1,0:T(8,128)S(1)}, f32[4,8,128]{2,1,0:T(8,128)S(1)}, u32[]{:S(2)}, u32[]{:S(2)}) collective-permute-start(f32[4,8,128]{2,1,0:T(8,128)S(1)} %get-tuple-element.56.for_partner), channel_id=1, source_target_pairs={{0,16},{16,0},{1,17},{17,1},{2,18},{18,2},{3,19},{19,3},{4,20},{20... | collective-permute-start | bytes 49160 | tf_op jit(solution)/shard_map/ppermute | solution.py:546
  49.0 0.0 collective-permute-done.7.theirs
  49.0 2.0 %direct_image.1 = (f32[8,8,128]{2,1,0:T(8,128)S(1)}, f32[4,8,128]{2,1,0:T(8,128)S(1)}, f32[8,128]{1,0:T(8,128)S(1)}) custom-call(s32[1,1]{1,0:T(1,128)S(4)} %get-tuple-element.33.counts, s32[1,1,64]{2,1,0:T(1,128)S(4)} %get-tuple-element.34.rows, s32[1,1,64]{2,1,0:T(1,128)S(4)} %get-tuple-element.35.columns, f32[64,128,128]{2,1,0:T(8,128)} %bitcast.6, ...), custom_call_target="tpu_custom_call" | custom-call | bytes 1 | tf_op jit(solution)/shard_map/direct_image/pallas_call | solution.py:26
  51.1 0.1 collective-permute-start.9
  51.2 1.9 %eliminate.1 = (f32[8,8]{1,0:T(8,128)S(1)}, f32[24,24]{1,0:T(8,128)S(1)}, f32[24,24]{1,0:T(8,128)S(1)}, f32[8,512]{1,0:T(8,128)}, f32[8,512]{1,0:T(8,128)}) custom-call(f32[8,128]{1,0:T(8,128)S(1)} %get-tuple-element.47.gram, f32[8,512]{1,0:T(8,128)S(1)} %copy-done, f32[8,512]{1,0:T(8,128)S(1)} %image.1.own.y_ref), custom_call_target="tpu_custom_call" | custom-call | bytes 1 | tf_op jit(solution)/shard_map/eliminate/pallas_call | solution.py:26
  53.1 0.3 collective-permute-done.8.received
  53.4 0.0 collective-permute-done.9.theirs
  53.4 0.4 all-to-all-done.2.inner_parts
  53.8 1.0 %finish.1 = (f32[8,512]{1,0:T(8,128)}, f32[24,24]{1,0:T(8,128)}) custom-call(f32[24,24]{1,0:T(8,128)S(1)} %get-tuple-element.50.inverse, f32[24,24]{1,0:T(8,128)S(1)} %get-tuple-element.51.pencil, f32[32,8,128]{2,1,0:T(8,128)S(1)} %all-to-all-done.2.inner_parts, f32[8,8]{1,0:T(8,128)S(1)} %get-tuple-element.57.ritz, f32[8,512]{1,0:T(8,128)S(1)} %image.1.own.y_ref, ...), custom_call_target="tpu_custom_call" | custom-call | bytes 1 | tf_op jit(solution)/shard_map/finish/pallas_call | solution.py:26
  (6 shorter events, 0.1 us)
Async XLA Ops:
  0.6 7.3 %copy-start = (f32[8,512]{1,0:T(8,128)S(1)}, f32[8,512]{1,0:T(8,128)}, u32[]{:S(2)}) copy-start(f32[8,512]{1,0:T(8,128)} %x_ref.3) | copy-start | bytes 49156
  0.6 4.8 %collective-permute-start = (f32[8,512]{1,0:T(8,128)}, f32[8,512]{1,0:T(8,128)S(1)}, u32[]{:S(2)}, u32[]{:S(2)}) collective-permute-start(f32[8,512]{1,0:T(8,128)} %x_ref.3), channel_id=1, source_target_pairs={{0,1},{1,0},{2,3},{3,2},{4,5},{5,4},{6,7},{7,6},{8,9},{9,8},{10,11... | collective-permute-start | bytes 49160 | tf_op jit(solution)/shard_map/ppermute | solution.py:546
  1.2 6.7 %collective-permute-start.1 = (f32[8,512]{1,0:T(8,128)}, f32[8,512]{1,0:T(8,128)S(1)}, u32[]{:S(2)}, u32[]{:S(2)}) collective-permute-start(f32[8,512]{1,0:T(8,128)} %x_ref.3), channel_id=1, source_target_pairs={{0,16},{16,0},{1,17},{17,1},{2,18},{18,2},{3,19},{19,3},{4,20},{20... | collective-permute-start | bytes 49160 | tf_op jit(solution)/shard_map/ppermute | solution.py:546
  7.8 15.1 %copy-start.2 = (f32[512]{0:T(512)S(1)}, f32[512]{0:T(512)}, u32[]{:S(2)}) copy-start(f32[512]{0:T(512)} %param.12) | copy-start | bytes 6148
  7.9 16.8 %copy-start.1 = (f32[8,512]{1,0:T(8,128)S(1)}, f32[8,512]{1,0:T(8,128)}, u32[]{:S(2)}) copy-start(f32[8,512]{1,0:T(8,128)} %p_ref.1) | copy-start | bytes 49156
  7.9 21.5 %copy-start.3 = (f32[8,512]{1,0:T(8,128)S(1)}, f32[8,512]{1,0:T(8,128)}, u32[]{:S(2)}) copy-start(f32[8,512]{1,0:T(8,128)} %q_ref.1) | copy-start | bytes 49156
  21.7 1.2 %collective-permute-start.2 = (f32[4,8,128]{2,1,0:T(8,128)S(1)}, f32[4,8,128]{2,1,0:T(8,128)S(1)}, u32[]{:S(2)}, u32[]{:S(2)}) collective-permute-start(f32[4,8,128]{2,1,0:T(8,128)S(1)} %partner_sums.2.sums), channel_id=1, source_target_pairs={{0,1},{1,0},{2,3},{3,2},{4,5},{5,4},{6,7},{7,6},{8,9},{9,8},{10,11... | collective-permute-start | bytes 49160 | tf_op jit(solution)/shard_map/ppermute | solution.py:546
  23.0 1.6 %collective-permute-start.3 = (f32[8,8,128]{2,1,0:T(8,128)S(1)}, f32[8,8,128]{2,1,0:T(8,128)S(1)}, u32[]{:S(2)}, u32[]{:S(2)}) collective-permute-start(f32[8,8,128]{2,1,0:T(8,128)S(1)} %get-tuple-element.38.mine), channel_id=1, source_target_pairs={{0,1},{1,0},{2,3},{3,2},{4,5},{5,4},{6,7},{7,6},{8,9},{9,8},{10,11... | collective-permute-start | bytes 98312 | tf_op jit(solution)/shard_map/ppermute | solution.py:546
  23.8 5.6 %collective-permute-start.4 = (f32[8,8,128]{2,1,0:T(8,128)S(1)}, f32[8,8,128]{2,1,0:T(8,128)S(1)}, u32[]{:S(2)}, u32[]{:S(2)}) collective-permute-start(f32[8,8,128]{2,1,0:T(8,128)S(1)} %get-tuple-element.40), channel_id=1, source_target_pairs={{0,16},{16,0},{1,17},{17,1},{2,18},{18,2},{3,19},{19,3},{4,20},{20... | collective-permute-start | bytes 98312 | tf_op jit(solution)/shard_map/ppermute | solution.py:546
  24.6 5.8 %collective-permute-start.5 = (f32[8,8,128]{2,1,0:T(8,128)S(1)}, f32[8,8,128]{2,1,0:T(8,128)S(1)}, u32[]{:S(2)}, u32[]{:S(2)}) collective-permute-start(f32[8,8,128]{2,1,0:T(8,128)S(1)} %get-tuple-element.39.base), channel_id=1, source_target_pairs={{0,16},{16,0},{1,17},{17,1},{2,18},{18,2},{3,19},{19,3},{4,20},{20... | collective-permute-start | bytes 98312 | tf_op jit(solution)/shard_map/ppermute | solution.py:546
  26.8 2.6 %collective-permute-start.6 = (f32[8,512]{1,0:T(8,128)S(1)}, f32[8,512]{1,0:T(8,128)S(1)}, u32[]{:S(2)}, u32[]{:S(2)}) collective-permute-start(f32[8,512]{1,0:T(8,128)S(1)} %copy-done.1), channel_id=1, source_target_pairs={{0,1},{1,0},{2,3},{3,2},{4,5},{5,4},{6,7},{7,6},{8,9},{9,8},{10,11... | collective-permute-start | bytes 49160 | tf_op jit(solution)/shard_map/ppermute | solution.py:546
  43.6 10.2 %all-to-all-start.2 = ((f32[32,8,128]{2,1,0:T(8,128)}), f32[32,8,128]{2,1,0:T(8,128)S(1)}, u32[]{:S(2)}, u32[]{:S(2)}) async-start(f32[32,8,128]{2,1,0:T(8,128)} %inner_products.1), calls=%async_computation.2 | async-start | bytes 262144 | tf_op jit(solution)/shard_map/all_to_all | solution.py:679
  46.1 2.9 %collective-permute-start.7 = (f32[8,128]{1,0:T(8,128)S(1)}, f32[8,128]{1,0:T(8,128)S(1)}, u32[]{:S(2)}, u32[]{:S(2)}) collective-permute-start(f32[8,128]{1,0:T(8,128)S(1)} %get-tuple-element.46.mine), channel_id=1, source_target_pairs={{0,1},{1,0},{2,3},{3,2},{4,5},{5,4},{6,7},{7,6},{8,9},{9,8},{10,11... | collective-permute-start | bytes 12296 | tf_op jit(solution)/shard_map/ppermute | solution.py:546
  46.3 7.1 %collective-permute-start.8 = (f32[4,8,128]{2,1,0:T(8,128)S(1)}, f32[4,8,128]{2,1,0:T(8,128)S(1)}, u32[]{:S(2)}, u32[]{:S(2)}) collective-permute-start(f32[4,8,128]{2,1,0:T(8,128)S(1)} %get-tuple-element.56.for_partner), channel_id=1, source_target_pairs={{0,16},{16,0},{1,17},{17,1},{2,18},{18,2},{3,19},{19,3},{4,20},{20... | collective-permute-start | bytes 49160 | tf_op jit(solution)/shard_map/ppermute | solution.py:546
  51.1 2.3 %collective-permute-start.9 = (f32[4,8,128]{2,1,0:T(8,128)S(1)}, f32[4,8,128]{2,1,0:T(8,128)S(1)}, u32[]{:S(2)}, u32[]{:S(2)}) collective-permute-start(f32[4,8,128]{2,1,0:T(8,128)S(1)} %get-tuple-element.59), channel_id=1, source_target_pairs={{0,1},{1,0},{2,3},{3,2},{4,5},{5,4},{6,7},{7,6},{8,9},{9,8},{10,11... | collective-permute-start | bytes 49160 | tf_op jit(solution)/shard_map/ppermute | solution.py:546

commit v8 on v7

--- a/solution.py
+++ b/solution.py
@@ -331,7 +331,9 @@
     )
 
 
-def combine_kernel(paired, parts, row_sum, diagonal, vectors, sums, other_sums, mine, shipped, *rows):
+def combine_kernel(
+    paired, parts, row_sum, diagonal, vectors, sums, other_sums, previous, mine, shipped, *rows
+):
     tiles = parts.shape[1] // 4
     for t in range(tiles):
         shipped[t] = sums[t]
@@ -340,6 +342,7 @@
         if paired:
             mine[t] = total + row_sum[t]
             mine[tiles + t] = row_sum[tiles + t]
+            mine[2 * tiles + t] = previous[:, lanes(t)]
         else:
             mine[:, lanes(t)] = total
             for c in range(rows[0].shape[0]):
@@ -374,6 +377,7 @@
         other = base_other[...] + jnp.concatenate(
             [sums_other[tiles + t] for t in range(tiles)], axis=1
         )
+        p_other = jnp.concatenate([p_other[2 * tiles + t] for t in range(tiles)], axis=1)
     for t in range(tiles):
         for (c, values), (_, previous) in zip(
             row_block_tiles(t, own, other, paired), row_block_tiles(t, p_ref, p_other, paired)
@@ -601,17 +605,17 @@
         call,
         functools.partial(combine_kernel, paired),
         "combine",
-        operands=[parts, row_sum, diagonal, current, sums, other_sums],
-        specs=[in_vmem] * 6,
+        operands=[parts, row_sum, diagonal, current, sums, other_sums, previous],
+        specs=[in_vmem] * 7,
     )
     if paired:
-        previous_other = swap(previous)
-        mine, shipped = combine(out_shape=[shape(2 * tiles, 8, side)] * 2)
+        mine, shipped = combine(out_shape=[shape(3 * tiles, 8, side), shape(2 * tiles, 8, side)])
+        theirs = previous_other = swap(mine)
         base, base_other = call(
             base_kernel,
             "base",
             [shape(2 * tiles, 8, side), shape(8, width)],
-            [mine, swap(mine), previous],
+            [mine, theirs, previous],
             [in_vmem] * 3,
         )
     else:

time: 55.4 us -> 55.5 us (level)
  Pallas kernels: 10.4 us -> 12.1 us
  starting transfers between devices: 13.5 us -> 12.7 us
    pallas_call x14, Pallas kernels: 10.4 us -> 12.1 us  [call(): pl.pallas_call(kernel, out_shape=out_shape, in_specs=specs, out_specs=jax...]
    ppermute x10 -> x9, starting transfers between devices: 11 us -> 10.2 us  [swap(): return lax.ppermute(values, axis, [(0, 1), (1, 0)])]
    ppermute x10 -> x9, waiting for transfers between devices: 3.5 us -> 3.42 us  [swap(): return lax.ppermute(values, axis, [(0, 1), (1, 0)])]
  transfers between devices with their start and end apart: 11 -> 10, of which waited for: 5 -> 4; matrix products, arithmetic and copies ran while one was open for 0% -> 0% of each run, Pallas kernels for 15% -> 17%
where the time goes in v8:
time: 55.5 us; the launch traced here: 55.2 us
  blocking collectives  25.2 us (45%)
  starting transfers between devices  12.7 us (23%)
  Pallas kernels  12.1 us (22%)
  waiting for transfers between devices  3.8 us (7%)
  between operations  1.43 us (3%)
    all_to_all x2, blocking collectives, to_near(): lax.all_to_all(values, devices, 0, 0, tiled=True, axis_index_groups=groups)  25.2 us
    pallas_call x14, Pallas kernels, call(): pl.pallas_call(kernel, out_shape=out_shape, in_specs=specs, out_specs=jax...  12.1 us
    ppermute x9, starting transfers between devices, swap(): return lax.ppermute(values, axis, [(0, 1), (1, 0)])  10.2 us
    ppermute x9, waiting for transfers between devices, swap(): return lax.ppermute(values, axis, [(0, 1), (1, 0)])  3.42 us
    all_to_all x1, starting transfers between devices, local(): lax.all_to_all(spread, devices, 0, 0, tiled=True, axis_index_groups=every...  2.56 us
  transfers between devices with their start and end apart: 10, of which 4 were waited for; matrix products, arithmetic and copies ran while one was open for 0% of the time, Pallas kernels for 17%

profile of v8, /device:TPU:0, one launch (start us, length us, event | category | flops | bytes accessed | tf_op | source)
XLA Modules:
  0.0 55.2 jit_solution(16037026959777983945)
XLA Ops:
  0.6 0.0 copy-start
  0.6 0.5 collective-permute-start
  1.2 3.7 %collective-permute-start.1 = (f32[8,512]{1,0:T(8,128)}, f32[8,512]{1,0:T(8,128)S(1)}, u32[]{:S(2)}, u32[]{:S(2)}) collective-permute-start(f32[8,512]{1,0:T(8,128)} %x_ref.3), channel_id=1, source_target_pairs={{0,16},{16,0},{1,17},{17,1},{2,18},{18,2},{3,19},{19,3},{4,20},{20... | collective-permute-start | bytes 49160 | tf_op jit(solution)/shard_map/ppermute | solution.py:550
  5.5 0.0 collective-permute-done.refs_5_
  5.5 2.9 %transposed_current.1 = (s32[1,1]{1,0:T(1,128)S(4)}, s32[1,1,64]{2,1,0:T(1,128)S(4)}, s32[1,1,64]{2,1,0:T(1,128)S(4)}, f32[64,8,128]{2,1,0:T(8,128)S(1)}, bf16[64,128,256]{2,1,0:T(8,128)(2,1)S(1)}) custom-call(s32[1,1]{1,0:T(1,128)S(6)} %copy.12.refs_0_, s32[1,1,64]{2,1,0:T(1,128)} %refs_1_.1, s32[1,1,64]{2,1,0:T(1,128)} %refs_2_.1, ...), custom_call_target="tpu_custom_call" | custom-call | bytes 1 | tf_op jit(solution)/shard_map/transposed_current/pallas_call | solution.py:26
  8.4 0.0 copy-start.1
  8.4 0.0 copy-start.2
  8.4 0.0 copy-start.3
  8.4 0.0 collective-permute-done.1.partner.x_partner
  8.4 0.0 copy-done
  8.5 13.6 %all_to_all.15.parts = f32[8,16,8,128]{3,2,1,0:T(8,128)S(1)} all-to-all(f32[8,16,8,128]{3,2,1,0:T(8,128)S(1)} %assemble_current.1), channel_id=1, replica_groups={{0,2,4,6,8,10,12,14},{9,11,13,15,1,3,5,7},{16,18,20,22,24,26,28,30},{25..., dimensions={0} | all-to-all | bytes 1048576 | tf_op jit(solution)/shard_map/all_to_all | solution.py:563
  22.1 0.1 collective-permute-start.2
  22.2 1.4 %direct_current.1.row_sum = f32[8,8,128]{2,1,0:T(8,128)S(1)} custom-call(s32[1,1]{1,0:T(1,128)S(4)} %get-tuple-element.33.counts, s32[1,1,64]{2,1,0:T(1,128)S(4)} %get-tuple-element.34.rows, s32[1,1,64]{2,1,0:T(1,128)S(4)} %get-tuple-element.35.columns, bf16[64,128,256]{2,1,0:T(8,128)(2,1)S(1)} %get-tuple-element.37.held, f32[8,16,8,128]{3,2,1,0:T(8,128)S(1)} %all_to_all.15.parts), custom_call_target="tpu_custom_call" | custom-call | bytes 1 | tf_op jit(solution)/shard_map/direct_current/pallas_call | solution.py:26
  23.6 0.0 collective-permute-done.2.other_sums
  23.6 0.0 copy-done.1
  23.6 0.0 copy-done.2
  23.6 0.1 collective-permute-start.3
  23.7 1.0 %collective-permute-start.4 = (f32[8,8,128]{2,1,0:T(8,128)S(1)}, f32[8,8,128]{2,1,0:T(8,128)S(1)}, u32[]{:S(2)}, u32[]{:S(2)}) collective-permute-start(f32[8,8,128]{2,1,0:T(8,128)S(1)} %get-tuple-element.40), channel_id=1, source_target_pairs={{0,16},{16,0},{1,17},{17,1},{2,18},{18,2},{3,19},{19,3},{4,20},{20... | collective-permute-start | bytes 98312 | tf_op jit(solution)/shard_map/ppermute | solution.py:550
  24.7 0.2 collective-permute-done.3.theirs.p_other
  25.0 1.8 %collective-permute-start.5 = (f32[8,8,128]{2,1,0:T(8,128)S(1)}, f32[8,8,128]{2,1,0:T(8,128)S(1)}, u32[]{:S(2)}, u32[]{:S(2)}) collective-permute-start(f32[8,8,128]{2,1,0:T(8,128)S(1)} %get-tuple-element.39.base), channel_id=1, source_target_pairs={{0,16},{16,0},{1,17},{17,1},{2,18},{18,2},{3,19},{19,3},{4,20},{20... | collective-permute-start | bytes 98312 | tf_op jit(solution)/shard_map/ppermute | solution.py:550
  26.8 2.9 %collective-permute-done.4.received.sums_other = f32[8,8,128]{2,1,0:T(8,128)S(1)} collective-permute-done((f32[8,8,128]{2,1,0:T(8,128)S(1)}, f32[8,8,128]{2,1,0:T(8,128)S(1)}, u32[]{:S(2)}, u32[]{:S(2)}) %collective-permute-start.4) | collective-permute-done | bytes 32800 | tf_op jit(solution)/shard_map/ppermute | solution.py:550
  29.7 0.0 copy-done.3
  29.7 1.4 %transposed_image.1 = (f32[64,16,128]{2,1,0:T(8,128)S(1)}, bf16[64,32,128]{2,1,0:T(8,128)(2,1)S(1)}, f32[8,128]{1,0:T(8,128)S(1)}, bf16[32,128,256]{2,1,0:T(8,12...) custom-call(s32[1,1]{1,0:T(1,128)S(4)} %get-tuple-element.33.counts, ...), custom_call_target="tpu_custom_call" | custom-call | bytes 1 | tf_op jit(solution)/shard_map/transposed_image/pallas_call | solution.py:26
  31.1 0.0 collective-permute-done.5.base_partner
  31.1 0.3 assemble_image.1
  31.3 11.5 %all_to_all.16.parts = f32[8,17,8,128]{3,2,1,0:T(8,128)S(1)} all-to-all(f32[8,17,8,128]{3,2,1,0:T(8,128)S(1)} %get-tuple-element.44), channel_id=1, replica_groups={{0,2,4,6,8,10,12,14},{9,11,13,15,1,3,5,7},{16,18,20,22,24,26,28,30},{25..., dimensions={0} | all-to-all | bytes 1114112 | tf_op jit(solution)/shard_map/all_to_all | solution.py:563
  42.9 1.1 %inner_products.1 = f32[32,8,128]{2,1,0:T(8,128)} custom-call(f32[8,17,8,128]{3,2,1,0:T(8,128)S(1)} %all_to_all.16.parts, bf16[64,32,128]{2,1,0:T(8,128)(2,1)S(1)} %get-tuple-element.52.sum_halves, bf16[4,32,128]{2,1,0:T(8,128)(2,1)S(1)} %get-tuple-element.53.own_halves, bf16[4,32,128]{2,1,0:T(8,128)(2,1)S(1)} %get-tuple-element.54.partner_halves, ...), custom_call_target="tpu_custom_call" | custom-call | bytes 1 | tf_op jit(solution)/shard_map/inner_products/pallas_call | solution.py:26
  44.0 2.6 %all-to-all-start.2 = ((f32[32,8,128]{2,1,0:T(8,128)}), f32[32,8,128]{2,1,0:T(8,128)S(1)}, u32[]{:S(2)}, u32[]{:S(2)}) async-start(f32[32,8,128]{2,1,0:T(8,128)} %inner_products.1), calls=%async_computation.2 | async-start | bytes 262144 | tf_op jit(solution)/shard_map/all_to_all | solution.py:683
  46.6 0.2 collective-permute-start.6
  46.7 2.7 %collective-permute-start.7 = (f32[4,8,128]{2,1,0:T(8,128)S(1)}, f32[4,8,128]{2,1,0:T(8,128)S(1)}, u32[]{:S(2)}, u32[]{:S(2)}) collective-permute-start(f32[4,8,128]{2,1,0:T(8,128)S(1)} %get-tuple-element.56.for_partner), channel_id=1, source_target_pairs={{0,16},{16,0},{1,17},{17,1},{2,18},{18,2},{3,19},{19,3},{4,20},{20... | collective-permute-start | bytes 49160 | tf_op jit(solution)/shard_map/ppermute | solution.py:550
  49.4 0.0 collective-permute-done.6.theirs
  49.4 2.1 %direct_image.1 = (f32[8,8,128]{2,1,0:T(8,128)S(1)}, f32[4,8,128]{2,1,0:T(8,128)S(1)}, f32[8,128]{1,0:T(8,128)S(1)}) custom-call(s32[1,1]{1,0:T(1,128)S(4)} %get-tuple-element.33.counts, s32[1,1,64]{2,1,0:T(1,128)S(4)} %get-tuple-element.34.rows, s32[1,1,64]{2,1,0:T(1,128)S(4)} %get-tuple-element.35.columns, f32[64,128,128]{2,1,0:T(8,128)} %bitcast.6, ...), custom_call_target="tpu_custom_call" | custom-call | bytes 1 | tf_op jit(solution)/shard_map/direct_image/pallas_call | solution.py:26
  51.5 0.1 collective-permute-start.8
  51.6 1.9 %eliminate.1 = (f32[8,8]{1,0:T(8,128)S(1)}, f32[24,24]{1,0:T(8,128)S(1)}, f32[24,24]{1,0:T(8,128)S(1)}, f32[8,512]{1,0:T(8,128)}, f32[8,512]{1,0:T(8,128)}) custom-call(f32[8,128]{1,0:T(8,128)S(1)} %get-tuple-element.47.gram, f32[8,512]{1,0:T(8,128)S(1)} %copy-done, f32[8,512]{1,0:T(8,128)S(1)} %image.1.own.y_ref), custom_call_target="tpu_custom_call" | custom-call | bytes 1 | tf_op jit(solution)/shard_map/eliminate/pallas_call | solution.py:26
  53.5 0.3 collective-permute-done.7.received
  53.8 0.0 collective-permute-done.8.theirs
  53.8 0.4 all-to-all-done.2.inner_parts
  54.2 1.0 %finish.1 = (f32[8,512]{1,0:T(8,128)}, f32[24,24]{1,0:T(8,128)}) custom-call(f32[24,24]{1,0:T(8,128)S(1)} %get-tuple-element.50.inverse, f32[24,24]{1,0:T(8,128)S(1)} %get-tuple-element.51.pencil, f32[32,8,128]{2,1,0:T(8,128)S(1)} %all-to-all-done.2.inner_parts, f32[8,8]{1,0:T(8,128)S(1)} %get-tuple-element.57.ritz, f32[8,512]{1,0:T(8,128)S(1)} %image.1.own.y_ref, ...), custom_call_target="tpu_custom_call" | custom-call | bytes 1 | tf_op jit(solution)/shard_map/finish/pallas_call | solution.py:26
  (6 shorter events, 0.1 us)
Async XLA Ops:
  0.6 7.8 %copy-start = (f32[8,512]{1,0:T(8,128)S(1)}, f32[8,512]{1,0:T(8,128)}, u32[]{:S(2)}) copy-start(f32[8,512]{1,0:T(8,128)} %x_ref.3) | copy-start | bytes 49156
  0.6 4.8 %collective-permute-start = (f32[8,512]{1,0:T(8,128)}, f32[8,512]{1,0:T(8,128)S(1)}, u32[]{:S(2)}, u32[]{:S(2)}) collective-permute-start(f32[8,512]{1,0:T(8,128)} %x_ref.3), channel_id=1, source_target_pairs={{0,1},{1,0},{2,3},{3,2},{4,5},{5,4},{6,7},{7,6},{8,9},{9,8},{10,11... | collective-permute-start | bytes 49160 | tf_op jit(solution)/shard_map/ppermute | solution.py:550
  1.2 7.3 %collective-permute-start.1 = (f32[8,512]{1,0:T(8,128)}, f32[8,512]{1,0:T(8,128)S(1)}, u32[]{:S(2)}, u32[]{:S(2)}) collective-permute-start(f32[8,512]{1,0:T(8,128)} %x_ref.3), channel_id=1, source_target_pairs={{0,16},{16,0},{1,17},{17,1},{2,18},{18,2},{3,19},{19,3},{4,20},{20... | collective-permute-start | bytes 49160 | tf_op jit(solution)/shard_map/ppermute | solution.py:550
  8.4 15.2 %copy-start.1 = (f32[8,512]{1,0:T(8,128)S(1)}, f32[8,512]{1,0:T(8,128)}, u32[]{:S(2)}) copy-start(f32[8,512]{1,0:T(8,128)} %p_ref.1) | copy-start | bytes 49156
  8.4 15.2 %copy-start.2 = (f32[512]{0:T(512)S(1)}, f32[512]{0:T(512)}, u32[]{:S(2)}) copy-start(f32[512]{0:T(512)} %param.12) | copy-start | bytes 6148
  8.4 21.3 %copy-start.3 = (f32[8,512]{1,0:T(8,128)S(1)}, f32[8,512]{1,0:T(8,128)}, u32[]{:S(2)}) copy-start(f32[8,512]{1,0:T(8,128)} %q_ref.1) | copy-start | bytes 49156
  22.1 1.4 %collective-permute-start.2 = (f32[4,8,128]{2,1,0:T(8,128)S(1)}, f32[4,8,128]{2,1,0:T(8,128)S(1)}, u32[]{:S(2)}, u32[]{:S(2)}) collective-permute-start(f32[4,8,128]{2,1,0:T(8,128)S(1)} %partner_sums.2.sums), channel_id=1, source_target_pairs={{0,1},{1,0},{2,3},{3,2},{4,5},{5,4},{6,7},{7,6},{8,9},{9,8},{10,11... | collective-permute-start | bytes 49160 | tf_op jit(solution)/shard_map/ppermute | solution.py:550
  23.6 1.3 %collective-permute-start.3 = (f32[12,8,128]{2,1,0:T(8,128)S(1)}, f32[12,8,128]{2,1,0:T(8,128)S(1)}, u32[]{:S(2)}, u32[]{:S(2)}) collective-permute-start(f32[12,8,128]{2,1,0:T(8,128)S(1)} %get-tuple-element.38.mine), channel_id=1, source_target_pairs={{0,1},{1,0},{2,3},{3,2},{4,5},{5,4},{6,7},{7,6},{8,9},{9,8},{10,11... | collective-permute-start | bytes 147464 | tf_op jit(solution)/shard_map/ppermute | solution.py:550
  23.7 5.9 %collective-permute-start.4 = (f32[8,8,128]{2,1,0:T(8,128)S(1)}, f32[8,8,128]{2,1,0:T(8,128)S(1)}, u32[]{:S(2)}, u32[]{:S(2)}) collective-permute-start(f32[8,8,128]{2,1,0:T(8,128)S(1)} %get-tuple-element.40), channel_id=1, source_target_pairs={{0,16},{16,0},{1,17},{17,1},{2,18},{18,2},{3,19},{19,3},{4,20},{20... | collective-permute-start | bytes 98312 | tf_op jit(solution)/shard_map/ppermute | solution.py:550
  25.0 6.1 %collective-permute-start.5 = (f32[8,8,128]{2,1,0:T(8,128)S(1)}, f32[8,8,128]{2,1,0:T(8,128)S(1)}, u32[]{:S(2)}, u32[]{:S(2)}) collective-permute-start(f32[8,8,128]{2,1,0:T(8,128)S(1)} %get-tuple-element.39.base), channel_id=1, source_target_pairs={{0,16},{16,0},{1,17},{17,1},{2,18},{18,2},{3,19},{19,3},{4,20},{20... | collective-permute-start | bytes 98312 | tf_op jit(solution)/shard_map/ppermute | solution.py:550
  44.0 10.2 %all-to-all-start.2 = ((f32[32,8,128]{2,1,0:T(8,128)}), f32[32,8,128]{2,1,0:T(8,128)S(1)}, u32[]{:S(2)}, u32[]{:S(2)}) async-start(f32[32,8,128]{2,1,0:T(8,128)} %inner_products.1), calls=%async_computation.2 | async-start | bytes 262144 | tf_op jit(solution)/shard_map/all_to_all | solution.py:683
  46.6 2.9 %collective-permute-start.6 = (f32[8,128]{1,0:T(8,128)S(1)}, f32[8,128]{1,0:T(8,128)S(1)}, u32[]{:S(2)}, u32[]{:S(2)}) collective-permute-start(f32[8,128]{1,0:T(8,128)S(1)} %get-tuple-element.46.mine), channel_id=1, source_target_pairs={{0,1},{1,0},{2,3},{3,2},{4,5},{5,4},{6,7},{7,6},{8,9},{9,8},{10,11... | collective-permute-start | bytes 12296 | tf_op jit(solution)/shard_map/ppermute | solution.py:550
  46.7 7.1 %collective-permute-start.7 = (f32[4,8,128]{2,1,0:T(8,128)S(1)}, f32[4,8,128]{2,1,0:T(8,128)S(1)}, u32[]{:S(2)}, u32[]{:S(2)}) collective-permute-start(f32[4,8,128]{2,1,0:T(8,128)S(1)} %get-tuple-element.56.for_partner), channel_id=1, source_target_pairs={{0,16},{16,0},{1,17},{17,1},{2,18},{18,2},{3,19},{19,3},{4,20},{20... | collective-permute-start | bytes 49160 | tf_op jit(solution)/shard_map/ppermute | solution.py:550
  51.5 2.3 %collective-permute-start.8 = (f32[4,8,128]{2,1,0:T(8,128)S(1)}, f32[4,8,128]{2,1,0:T(8,128)S(1)}, u32[]{:S(2)}, u32[]{:S(2)}) collective-permute-start(f32[4,8,128]{2,1,0:T(8,128)S(1)} %get-tuple-element.59), channel_id=1, source_target_pairs={{0,1},{1,0},{2,3},{3,2},{4,5},{5,4},{6,7},{7,6},{8,9},{9,8},{10,11... | collective-permute-start | bytes 49160 | tf_op jit(solution)/shard_map/ppermute | solution.py:550

commit v9 on v8

--- a/solution.py
+++ b/solution.py
@@ -91,7 +91,7 @@
         self.reach = (self.live + loop_step - 1) // loop_step * loop_step
         here = lax.axis_index("col")
         self.row_mask = here * tiles if paired else 0
-        self.column_mask = lax.axis_index("half") * (column_tiles // 2) + lax.rem(here, 2) * (
+        self.column_mask = lax.axis_index("half") * (column_tiles // 2) + lax.rem(here + 1, 2) * (
             column_tiles // 4
         )
 
@@ -556,7 +556,7 @@
 
     def to_near(values):
         groups = [
-            [(h * near + (p + c % 2 * (near // 2)) % near) * n_col + c for p in range(near)]
+            [(h * near + (p + (c + 1) % 2 * (near // 2)) % near) * n_col + c for p in range(near)]
             for h in range(2)
             for c in range(n_col)
         ]

time: 55.5 us -> 56.1 us (1.011)
  Pallas kernels: 12.1 us -> 10.4 us
  blocking collectives: 25.2 us -> 26.2 us
  starting transfers between devices: 12.7 us -> 13.6 us
    pallas_call x14, Pallas kernels: 12.1 us -> 10.4 us  [call(): pl.pallas_call(kernel, out_shape=out_shape, in_specs=specs, out_specs=jax...]
    all_to_all x2, blocking collectives: 25.2 us -> 26.2 us  [to_near(): lax.all_to_all(values, devices, 0, 0, tiled=True, axis_index_groups=groups)]
    ppermute x9, starting transfers between devices: 10.2 us -> 11 us  [swap(): return lax.ppermute(values, axis, [(0, 1), (1, 0)])]
  transfers between devices with their start and end apart: 10 -> 10, of which waited for: 4 -> 4; matrix products, arithmetic and copies ran while one was open for 0% -> 0% of each run, Pallas kernels for 17% -> 14%
where the time goes in v9:
time: 56.1 us; the launch traced here: 56 us
  blocking collectives  26.2 us (47%)
  starting transfers between devices  13.6 us (24%)
  Pallas kernels  10.4 us (19%)
  waiting for transfers between devices  4.36 us (8%)
  between operations  1.4 us (2%)
    all_to_all x2, blocking collectives, to_near(): lax.all_to_all(values, devices, 0, 0, tiled=True, axis_index_groups=groups)  26.2 us
    ppermute x9, starting transfers between devices, swap(): return lax.ppermute(values, axis, [(0, 1), (1, 0)])  11 us
    pallas_call x14, Pallas kernels, call(): pl.pallas_call(kernel, out_shape=out_shape, in_specs=specs, out_specs=jax...  10.4 us
    ppermute x9, waiting for transfers between devices, swap(): return lax.ppermute(values, axis, [(0, 1), (1, 0)])  3.97 us
    all_to_all x1, starting transfers between devices, local(): lax.all_to_all(spread, devices, 0, 0, tiled=True, axis_index_groups=every...  2.56 us
  transfers between devices with their start and end apart: 10, of which 4 were waited for; matrix products, arithmetic and copies ran while one was open for 0% of the time, Pallas kernels for 14%

profile of v9, /device:TPU:0, one launch (start us, length us, event | category | flops | bytes accessed | tf_op | source)
XLA Modules:
  0.0 56.0 jit_solution(9832446742662623382)
XLA Ops:
  0.6 0.0 copy-start
  0.6 0.5 collective-permute-start
  1.2 3.7 %collective-permute-start.1 = (f32[8,512]{1,0:T(8,128)}, f32[8,512]{1,0:T(8,128)S(1)}, u32[]{:S(2)}, u32[]{:S(2)}) collective-permute-start(f32[8,512]{1,0:T(8,128)} %x_ref.3), channel_id=1, source_target_pairs={{0,16},{16,0},{1,17},{17,1},{2,18},{18,2},{3,19},{19,3},{4,20},{20... | collective-permute-start | bytes 49160 | tf_op jit(solution)/shard_map/ppermute | solution.py:550
  5.5 0.0 collective-permute-done.refs_5_
  5.5 2.3 %transposed_current.1 = (s32[1,1]{1,0:T(1,128)S(4)}, s32[1,1,64]{2,1,0:T(1,128)S(4)}, s32[1,1,64]{2,1,0:T(1,128)S(4)}, f32[64,8,128]{2,1,0:T(8,128)S(1)}, bf16[64,128,256]{2,1,0:T(8,128)(2,1)S(1)}) custom-call(s32[1,1]{1,0:T(1,128)S(6)} %copy.12.refs_0_, s32[1,1,64]{2,1,0:T(1,128)} %refs_1_.1, s32[1,1,64]{2,1,0:T(1,128)} %refs_2_.1, ...), custom_call_target="tpu_custom_call" | custom-call | bytes 1 | tf_op jit(solution)/shard_map/transposed_current/pallas_call | solution.py:26
  7.8 0.0 copy-start.1
  7.9 0.0 copy-start.2
  7.9 0.0 copy-start.3
  7.9 0.0 collective-permute-done.1.partner.x_partner
  7.9 0.0 copy-done
  8.0 14.1 %all_to_all.15.parts = f32[8,16,8,128]{3,2,1,0:T(8,128)S(1)} all-to-all(f32[8,16,8,128]{3,2,1,0:T(8,128)S(1)} %assemble_current.1), channel_id=1, replica_groups={{8,10,12,14,0,2,4,6},{1,3,5,7,9,11,13,15},{24,26,28,30,16,18,20,22},{17..., dimensions={0} | all-to-all | bytes 1048576 | tf_op jit(solution)/shard_map/all_to_all | solution.py:563
  22.1 0.1 collective-permute-start.2
  22.2 0.7 %direct_current.1.row_sum = f32[8,8,128]{2,1,0:T(8,128)S(1)} custom-call(s32[1,1]{1,0:T(1,128)S(4)} %get-tuple-element.33.counts, s32[1,1,64]{2,1,0:T(1,128)S(4)} %get-tuple-element.34.rows, s32[1,1,64]{2,1,0:T(1,128)S(4)} %get-tuple-element.35.columns, bf16[64,128,256]{2,1,0:T(8,128)(2,1)S(1)} %get-tuple-element.37.held, f32[8,16,8,128]{3,2,1,0:T(8,128)S(1)} %all_to_all.15.parts), custom_call_target="tpu_custom_call" | custom-call | bytes 1 | tf_op jit(solution)/shard_map/direct_current/pallas_call | solution.py:26
  22.9 0.5 collective-permute-done.2.other_sums
  23.3 0.0 copy-done.1
  23.3 0.0 copy-done.2
  23.4 0.8 %collective-permute-start.3 = (f32[12,8,128]{2,1,0:T(8,128)S(1)}, f32[12,8,128]{2,1,0:T(8,128)S(1)}, u32[]{:S(2)}, u32[]{:S(2)}) collective-permute-start(f32[12,8,128]{2,1,0:T(8,128)S(1)} %get-tuple-element.38.mine), channel_id=1, source_target_pairs={{0,1},{1,0},{2,3},{3,2},{4,5},{5,4},{6,7},{7,6},{8,9},{9,8},{10,11... | collective-permute-start | bytes 147464 | tf_op jit(solution)/shard_map/ppermute | solution.py:550
  24.1 1.4 %collective-permute-start.4 = (f32[8,8,128]{2,1,0:T(8,128)S(1)}, f32[8,8,128]{2,1,0:T(8,128)S(1)}, u32[]{:S(2)}, u32[]{:S(2)}) collective-permute-start(f32[8,8,128]{2,1,0:T(8,128)S(1)} %get-tuple-element.40), channel_id=1, source_target_pairs={{0,16},{16,0},{1,17},{17,1},{2,18},{18,2},{3,19},{19,3},{4,20},{20... | collective-permute-start | bytes 98312 | tf_op jit(solution)/shard_map/ppermute | solution.py:550
  25.5 0.0 collective-permute-done.3.theirs.p_other
  25.5 1.6 %collective-permute-start.5 = (f32[8,8,128]{2,1,0:T(8,128)S(1)}, f32[8,8,128]{2,1,0:T(8,128)S(1)}, u32[]{:S(2)}, u32[]{:S(2)}) collective-permute-start(f32[8,8,128]{2,1,0:T(8,128)S(1)} %get-tuple-element.39.base), channel_id=1, source_target_pairs={{0,16},{16,0},{1,17},{17,1},{2,18},{18,2},{3,19},{19,3},{4,20},{20... | collective-permute-start | bytes 98312 | tf_op jit(solution)/shard_map/ppermute | solution.py:550
  27.1 3.2 %collective-permute-done.4.received.sums_other = f32[8,8,128]{2,1,0:T(8,128)S(1)} collective-permute-done((f32[8,8,128]{2,1,0:T(8,128)S(1)}, f32[8,8,128]{2,1,0:T(8,128)S(1)}, u32[]{:S(2)}, u32[]{:S(2)}) %collective-permute-start.4) | collective-permute-done | bytes 32800 | tf_op jit(solution)/shard_map/ppermute | solution.py:550
  30.3 0.0 copy-done.3
  30.3 1.0 %transposed_image.1 = (f32[64,16,128]{2,1,0:T(8,128)S(1)}, bf16[64,32,128]{2,1,0:T(8,128)(2,1)S(1)}, f32[8,128]{1,0:T(8,128)S(1)}, bf16[32,128,256]{2,1,0:T(8,12...) custom-call(s32[1,1]{1,0:T(1,128)S(4)} %get-tuple-element.33.counts, ...), custom_call_target="tpu_custom_call" | custom-call | bytes 1 | tf_op jit(solution)/shard_map/transposed_image/pallas_call | solution.py:26
  31.3 0.0 collective-permute-done.5.base_partner
  31.3 0.3 assemble_image.1
  31.6 12.0 %all_to_all.16.parts = f32[8,17,8,128]{3,2,1,0:T(8,128)S(1)} all-to-all(f32[8,17,8,128]{3,2,1,0:T(8,128)S(1)} %get-tuple-element.44), channel_id=1, replica_groups={{8,10,12,14,0,2,4,6},{1,3,5,7,9,11,13,15},{24,26,28,30,16,18,20,22},{17..., dimensions={0} | all-to-all | bytes 1114112 | tf_op jit(solution)/shard_map/all_to_all | solution.py:563
  43.6 1.1 %inner_products.1 = f32[32,8,128]{2,1,0:T(8,128)} custom-call(f32[8,17,8,128]{3,2,1,0:T(8,128)S(1)} %all_to_all.16.parts, bf16[64,32,128]{2,1,0:T(8,128)(2,1)S(1)} %get-tuple-element.52.sum_halves, bf16[4,32,128]{2,1,0:T(8,128)(2,1)S(1)} %get-tuple-element.53.own_halves, bf16[4,32,128]{2,1,0:T(8,128)(2,1)S(1)} %get-tuple-element.54.partner_halves, ...), custom_call_target="tpu_custom_call" | custom-call | bytes 1 | tf_op jit(solution)/shard_map/inner_products/pallas_call | solution.py:26
  44.7 2.6 %all-to-all-start.2 = ((f32[32,8,128]{2,1,0:T(8,128)}), f32[32,8,128]{2,1,0:T(8,128)S(1)}, u32[]{:S(2)}, u32[]{:S(2)}) async-start(f32[32,8,128]{2,1,0:T(8,128)} %inner_products.1), calls=%async_computation.2 | async-start | bytes 262144 | tf_op jit(solution)/shard_map/all_to_all | solution.py:683
  47.3 0.2 collective-permute-start.6
  47.4 2.7 %collective-permute-start.7 = (f32[4,8,128]{2,1,0:T(8,128)S(1)}, f32[4,8,128]{2,1,0:T(8,128)S(1)}, u32[]{:S(2)}, u32[]{:S(2)}) collective-permute-start(f32[4,8,128]{2,1,0:T(8,128)S(1)} %get-tuple-element.56.for_partner), channel_id=1, source_target_pairs={{0,16},{16,0},{1,17},{17,1},{2,18},{18,2},{3,19},{19,3},{4,20},{20... | collective-permute-start | bytes 49160 | tf_op jit(solution)/shard_map/ppermute | solution.py:550
  50.1 0.0 collective-permute-done.6.theirs
  50.2 2.0 %direct_image.1 = (f32[8,8,128]{2,1,0:T(8,128)S(1)}, f32[4,8,128]{2,1,0:T(8,128)S(1)}, f32[8,128]{1,0:T(8,128)S(1)}) custom-call(s32[1,1]{1,0:T(1,128)S(4)} %get-tuple-element.33.counts, s32[1,1,64]{2,1,0:T(1,128)S(4)} %get-tuple-element.34.rows, s32[1,1,64]{2,1,0:T(1,128)S(4)} %get-tuple-element.35.columns, f32[64,128,128]{2,1,0:T(8,128)} %bitcast.6, ...), custom_call_target="tpu_custom_call" | custom-call | bytes 1 | tf_op jit(solution)/shard_map/direct_image/pallas_call | solution.py:26
  52.2 0.1 collective-permute-start.8
  52.3 1.9 %eliminate.1 = (f32[8,8]{1,0:T(8,128)S(1)}, f32[24,24]{1,0:T(8,128)S(1)}, f32[24,24]{1,0:T(8,128)S(1)}, f32[8,512]{1,0:T(8,128)}, f32[8,512]{1,0:T(8,128)}) custom-call(f32[8,128]{1,0:T(8,128)S(1)} %get-tuple-element.47.gram, f32[8,512]{1,0:T(8,128)S(1)} %copy-done, f32[8,512]{1,0:T(8,128)S(1)} %image.1.own.y_ref), custom_call_target="tpu_custom_call" | custom-call | bytes 1 | tf_op jit(solution)/shard_map/eliminate/pallas_call | solution.py:26
  54.2 0.3 collective-permute-done.7.received
  54.5 0.0 collective-permute-done.8.theirs
  54.5 0.4 all-to-all-done.2.inner_parts
  54.9 1.0 %finish.1 = (f32[8,512]{1,0:T(8,128)}, f32[24,24]{1,0:T(8,128)}) custom-call(f32[24,24]{1,0:T(8,128)S(1)} %get-tuple-element.50.inverse, f32[24,24]{1,0:T(8,128)S(1)} %get-tuple-element.51.pencil, f32[32,8,128]{2,1,0:T(8,128)S(1)} %all-to-all-done.2.inner_parts, f32[8,8]{1,0:T(8,128)S(1)} %get-tuple-element.57.ritz, f32[8,512]{1,0:T(8,128)S(1)} %image.1.own.y_ref, ...), custom_call_target="tpu_custom_call" | custom-call | bytes 1 | tf_op jit(solution)/shard_map/finish/pallas_call | solution.py:26
  (6 shorter events, 0.1 us)
Async XLA Ops:
  0.6 7.3 %copy-start = (f32[8,512]{1,0:T(8,128)S(1)}, f32[8,512]{1,0:T(8,128)}, u32[]{:S(2)}) copy-start(f32[8,512]{1,0:T(8,128)} %x_ref.3) | copy-start | bytes 49156
  0.6 4.8 %collective-permute-start = (f32[8,512]{1,0:T(8,128)}, f32[8,512]{1,0:T(8,128)S(1)}, u32[]{:S(2)}, u32[]{:S(2)}) collective-permute-start(f32[8,512]{1,0:T(8,128)} %x_ref.3), channel_id=1, source_target_pairs={{0,1},{1,0},{2,3},{3,2},{4,5},{5,4},{6,7},{7,6},{8,9},{9,8},{10,11... | collective-permute-start | bytes 49160 | tf_op jit(solution)/shard_map/ppermute | solution.py:550
  1.2 6.7 %collective-permute-start.1 = (f32[8,512]{1,0:T(8,128)}, f32[8,512]{1,0:T(8,128)S(1)}, u32[]{:S(2)}, u32[]{:S(2)}) collective-permute-start(f32[8,512]{1,0:T(8,128)} %x_ref.3), channel_id=1, source_target_pairs={{0,16},{16,0},{1,17},{17,1},{2,18},{18,2},{3,19},{19,3},{4,20},{20... | collective-permute-start | bytes 49160 | tf_op jit(solution)/shard_map/ppermute | solution.py:550
  7.8 15.5 %copy-start.1 = (f32[8,512]{1,0:T(8,128)S(1)}, f32[8,512]{1,0:T(8,128)}, u32[]{:S(2)}) copy-start(f32[8,512]{1,0:T(8,128)} %p_ref.1) | copy-start | bytes 49156
  7.9 15.5 %copy-start.2 = (f32[512]{0:T(512)S(1)}, f32[512]{0:T(512)}, u32[]{:S(2)}) copy-start(f32[512]{0:T(512)} %param.12) | copy-start | bytes 6148
  7.9 22.5 %copy-start.3 = (f32[8,512]{1,0:T(8,128)S(1)}, f32[8,512]{1,0:T(8,128)}, u32[]{:S(2)}) copy-start(f32[8,512]{1,0:T(8,128)} %q_ref.1) | copy-start | bytes 49156
  22.1 1.2 %collective-permute-start.2 = (f32[4,8,128]{2,1,0:T(8,128)S(1)}, f32[4,8,128]{2,1,0:T(8,128)S(1)}, u32[]{:S(2)}, u32[]{:S(2)}) collective-permute-start(f32[4,8,128]{2,1,0:T(8,128)S(1)} %partner_sums.2.sums), channel_id=1, source_target_pairs={{0,1},{1,0},{2,3},{3,2},{4,5},{5,4},{6,7},{7,6},{8,9},{9,8},{10,11... | collective-permute-start | bytes 49160 | tf_op jit(solution)/shard_map/ppermute | solution.py:550
  23.4 2.2 %collective-permute-start.3 = (f32[12,8,128]{2,1,0:T(8,128)S(1)}, f32[12,8,128]{2,1,0:T(8,128)S(1)}, u32[]{:S(2)}, u32[]{:S(2)}) collective-permute-start(f32[12,8,128]{2,1,0:T(8,128)S(1)} %get-tuple-element.38.mine), channel_id=1, source_target_pairs={{0,1},{1,0},{2,3},{3,2},{4,5},{5,4},{6,7},{7,6},{8,9},{9,8},{10,11... | collective-permute-start | bytes 147464 | tf_op jit(solution)/shard_map/ppermute | solution.py:550
  24.1 6.2 %collective-permute-start.4 = (f32[8,8,128]{2,1,0:T(8,128)S(1)}, f32[8,8,128]{2,1,0:T(8,128)S(1)}, u32[]{:S(2)}, u32[]{:S(2)}) collective-permute-start(f32[8,8,128]{2,1,0:T(8,128)S(1)} %get-tuple-element.40), channel_id=1, source_target_pairs={{0,16},{16,0},{1,17},{17,1},{2,18},{18,2},{3,19},{19,3},{4,20},{20... | collective-permute-start | bytes 98312 | tf_op jit(solution)/shard_map/ppermute | solution.py:550
  25.5 5.8 %collective-permute-start.5 = (f32[8,8,128]{2,1,0:T(8,128)S(1)}, f32[8,8,128]{2,1,0:T(8,128)S(1)}, u32[]{:S(2)}, u32[]{:S(2)}) collective-permute-start(f32[8,8,128]{2,1,0:T(8,128)S(1)} %get-tuple-element.39.base), channel_id=1, source_target_pairs={{0,16},{16,0},{1,17},{17,1},{2,18},{18,2},{3,19},{19,3},{4,20},{20... | collective-permute-start | bytes 98312 | tf_op jit(solution)/shard_map/ppermute | solution.py:550
  44.7 10.2 %all-to-all-start.2 = ((f32[32,8,128]{2,1,0:T(8,128)}), f32[32,8,128]{2,1,0:T(8,128)S(1)}, u32[]{:S(2)}, u32[]{:S(2)}) async-start(f32[32,8,128]{2,1,0:T(8,128)} %inner_products.1), calls=%async_computation.2 | async-start | bytes 262144 | tf_op jit(solution)/shard_map/all_to_all | solution.py:683
  47.3 2.9 %collective-permute-start.6 = (f32[8,128]{1,0:T(8,128)S(1)}, f32[8,128]{1,0:T(8,128)S(1)}, u32[]{:S(2)}, u32[]{:S(2)}) collective-permute-start(f32[8,128]{1,0:T(8,128)S(1)} %get-tuple-element.46.mine), channel_id=1, source_target_pairs={{0,1},{1,0},{2,3},{3,2},{4,5},{5,4},{6,7},{7,6},{8,9},{9,8},{10,11... | collective-permute-start | bytes 12296 | tf_op jit(solution)/shard_map/ppermute | solution.py:550
  47.4 7.1 %collective-permute-start.7 = (f32[4,8,128]{2,1,0:T(8,128)S(1)}, f32[4,8,128]{2,1,0:T(8,128)S(1)}, u32[]{:S(2)}, u32[]{:S(2)}) collective-permute-start(f32[4,8,128]{2,1,0:T(8,128)S(1)} %get-tuple-element.56.for_partner), channel_id=1, source_target_pairs={{0,16},{16,0},{1,17},{17,1},{2,18},{18,2},{3,19},{19,3},{4,20},{20... | collective-permute-start | bytes 49160 | tf_op jit(solution)/shard_map/ppermute | solution.py:550
  52.2 2.3 %collective-permute-start.8 = (f32[4,8,128]{2,1,0:T(8,128)S(1)}, f32[4,8,128]{2,1,0:T(8,128)S(1)}, u32[]{:S(2)}, u32[]{:S(2)}) collective-permute-start(f32[4,8,128]{2,1,0:T(8,128)S(1)} %get-tuple-element.59), channel_id=1, source_target_pairs={{0,1},{1,0},{2,3},{3,2},{4,5},{5,4},{6,7},{7,6},{8,9},{9,8},{10,11... | collective-permute-start | bytes 49160 | tf_op jit(solution)/shard_map/ppermute | solution.py:550
